TPU v7x, 256 devices: a whole 4x4x8 slice. The times are simulated.
256 devices in a mesh: dp: 4 (over x), seq: 16 (over z, core), head: 4 (over y).
Axes of the slice: x: 4, y: 4, z: 8, core: 2. Of those that a mesh axis runs over, the one named last changes fastest.
Arguments:
- queries: bfloat16 [4, 4096, 2048], P('dp', 'seq', 'head'), may hold values from -5.5 to 5.5
- keys: bfloat16 [4, 4096, 2048], P('dp', 'seq', 'head'), may hold values from -5.5 to 5.5
- values: bfloat16 [4, 4096, 2048], P('dp', 'seq', 'head'), may hold values from -5.5 to 5.5
- out_weight: bfloat16 [2048, 2048], P('head'), may hold values from -0.125 to 0.125
- out_grad: bfloat16 [4, 4096, 2048], P('dp', 'seq', 'head'), may hold values from -6 to 6
Outputs:
- mixed: bfloat16 [4, 4096, 2048], P('dp', 'seq', 'head')
- grad_queries: bfloat16 [4, 4096, 2048], P('dp', 'seq', 'head')
- grad_keys: bfloat16 [4, 4096, 2048], P('dp', 'seq', 'head')
- grad_values: bfloat16 [4, 4096, 2048], P('dp', 'seq', 'head')
- grad_out_weight: float32 [2048, 2048], P('head', 'seq')
All inputs are finite; a program needn't handle non-finite values.
Results may differ from a plain program's by a relative error of at most 0.025.
Values may be sent and summed in bfloat16 or wider, within the bound.
No kernel may reach another device: no remote copies, remote signals or barrier semaphores. Data moves between devices by JAX's collectives and lax.ppermute only.
A program may use at most 128 MiB of HBM per device.

v0:
```python
import math

import jax
import jax.numpy as jnp
from jax import lax
from jax.sharding import PartitionSpec as P

DH = 128
NR = 128
C = 64


def padded(x, sides, width):
    for axis, dim in sides:
        size, length = (lax.axis_size(axis), x.shape[dim])
        up = [(i, (i + 1) % size) for i in range(size - 1)]
        down = [(j, i) for i, j in up]
        last = lax.slice_in_dim(x, length - width, length, axis=dim)
        leading = lax.slice_in_dim(x, 0, width, axis=dim)
        before = lax.ppermute(last, axis, up)
        after = lax.ppermute(leading, axis, down)
        x = jnp.concatenate([before, x, after], axis=dim)
    return x


def from_partner(value, axis, bit):
    mask = 2**bit
    pairs = [(source, source ^ mask) for source in range(lax.axis_size(axis))]
    return lax.ppermute(value, axis, pairs)


def spread_rows(source, factor, axis_at):
    shape_now = source.shape
    expanded = jnp.expand_dims(source, axis_at + 1)
    target = shape_now[: axis_at + 1] + (factor,) + shape_now[axis_at + 1 :]
    widened = jnp.broadcast_to(expanded, target)
    merged = shape_now[:axis_at] + (shape_now[axis_at] * factor,) + shape_now[axis_at + 1 :]
    return widened.reshape(merged) / factor


def halve_rows(source):
    batch_size, row_total, width_all = source.shape
    return source.reshape(batch_size, row_total // 2, 2, width_all).mean(axis=2)


def body(queries, keys, values, out_weight, out_grad):
    seq_count = lax.axis_size("seq")
    level_count = seq_count.bit_length() - 1
    position = lax.axis_index("seq")
    batch_size, local_rows, width = queries.shape
    head_count = width // DH
    block_count = local_rows // NR
    group_size = local_rows // C
    score_scale = 1.0 / math.sqrt(DH)
    coarse_rows = (level_count + 2) * C
    paired = jnp.concatenate([keys, values], axis=2)
    extended = padded(paired, (("seq", 1),), NR)
    own_pool = paired.astype(jnp.float32).reshape(batch_size, C, group_size, 2 * width).mean(axis=2)
    current = own_pool
    siblings = []
    for bit_index in range(level_count):
        other = from_partner(current, "seq", bit_index)
        siblings.append(other)
        upper_side = position >> bit_index & 1 == 1
        lower_half = jnp.where(upper_side, other, current)
        upper_half = jnp.where(upper_side, current, other)
        current = jnp.concatenate([halve_rows(lower_half), halve_rows(upper_half)], axis=1)
    coarse = jnp.concatenate([own_pool] + siblings + [current], axis=1).astype(jnp.bfloat16)
    coarse_keys = coarse[:, :, :width].reshape(batch_size, coarse_rows, head_count, DH)
    coarse_values = coarse[:, :, width:].reshape(batch_size, coarse_rows, head_count, DH)
    framed = extended.reshape(batch_size, block_count + 2, NR, 2 * width)
    window = jnp.concatenate([framed[:, :-2], framed[:, 1:-1], framed[:, 2:]], axis=2)
    fine_keys = window[..., :width].reshape(batch_size, block_count, 3 * NR, head_count, DH)
    fine_values = window[..., width:].reshape(batch_size, block_count, 3 * NR, head_count, DH)
    slot_index = jnp.arange(block_count)[:, None] * NR + jnp.arange(3 * NR)[None, :]
    lower_edge = (slot_index < NR) & (position == 0)
    upper_edge = (slot_index >= NR + local_rows) & (position == seq_count - 1)
    visible = jnp.logical_not(lower_edge | upper_edge)
    query_blocks = queries.reshape(batch_size, block_count, NR, head_count, DH)
    fine_scores = (
        jnp.einsum(
            "bnqhd,bnkhd->bhnqk", query_blocks, fine_keys, preferred_element_type=jnp.float32
        )
        * score_scale
    )
    fine_scores = jnp.where(visible[None, None, :, None, :], fine_scores, -jnp.inf)
    coarse_scores = (
        jnp.einsum(
            "bnqhd,bchd->bhnqc", query_blocks, coarse_keys, preferred_element_type=jnp.float32
        )
        * score_scale
    )
    highest = jnp.maximum(jnp.max(fine_scores, axis=-1), jnp.max(coarse_scores, axis=-1))
    fine_exp = jnp.exp(fine_scores - highest[..., None])
    coarse_exp = jnp.exp(coarse_scores - highest[..., None])
    totals = jnp.sum(fine_exp, axis=-1) + jnp.sum(coarse_exp, axis=-1)
    fine_probs = fine_exp / totals[..., None]
    coarse_probs = coarse_exp / totals[..., None]
    fine_weights = fine_probs.astype(jnp.bfloat16)
    coarse_weights = coarse_probs.astype(jnp.bfloat16)
    attended_wide = jnp.einsum(
        "bhnqk,bnkhd->bnqhd", fine_weights, fine_values, preferred_element_type=jnp.float32
    )
    attended_wide = attended_wide + jnp.einsum(
        "bhnqc,bchd->bnqhd", coarse_weights, coarse_values, preferred_element_type=jnp.float32
    )
    attended = attended_wide.astype(jnp.bfloat16)
    attended_rows = attended.reshape(batch_size, local_rows, width)
    partial_mix = jnp.einsum(
        "blf,fd->bld", attended_rows, out_weight, preferred_element_type=jnp.float32
    )
    mixed = lax.psum_scatter(partial_mix, "head", scatter_dimension=2, tiled=True).astype(
        jnp.bfloat16
    )
    piece_cols = lax.all_gather(out_grad, "head", axis=2, tiled=True)
    grad_attended = jnp.einsum(
        "bld,fd->blf", piece_cols, out_weight, preferred_element_type=jnp.float32
    )
    block_terms = jnp.einsum(
        "blf,bld->fd", attended_rows, piece_cols, preferred_element_type=jnp.float32
    )
    weight_terms = block_terms
    grad_attended, weight_terms = (grad_attended, weight_terms)
    weight_share = lax.psum_scatter(
        weight_terms.astype(jnp.bfloat16), "seq", scatter_dimension=1, tiled=True
    )
    grad_out_weight = lax.psum(weight_share, "dp").astype(jnp.float32)
    grad_blocks = grad_attended.astype(jnp.bfloat16).reshape(
        batch_size, block_count, NR, head_count, DH
    )
    row_delta = jnp.einsum(
        "bnqhd,bnqhd->bhnq", grad_blocks.astype(jnp.float32), attended.astype(jnp.float32)
    )
    fine_pgrad = jnp.einsum(
        "bnqhd,bnkhd->bhnqk", grad_blocks, fine_values, preferred_element_type=jnp.float32
    )
    coarse_pgrad = jnp.einsum(
        "bnqhd,bchd->bhnqc", grad_blocks, coarse_values, preferred_element_type=jnp.float32
    )
    fine_sgrad = (fine_probs * (fine_pgrad - row_delta[..., None]) * score_scale).astype(
        jnp.bfloat16
    )
    coarse_sgrad = (coarse_probs * (coarse_pgrad - row_delta[..., None]) * score_scale).astype(
        jnp.bfloat16
    )
    grad_query = jnp.einsum(
        "bhnqk,bnkhd->bnqhd", fine_sgrad, fine_keys, preferred_element_type=jnp.float32
    )
    grad_query = grad_query + jnp.einsum(
        "bhnqc,bchd->bnqhd", coarse_sgrad, coarse_keys, preferred_element_type=jnp.float32
    )
    grad_queries = grad_query.astype(jnp.bfloat16).reshape(batch_size, local_rows, width)
    key_part = jnp.einsum(
        "bhnqk,bnqhd->bnkhd", fine_sgrad, query_blocks, preferred_element_type=jnp.float32
    )
    value_part = jnp.einsum(
        "bhnqk,bnqhd->bnkhd", fine_weights, grad_blocks, preferred_element_type=jnp.float32
    )
    key_part = key_part.reshape(batch_size, block_count, 3 * NR, width)
    value_part = value_part.reshape(batch_size, block_count, 3 * NR, width)
    fine_grad = jnp.concatenate([key_part, value_part], axis=3).reshape(
        batch_size, block_count, 3, NR, 2 * width
    )
    extended_grad = jnp.zeros((batch_size, block_count + 2, NR, 2 * width), jnp.float32)
    extended_grad = (
        extended_grad.at[:, :-2]
        .add(fine_grad[:, :, 0])
        .at[:, 1:-1]
        .add(fine_grad[:, :, 1])
        .at[:, 2:]
        .add(fine_grad[:, :, 2])
    )
    extended_grad = extended_grad.reshape(batch_size, local_rows + 2 * NR, 2 * width)
    rim_rows = jnp.concatenate([extended_grad[:, :NR], extended_grad[:, -NR:]], axis=1)
    returned = padded(rim_rows, (("seq", 1),), NR)
    middle = extended_grad[:, NR : NR + local_rows]
    middle = (
        middle.at[:, :NR].add(returned[:, :NR]).at[:, local_rows - NR :].add(returned[:, 3 * NR :])
    )
    coarse_kgrad = jnp.einsum(
        "bhnqc,bnqhd->bchd", coarse_sgrad, query_blocks, preferred_element_type=jnp.float32
    )
    coarse_vgrad = jnp.einsum(
        "bhnqc,bnqhd->bchd", coarse_weights, grad_blocks, preferred_element_type=jnp.float32
    )
    coarse_grad = jnp.concatenate(
        [
            coarse_kgrad.reshape(batch_size, coarse_rows, width),
            coarse_vgrad.reshape(batch_size, coarse_rows, width),
        ],
        axis=2,
    )
    grad_stack = coarse_grad[:, C:].reshape(batch_size, level_count + 1, C, 2 * width)
    received = []
    for bit_index in range(level_count):
        incoming = from_partner(grad_stack.astype(jnp.bfloat16), "seq", bit_index).astype(
            grad_stack.dtype
        )
        received.append(incoming[:, 0])
        grad_stack = (grad_stack + incoming)[:, 1:]
    subtree_grad = grad_stack[:, 0]
    for bit_index in reversed(range(level_count)):
        upper_bit = position >> bit_index & 1
        half_rows = lax.dynamic_slice_in_dim(subtree_grad, upper_bit * (C // 2), C // 2, 1)
        subtree_grad = spread_rows(half_rows, 2, 1) + received[bit_index]
    own_grad = subtree_grad + coarse_grad[:, :C]
    total_grad = middle + spread_rows(own_grad, group_size, 1)
    grad_keys = total_grad[..., :width].astype(jnp.bfloat16)
    grad_values = total_grad[..., width:].astype(jnp.bfloat16)
    return (mixed, grad_queries, grad_keys, grad_values, grad_out_weight)


def solution(mesh):
    placed = (
        P("dp", "seq", "head"),
        P("dp", "seq", "head"),
        P("dp", "seq", "head"),
        P("head", None),
        P("dp", "seq", "head"),
    )
    return jax.shard_map(
        body,
        mesh=mesh,
        in_specs=placed,
        out_specs=(
            P("dp", "seq", "head"),
            P("dp", "seq", "head"),
            P("dp", "seq", "head"),
            P("dp", "seq", "head"),
            P("head", "seq"),
        ),
        check_vma=False,
    )
```

profile of v0, /device:TPU:8, one launch (start us, length us, event | category | flops | bytes accessed | tf_op | source)
XLA Modules:
  0.0 269.8 jit_solution(5480749946950976399)
XLA Ops:
  12.4 3.1 %collective-permute-start = (bf16[1,128,1024]{2,1,0:T(8,128)(2,1)}, bf16[1,128,1024]{2,1,0:T(8,128)(2,1)}, u32[]{:S(2)}, u32[]{:S(2)}) collective-permute-start(bf16[1,128,1024]{2,1,0:T(8,128)(2,1)} %get-tuple-element.85), channel_id=1, source_target_pairs={{0,4},{4,8},{8,12},{12,16},{16,20},{20,24},{24,28},{28,32},{32,36}... | collective-permute-start | bytes 786440 | tf_op jit(solution)/shard_map/ppermute | solution.py:20
  25.8 3.1 %collective-permute-start.3 = (f32[1,64,1024]{2,1,0:T(8,128)}, f32[1,64,1024]{2,1,0:T(8,128)}, u32[]{:S(2)}, u32[]{:S(2)}) collective-permute-start(f32[1,64,1024]{2,1,0:T(8,128)} %pad_maximum_fusion.4), channel_id=1, source_target_pairs={{0,8},{4,12},{8,0},{12,4},{16,24},{20,28},{24,16},{28,20},{32,40},... | collective-permute-start | bytes 786440 | tf_op jit(solution)/shard_map/ppermute | solution.py:29
  33.2 2.8 %collective-permute-done.3 = f32[1,64,1024]{2,1,0:T(8,128)} collective-permute-done((f32[1,64,1024]{2,1,0:T(8,128)}, f32[1,64,1024]{2,1,0:T(8,128)}, u32[]{:S(2)}, u32[]{:S(2)}) %collective-permute-start.3) | collective-permute-done | bytes 262176 | tf_op jit(solution)/shard_map/ppermute | solution.py:29
  43.0 3.1 %collective-permute-start.4 = (f32[1,64,1024]{2,1,0:T(8,128)}, f32[1,64,1024]{2,1,0:T(8,128)}, u32[]{:S(2)}, u32[]{:S(2)}) collective-permute-start(f32[1,64,1024]{2,1,0:T(8,128)} %pad_maximum_fusion.5), channel_id=1, source_target_pairs={{0,16},{4,20},{8,24},{12,28},{16,0},{20,4},{24,8},{28,12},{32,48},... | collective-permute-start | bytes 786440 | tf_op jit(solution)/shard_map/ppermute | solution.py:29
  47.9 2.3 copy.127
  51.8 7.3 %collective-permute-done.4 = f32[1,64,1024]{2,1,0:T(8,128)} collective-permute-done((f32[1,64,1024]{2,1,0:T(8,128)}, f32[1,64,1024]{2,1,0:T(8,128)}, u32[]{:S(2)}, u32[]{:S(2)}) %collective-permute-start.4) | collective-permute-done | bytes 262176 | tf_op jit(solution)/shard_map/ppermute | solution.py:29
  62.7 2.7 %collective-permute-start.5 = (f32[1,64,1024]{2,1,0:T(8,128)S(1)}, f32[1,64,1024]{2,1,0:T(8,128)S(1)}, u32[]{:S(2)}, u32[]{:S(2)}) collective-permute-start(f32[1,64,1024]{2,1,0:T(8,128)S(1)} %pad_maximum_fusion.6), channel_id=1, source_target_pairs={{0,32},{4,36},{8,40},{12,44},{16,48},{20,52},{24,56},{28,60},{32,0... | collective-permute-start | bytes 786440 | tf_op jit(solution)/shard_map/ppermute | solution.py:29
  68.7 9.6 %collective-permute-done.5 = f32[1,64,1024]{2,1,0:T(8,128)S(1)} collective-permute-done((f32[1,64,1024]{2,1,0:T(8,128)S(1)}, f32[1,64,1024]{2,1,0:T(8,128)S(1)}, u32[]{:S(2)}, u32[]{:S(2)}) %collective-permute-start.5) | collective-permute-done | bytes 262176 | tf_op jit(solution)/shard_map/ppermute | solution.py:29
  89.8 2.7 convolution_convert_fusion.1
  94.3 2.0 copy.177
  96.3 2.7 %multiply_reduce_fusion = (f32[4,2,128]{2,0,1:T(4,128)S(1)}, bf16[1,2,128,4,128]{2,4,3,1,0:T(8,128)(2,1)}) fusion(f32[4,2,128,128]{2,3,0,1:T(8,128)} %copy.177, f32[1,2,128,4,128]{2,4,3,1,0:T(8,128)} %convolution_bitcast_fusion.5, bf16[2,384,4,128]{1,3,2,0:T(8,128)(2,1)} %bitcast.216, bf16[4,2,128,384]{2,3,1,0:T(8,128)(2,1)} %get-tuple-element.95), kind=kOutput, calls=%fused_computation.64 | convolution fusion | flops 101317632 | bytes 2887680 | tf_op jit(solution)/shard_map/bhnqk,bnkhd->bnqhd/dot_general | solution.py:101
  100.9 3.4 %convolution_convert_fusion = bf16[512,2048]{1,0:T(8,128)(2,1)} fusion(bf16[1,256,2048]{2,1,0:T(8,128)(2,1)} %all-gather.2.cloned.1.call-done, bf16[32,8,4,128]{3,2,1,0:T(4,128)(2,1)} %bitcast.218), kind=kOutput, calls=%fused_computation | convolution fusion | flops 537919488 | bytes 3407872 | tf_op jit(solution)/shard_map/blf,bld->fd/dot_general | solution.py:119
  104.3 3.9 %copy.200 = bf16[512,2048]{0,1:T(8,128)(2,1)} copy(bf16[512,2048]{1,0:T(8,128)(2,1)} %convolution_convert_fusion) | data formatting | bytes 4194304
  109.2 2.2 fusion.66
  111.3 2.4 copy.164
  113.7 2.0 multiply_convert_fusion
  118.1 2.3 multiply_convert_fusion.1
  121.7 2.2 copy.151
  125.6 2.7 copy.154
  128.2 2.0 fusion.19
  136.8 2.0 convolution_bitcast_fusion
  138.9 3.5 %fusion.15 = f32[1,4,128,1024]{3,0,2,1:T(1,128)} fusion(f32[1,4,128,1024]{3,0,2,1:T(1,128)} %copy-done.3, f32[1,2,3,128,512]{4,0,3,2,1:T(1,128)} %bitcast.202, f32[1,2,3,128,512]{4,0,3,2,1:T(1,128)} %bitcast.199), kind=kLoop, calls=%fused_computation.41 | loop fusion | flops 524288 | bytes 5242880 | tf_op jit(solution)/shard_map/scatter-add | solution.py:171
  146.2 2.1 fusion.59
  149.9 2.1 collective-permute-start.6
  158.2 3.5 %collective-permute-done.9 = bf16[1,4,64,1024]{3,2,1,0:T(8,128)(2,1)} collective-permute-done((bf16[1,4,64,1024]{3,2,1,0:T(8,128)(2,1)}, bf16[1,4,64,1024]{3,2,1,0:T(8,128)(2,1)}, u32[]{:S(2)}, u32[]{:S(2)}) %collective-permute-start.9) | collective-permute-done | bytes 524320 | tf_op jit(solution)/shard_map/ppermute | solution.py:29
  163.0 5.0 %collective-permute-start.10 = (bf16[1,3,64,1024]{3,2,1,0:T(8,128)(2,1)S(1)}, bf16[1,3,64,1024]{3,2,1,0:T(8,128)(2,1)S(1)}, u32[]{:S(2)}, u32[]{:S(2)}) collective-permute-start(bf16[1,3,64,1024]{3,2,1,0:T(8,128)(2,1)S(1)} %get-tuple-element.69), channel_id=1, source_target_pairs={{0,16},{4,20},{8,24},{12,28},{16,0},{20,4},{24,8},{28,12},{32,48},... | collective-permute-start | bytes 1179656 | tf_op jit(solution)/shard_map/ppermute | solution.py:29
  169.3 19.7 %collective-permute-done.10 = bf16[1,3,64,1024]{3,2,1,0:T(8,128)(2,1)S(1)} collective-permute-done((bf16[1,3,64,1024]{3,2,1,0:T(8,128)(2,1)S(1)}, bf16[1,3,64,1024]{3,2,1,0:T(8,128)(2,1)S(1)}, u32[]{:S(2)}, u32[]{:S(2)}) %collective-permute-start.10) | collective-permute-done | bytes 393248 | tf_op jit(solution)/shard_map/ppermute | solution.py:29
  189.2 3.4 %collective-permute-start.11 = (bf16[1,2,64,1024]{3,2,1,0:T(8,128)(2,1)S(1)}, bf16[1,2,64,1024]{3,2,1,0:T(8,128)(2,1)S(1)}, u32[]{:S(2)}, u32[]{:S(2)}) collective-permute-start(bf16[1,2,64,1024]{3,2,1,0:T(8,128)(2,1)S(1)} %get-tuple-element.67), channel_id=1, source_target_pairs={{0,32},{4,36},{8,40},{12,44},{16,48},{20,52},{24,56},{28,60},{32,0... | collective-permute-start | bytes 786440 | tf_op jit(solution)/shard_map/ppermute | solution.py:29
  193.4 7.3 %collective-permute-done.11 = bf16[1,2,64,1024]{3,2,1,0:T(8,128)(2,1)S(1)} collective-permute-done((bf16[1,2,64,1024]{3,2,1,0:T(8,128)(2,1)S(1)}, bf16[1,2,64,1024]{3,2,1,0:T(8,128)(2,1)S(1)}, u32[]{:S(2)}, u32[]{:S(2)}) %collective-permute-start.11) | collective-permute-done | bytes 262176 | tf_op jit(solution)/shard_map/ppermute | solution.py:29
  207.6 2.6 div.133
  210.2 2.2 add_convert_fusion
  217.7 44.0 %all-reduce.3.cloned.1.call-done = bf16[512,128]{1,0:T(8,128)(2,1)} async-done(((bf16[512,128]{1,0:T(8,128)(2,1)}), bf16[512,128]{1,0:T(8,128)(2,1)}) %all-reduce.3.cloned.1.call-update) | async-done | bytes 131088 | tf_op jit(solution)/shard_map/psum | solution.py:127
  (202 shorter events, 93.6 us)
Async XLA Ops:
  7.2 82.6 %copy-start = (bf16[512,2048]{1,0:T(8,128)(2,1)S(1)}, bf16[512,2048]{1,0:T(8,128)(2,1)}, u32[]{:S(2)}) copy-start(bf16[512,2048]{1,0:T(8,128)(2,1)} %param.18) | copy-start | bytes 6291460
  7.2 4.3 %copy-start.31 = (bf16[1,256,512]{2,1,0:T(8,128)(2,1)S(1)}, bf16[1,256,512]{2,1,0:T(8,128)(2,1)}, u32[]{:S(2)}) copy-start(bf16[1,256,512]{2,1,0:T(8,128)(2,1)} %param.16) | copy-start | bytes 786436
  7.2 4.3 %copy-start.32 = (bf16[1,256,512]{2,1,0:T(8,128)(2,1)S(1)}, bf16[1,256,512]{2,1,0:T(8,128)(2,1)}, u32[]{:S(2)}) copy-start(bf16[1,256,512]{2,1,0:T(8,128)(2,1)} %param.17) | copy-start | bytes 786436
  7.2 82.6 %all-gather.2.cloned.1.call-start = ((), (), s32[]{:S(2)}) async-start(), calls=%async_computation.3 | async-start | bytes 1310720 | tf_op jit(solution)/shard_map/all_gather | solution.py:115
  7.9 204.4 %reduce-scatter.7.cloned.1.call-start = ((), (), s32[]{:S(2)}) async-start(), calls=%async_computation.5 | async-start | bytes 2228224
  11.5 7.3 %collective-permute-start.2 = (f32[1,64,1024]{2,1,0:T(8,128)}, f32[1,64,1024]{2,1,0:T(8,128)}, u32[]{:S(2)}, u32[]{:S(2)}) collective-permute-start(f32[1,64,1024]{2,1,0:T(8,128)} %multiply_bitcast_fusion), channel_id=1, source_target_pairs={{0,4},{4,0},{8,12},{12,8},{16,20},{20,16},{24,28},{28,24},{32,36},... | collective-permute-start | bytes 786440 | tf_op jit(solution)/shard_map/ppermute | solution.py:29
  12.4 16.6 %collective-permute-start = (bf16[1,128,1024]{2,1,0:T(8,128)(2,1)}, bf16[1,128,1024]{2,1,0:T(8,128)(2,1)}, u32[]{:S(2)}, u32[]{:S(2)}) collective-permute-start(bf16[1,128,1024]{2,1,0:T(8,128)(2,1)} %get-tuple-element.85), channel_id=1, source_target_pairs={{0,4},{4,8},{8,12},{12,16},{16,20},{20,24},{24,28},{28,32},{32,36}... | collective-permute-start | bytes 786440 | tf_op jit(solution)/shard_map/ppermute | solution.py:20
  15.5 13.5 %collective-permute-start.1 = (bf16[1,128,1024]{2,1,0:T(8,128)(2,1)}, bf16[1,128,1024]{2,1,0:T(8,128)(2,1)}, u32[]{:S(2)}, u32[]{:S(2)}) collective-permute-start(bf16[1,128,1024]{2,1,0:T(8,128)(2,1)} %get-tuple-element.86), channel_id=1, source_target_pairs={{4,0},{8,4},{12,8},{16,12},{20,16},{24,20},{28,24},{32,28},{36,32}... | collective-permute-start | bytes 786440 | tf_op jit(solution)/shard_map/ppermute | solution.py:21
  17.9 5.9 %copy-start.23 = (bf16[2,128,4,128]{3,2,1,0:T(4,128)(2,1)}, bf16[2,128,4,128]{3,2,1,0:T(4,128)(2,1)S(1)}, u32[]{:S(2)}) copy-start(bf16[2,128,4,128]{3,2,1,0:T(4,128)(2,1)S(1)} %reshape.804) | copy-start | bytes 786436
  25.8 10.2 %collective-permute-start.3 = (f32[1,64,1024]{2,1,0:T(8,128)}, f32[1,64,1024]{2,1,0:T(8,128)}, u32[]{:S(2)}, u32[]{:S(2)}) collective-permute-start(f32[1,64,1024]{2,1,0:T(8,128)} %pad_maximum_fusion.4), channel_id=1, source_target_pairs={{0,8},{4,12},{8,0},{12,4},{16,24},{20,28},{24,16},{28,20},{32,40},... | collective-permute-start | bytes 786440 | tf_op jit(solution)/shard_map/ppermute | solution.py:29
  33.2 12.9 %copy-start.19 = (bf16[1,2,384,512]{2,3,1,0:T(8,128)(2,1)}, bf16[1,2,384,512]{2,3,1,0:T(8,128)(2,1)S(1)}, u32[]{:S(2)}) copy-start(bf16[1,2,384,512]{2,3,1,0:T(8,128)(2,1)S(1)} %copy.128) | copy-start | bytes 2359300
  43.0 16.0 %collective-permute-start.4 = (f32[1,64,1024]{2,1,0:T(8,128)}, f32[1,64,1024]{2,1,0:T(8,128)}, u32[]{:S(2)}, u32[]{:S(2)}) collective-permute-start(f32[1,64,1024]{2,1,0:T(8,128)} %pad_maximum_fusion.5), channel_id=1, source_target_pairs={{0,16},{4,20},{8,24},{12,28},{16,0},{20,4},{24,8},{28,12},{32,48},... | collective-permute-start | bytes 786440 | tf_op jit(solution)/shard_map/ppermute | solution.py:29
  62.7 15.5 %collective-permute-start.5 = (f32[1,64,1024]{2,1,0:T(8,128)S(1)}, f32[1,64,1024]{2,1,0:T(8,128)S(1)}, u32[]{:S(2)}, u32[]{:S(2)}) collective-permute-start(f32[1,64,1024]{2,1,0:T(8,128)S(1)} %pad_maximum_fusion.6), channel_id=1, source_target_pairs={{0,32},{4,36},{8,40},{12,44},{16,48},{20,52},{24,56},{28,60},{32,0... | collective-permute-start | bytes 786440 | tf_op jit(solution)/shard_map/ppermute | solution.py:29
  108.2 107.7 %reduce-scatter.5.cloned.1.call-start = ((), (), s32[]{:S(2)}) async-start(), calls=%async_computation.2 | async-start | bytes 2621440 | tf_op jit(solution)/shard_map/reduce_scatter | solution.py:112
  118.1 3.3 %copy-start.24 = (bf16[2,128,4,128]{3,2,1,0:T(4,128)(2,1)S(1)}, bf16[2,128,4,128]{3,2,1,0:T(4,128)(2,1)}, u32[]{:S(2)}) copy-start(bf16[2,128,4,128]{3,2,1,0:T(4,128)(2,1)} %copy-done.23) | copy-start | bytes 786436
  132.6 4.1 %copy-start.25 = (bf16[1,2,128,4,128]{4,3,2,1,0:T(4,128)(2,1)S(1)}, bf16[1,2,128,4,128]{4,3,2,1,0:T(4,128)(2,1)}, u32[]{:S(2)}) copy-start(bf16[1,2,128,4,128]{4,3,2,1,0:T(4,128)(2,1)} %copy.138) | copy-start | bytes 786436
  132.6 9.7 %collective-permute-start.8 = (bf16[1,5,64,1024]{3,2,1,0:T(8,128)(2,1)}, bf16[1,5,64,1024]{3,2,1,0:T(8,128)(2,1)}, u32[]{:S(2)}, u32[]{:S(2)}) collective-permute-start(bf16[1,5,64,1024]{3,2,1,0:T(8,128)(2,1)} %convert_element_type.101), channel_id=1, source_target_pairs={{0,4},{4,0},{8,12},{12,8},{16,20},{20,16},{24,28},{28,24},{32,36},... | collective-permute-start | bytes 1966088 | tf_op jit(solution)/shard_map/ppermute | solution.py:29
  138.8 122.8 %all-reduce.3.cloned.1.call-start = ((), (), s32[]{:S(2)}) async-start(), calls=%async_computation.4 | async-start | bytes 262144 | tf_op jit(solution)/shard_map/psum | solution.py:127
  145.1 16.5 %collective-permute-start.9 = (bf16[1,4,64,1024]{3,2,1,0:T(8,128)(2,1)}, bf16[1,4,64,1024]{3,2,1,0:T(8,128)(2,1)}, u32[]{:S(2)}, u32[]{:S(2)}) collective-permute-start(bf16[1,4,64,1024]{3,2,1,0:T(8,128)(2,1)} %get-tuple-element.71), channel_id=1, source_target_pairs={{0,8},{4,12},{8,0},{12,4},{16,24},{20,28},{24,16},{28,20},{32,40},... | collective-permute-start | bytes 1572872 | tf_op jit(solution)/shard_map/ppermute | solution.py:29
  148.3 3.7 %copy-start.15 = (bf16[1,384,512]{1,2,0:T(8,128)(2,1)S(1)}, bf16[1,384,512]{1,2,0:T(8,128)(2,1)}, u32[]{:S(2)}) copy-start(bf16[1,384,512]{1,2,0:T(8,128)(2,1)} %copy-done.14) | copy-start | bytes 1179652
  148.3 3.7 %copy-start.18 = (bf16[4,2,128,384]{2,3,1,0:T(8,128)(2,1)S(1)}, bf16[4,2,128,384]{2,3,1,0:T(8,128)(2,1)}, u32[]{:S(2)}) copy-start(bf16[4,2,128,384]{2,3,1,0:T(8,128)(2,1)} %copy-done.17) | copy-start | bytes 2359300
  149.0 3.3 %copy-start.20 = (bf16[1,2,384,512]{2,3,1,0:T(8,128)(2,1)S(1)}, bf16[1,2,384,512]{2,3,1,0:T(8,128)(2,1)}, u32[]{:S(2)}) copy-start(bf16[1,2,384,512]{2,3,1,0:T(8,128)(2,1)} %copy-done.19) | copy-start | bytes 2359300
  149.0 3.3 %copy-start.22 = (bf16[4,2,128,384]{2,3,1,0:T(8,128)(2,1)S(1)}, bf16[4,2,128,384]{2,3,1,0:T(8,128)(2,1)}, u32[]{:S(2)}) copy-start(bf16[4,2,128,384]{2,3,1,0:T(8,128)(2,1)} %copy-done.21) | copy-start | bytes 2359300
  149.9 18.1 %collective-permute-start.6 = (f32[1,128,1024]{2,1,0:T(8,128)}, f32[1,128,1024]{2,1,0:T(8,128)}, u32[]{:S(2)}, u32[]{:S(2)}) collective-permute-start(f32[1,128,1024]{2,1,0:T(8,128)} %copy.204), channel_id=1, source_target_pairs={{0,4},{4,8},{8,12},{12,16},{16,20},{20,24},{24,28},{28,32},{32,36}... | collective-permute-start | bytes 1572872 | tf_op jit(solution)/shard_map/ppermute | solution.py:20
  156.5 6.3 %copy-start.16 = (f32[1,4,64,1024]{3,2,1,0:T(8,128)S(1)}, f32[1,4,64,1024]{3,2,1,0:T(8,128)}, u32[]{:S(2)}) copy-start(f32[1,4,64,1024]{3,2,1,0:T(8,128)} %get-tuple-element.72) | copy-start | bytes 3145732
  156.7 12.4 %collective-permute-start.7 = (f32[1,128,1024]{2,1,0:T(8,128)S(1)}, f32[1,128,1024]{2,1,0:T(8,128)S(1)}, u32[]{:S(2)}, u32[]{:S(2)}) collective-permute-start(f32[1,128,1024]{2,1,0:T(8,128)S(1)} %copy.205), channel_id=1, source_target_pairs={{4,0},{8,4},{12,8},{16,12},{20,16},{24,20},{28,24},{32,28},{36,32}... | collective-permute-start | bytes 1572872 | tf_op jit(solution)/shard_map/ppermute | solution.py:21
  162.8 5.2 %copy-start.26 = (f32[1,128,1024]{2,0,1:T(1,128)S(1)}, f32[1,128,1024]{2,0,1:T(1,128)}, u32[]{:S(2)}) copy-start(f32[1,128,1024]{2,0,1:T(1,128)} %get-tuple-element.75) | copy-start | bytes 1572868
  163.0 26.0 %collective-permute-start.10 = (bf16[1,3,64,1024]{3,2,1,0:T(8,128)(2,1)S(1)}, bf16[1,3,64,1024]{3,2,1,0:T(8,128)(2,1)S(1)}, u32[]{:S(2)}, u32[]{:S(2)}) collective-permute-start(bf16[1,3,64,1024]{3,2,1,0:T(8,128)(2,1)S(1)} %get-tuple-element.69), channel_id=1, source_target_pairs={{0,16},{4,20},{8,24},{12,28},{16,0},{20,4},{24,8},{28,12},{32,48},... | collective-permute-start | bytes 1179656 | tf_op jit(solution)/shard_map/ppermute | solution.py:29
  169.3 23.3 %copy-start.10 = (f32[1,256,1024]{2,1,0:T(8,128)}, f32[1,256,1024]{2,1,0:T(8,128)S(1)}, u32[]{:S(2)}) copy-start(f32[1,256,1024]{2,1,0:T(8,128)S(1)} %fusion.28) | copy-start | bytes 3145732
  189.2 11.5 %collective-permute-start.11 = (bf16[1,2,64,1024]{3,2,1,0:T(8,128)(2,1)S(1)}, bf16[1,2,64,1024]{3,2,1,0:T(8,128)(2,1)S(1)}, u32[]{:S(2)}, u32[]{:S(2)}) collective-permute-start(bf16[1,2,64,1024]{3,2,1,0:T(8,128)(2,1)S(1)} %get-tuple-element.67), channel_id=1, source_target_pairs={{0,32},{4,36},{8,40},{12,44},{16,48},{20,52},{24,56},{28,60},{32,0... | collective-permute-start | bytes 786440 | tf_op jit(solution)/shard_map/ppermute | solution.py:29
  201.2 4.1 %copy-start.8 = (f32[1,384,512]{2,1,0:T(8,128)S(1)}, f32[1,384,512]{2,1,0:T(8,128)}, u32[]{:S(2)}) copy-start(f32[1,384,512]{2,1,0:T(8,128)} %copy.164) | copy-start | bytes 2359300
  206.4 3.9 %copy-start.11 = (f32[1,256,1024]{2,1,0:T(8,128)S(1)}, f32[1,256,1024]{2,1,0:T(8,128)}, u32[]{:S(2)}) copy-start(f32[1,256,1024]{2,1,0:T(8,128)} %copy-done.10) | copy-start | bytes 3145732
  (17 other events, 29.1 us)
Sparse Core Ops, SparseCore 0:
  9.8 28.4 all-gather.1
  108.3 60.0 reduce-scatter.6
  171.0 30.1 reduce-scatter.4
  214.2 47.4 all-reduce.2
where the time goes:
time: 272 us; the launch traced here: 270 us
  waiting for transfers between devices  94.8 us (35%)
  local copies, waits for them, and re-layouts  65.2 us (24%)
  other arithmetic  46.3 us (17%)
  starting transfers between devices  25.3 us (9%)
  matrix products  23.6 us (9%)
  between operations  14.6 us (5%)
    ppermute x8, waiting for transfers between devices, from_partner(): return lax.ppermute(value, axis, pairs)  50.1 us
    psum x1, waiting for transfers between devices, body(): grad_out_weight = lax.psum(weight_share, 'dp').astype(jnp.float32)  44 us
    ppermute x8, starting transfers between devices, from_partner(): return lax.ppermute(value, axis, pairs)  17.3 us
    unnamed x73, local copies, waits for them, and re-layouts  16.6 us
    unnamed x7, other arithmetic  7.65 us
    reshape x8, local copies, waits for them, and re-layouts, halve_rows(): return source.reshape(batch_size, row_total // 2, 2, width_all).mean(axis=2)  7.34 us
  transfers between devices with their start and end apart: 16, of which 7 were waited for; matrix products, arithmetic and copies ran while one was open for 40% of the time, Pallas kernels for 0%

commit v1 on v0

v1 whole, which is shorter than its diff:
```python
import functools
import math

import jax
import jax.numpy as jnp
from jax import lax
from jax.experimental import pallas as pl
from jax.experimental.pallas import tpu as pltpu
from jax.sharding import Mesh, PartitionSpec as P

DH = 128
NR = 128
C = 64
HEADS = 4
ROWS = 256
WIDTH = 512
KEYS = 896
COARSE = 384
JOINT = 768
BF = jnp.bfloat16
F32 = jnp.float32
SCALE = 1.0 / math.sqrt(DH)
LOG2E = math.log2(math.e)
LIMIT = 40 * 1024 * 1024


def params(**kw):
    return pltpu.CompilerParams(vmem_limit_bytes=LIMIT, **kw)


def pool_matrix(rows, positions, flip=False):
    shape = (positions, rows) if flip else (rows, positions)
    r = lax.broadcasted_iota(jnp.int32, shape, 1 if flip else 0)
    p = lax.broadcasted_iota(jnp.int32, shape, 0 if flip else 1)
    l0 = (r < 64) & ((p >> 2) == r)
    l1 = (r >= 64) & (r < 96) & ((p >> 3) == r - 64)
    l2 = (r >= 96) & (r < 112) & ((p >> 4) == r - 96)
    l3 = (r >= 112) & (r < 120) & ((p >> 5) == r - 112)
    out = jnp.where(l0, 0.25, 0.0) + jnp.where(l1, 0.125, 0.0)
    out = out + jnp.where(l2, 0.0625, 0.0) + jnp.where(l3, 0.03125, 0.0)
    return out.astype(BF)


def top_matrix():
    r = lax.broadcasted_iota(jnp.int32, (64, 320), 0)
    j = lax.broadcasted_iota(jnp.int32, (64, 320), 1)
    l0 = (j < 128) & ((j >> 4) == r)
    l1 = (j >= 128) & (j < 192) & (8 + ((j - 128) >> 3) == r)
    l2 = (j >= 192) & (j < 256) & (16 + ((j - 192) >> 2) == r)
    l3 = (j >= 256) & (32 + ((j - 256) >> 1) == r)
    out = jnp.where(l0, 0.0625, 0.0) + jnp.where(l1, 0.125, 0.0)
    out = out + jnp.where(l2, 0.25, 0.0) + jnp.where(l3, 0.5, 0.0)
    return out.astype(BF)


def dot(a, b, dims):
    return lax.dot_general(a, b, (dims, ((), ())), preferred_element_type=F32)


NN = ((1,), (0,))
NT = ((1,), (1,))
TN = ((0,), (0,))


def prep_kernel(where_ref, k_ref, v_ref, own_ref, near_ref, far_ref, last_ref, first_ref):
    z = where_ref[0]
    m = pool_matrix(128, ROWS)
    for part, ref in enumerate((k_ref, v_ref)):
        x = ref[...]
        pooled = dot(m, x, NN).astype(BF)
        own_ref[part] = pooled[0:64]
        near_ref[part] = pooled[64:96]
        mid, low = pooled[96:112], pooled[112:128]
        for j in range(8):
            far_ref[j, part] = jnp.where((z ^ j) >= 4, low, mid)
        last_ref[part] = x[ROWS - NR :]
        first_ref[part] = x[:NR]


def fwd_kernel(
    where_ref, q_ref, k_ref, v_ref, prev_ref, next_ref, own_ref, sib_ref, near_ref, nearo_ref,
    far_ref, faro_ref, att_ref, attt_ref, prob_ref, keys_ref, vals_ref,
):
    z, s = where_ref[0], where_ref[2]
    top = top_matrix()
    for part, ref, out in ((0, k_ref, keys_ref), (1, v_ref, vals_ref)):
        out[0, 0:128] = prev_ref[part]
        out[0, 128:384] = ref[...]
        out[0, 384:448] = own_ref[part]
        out[0, 448:512] = sib_ref[part]
        out[0, 512:544] = near_ref[part]
        out[0, 544:576] = nearo_ref[part]
        for d in (2, 3):
            at = 576 + (d - 2) * 32
            out[0, at : at + 16] = far_ref[z ^ d, part]
            out[0, at + 16 : at + 32] = faro_ref[z ^ d, part]
        for d in range(4, 8):
            at = 640 + (d - 4) * 16
            both = jnp.concatenate([far_ref[z ^ d, part][0:8], faro_ref[z ^ d, part][0:8]], axis=0)
            out[0, at : at + 16] = both
        out[0, 704:768] = dot(top, out[0, 384:704], NN).astype(BF)
        out[0, 768:896] = next_ref[part]
    col = lax.broadcasted_iota(jnp.int32, (1, JOINT), 1)
    for n in range(2):
        q = q_ref[n * NR : (n + 1) * NR]
        scores = dot(q, keys_ref[0, n * NR : n * NR + JOINT], NT)
        if n == 0:
            hidden = (col < NR) & (s == 0)
        else:
            hidden = (col >= JOINT - NR) & (s == 15)
        scores = jnp.where(hidden, -jnp.inf, scores)
        highest = jnp.max(scores, axis=1, keepdims=True)
        e = jnp.exp2((scores - highest) * (SCALE * LOG2E))
        p = (e * (1.0 / jnp.sum(e, axis=1, keepdims=True))).astype(BF)
        prob_ref[0, n] = p
        att = dot(p, vals_ref[0, n * NR : n * NR + JOINT], NN)
        att_ref[n * NR : (n + 1) * NR] = att.astype(BF)
        attt_ref[:, n * NR : (n + 1) * NR] = att.T.astype(BF)


def wgrad_kernel(where_ref, attt_ref, og_ref, mine_ref, theirs_ref):
    c = where_ref[1]
    r = dot(attt_ref[...], og_ref[...], NN)
    lo, hi = r[:, :128].astype(BF), r[:, 128:].astype(BF)
    mine = jnp.where(c == 0, lo, hi)
    theirs = jnp.where(c == 0, hi, lo)
    for i in range(4):
        mine_ref[i, 0] = mine[i * 128 : (i + 1) * 128]
        theirs_ref[i, 0] = theirs[i * 128 : (i + 1) * 128]


def proj_kernel(att_ref, og_ref, w_ref, mix_ref, gatt_ref, acc_ref):
    j = pl.program_id(0)
    w = w_ref[...]
    mix_ref[...] = dot(att_ref[...], w, NN).astype(BF)
    term = dot(og_ref[...], w, NT)

    @pl.when(j == 0)
    def _():
        acc_ref[...] = term

    @pl.when(j > 0)
    def _():
        acc_ref[...] += term

    gatt_ref[...] = acc_ref[...].astype(BF)


def route_kernel(where_ref, mine_ref, got_ref, own_ref, up_ref, down_ref, across_ref):
    me = where_ref[3]
    for shift, out in ((0, own_ref), (1, up_ref), (3, down_ref), (2, across_ref)):
        i = (me + shift) & 3
        out[...] = (mine_ref[i].astype(F32) + got_ref[i].astype(F32)).astype(BF)


def bwd_kernel(
    q_ref, da_ref, att_ref, prob_ref, keys_ref, vals_ref,
    dq_ref, mid_ref, toprev_ref, tonext_ref, own_ref, cross_ref, minec_ref, gk_ref, gv_ref,
):
    gk_ref[768:896] = jnp.zeros((128, DH), F32)
    gv_ref[768:896] = jnp.zeros((128, DH), F32)
    for n in range(2):
        rows = slice(n * NR, (n + 1) * NR)
        span = slice(n * NR, n * NR + JOINT)
        q, da = q_ref[rows], da_ref[rows]
        delta = jnp.sum(da.astype(F32) * att_ref[rows].astype(F32), axis=1, keepdims=True)
        p = prob_ref[0, n]
        pgrad = dot(da, vals_ref[0, span], NT)
        sgrad = (p.astype(F32) * ((pgrad - delta) * SCALE)).astype(BF)
        dq_ref[rows] = dot(sgrad, keys_ref[0, span], NN).astype(BF)
        gk = dot(sgrad, q, TN)
        gv = dot(p, da, TN)
        if n == 0:
            gk_ref[0:768] = gk
            gv_ref[0:768] = gv
        else:
            gk_ref[span] += gk
            gv_ref[span] += gv
    top = top_matrix()
    for part, g in ((0, gk_ref), (1, gv_ref)):
        high = g[704:768]
        hi = high.astype(BF)
        lo = (high - hi.astype(F32)).astype(BF)
        g[384:704] += dot(top, hi, TN) + dot(top, lo, TN)
        toprev_ref[part] = g[0:128].astype(BF)
        mid_ref[part] = g[128:384]
        tonext_ref[part] = g[768:896].astype(BF)
        own_ref[part] = g[384:448]
        cross_ref[part, 0:64] = g[448:512].astype(BF)
        cross_ref[part, 64:96] = g[544:576].astype(BF)
        minec_ref[part, 0:32] = g[512:544]
        for d in (2, 3):
            at, to = 576 + (d - 2) * 32, 32 + (d - 2) * 16
            minec_ref[part, to : to + 16] = g[at : at + 16]
            cross_ref[part, 64 + to : 64 + to + 16] = g[at + 16 : at + 32].astype(BF)
        for d in (4, 6):
            at, to = 640 + (d - 4) * 16, 64 + (d - 4) * 8
            minec_ref[part, to : to + 8] = g[at : at + 8]
            minec_ref[part, to + 8 : to + 16] = g[at + 16 : at + 24]
            both = jnp.concatenate([g[at + 8 : at + 16], g[at + 24 : at + 32]], axis=0)
            cross_ref[part, 64 + to : 64 + to + 16] = both.astype(BF)


def gather_kernel(where_ref, minec_ref, got_ref, near_ref, far_ref):
    z = where_ref[0]
    for part in range(2):
        total = minec_ref[part] + got_ref[part, 64:160].astype(F32)
        near_ref[part] = total[0:32].astype(BF)
        far_ref[z, part] = jnp.zeros((16, WIDTH), BF)
        far_ref[z ^ 1, part] = jnp.zeros((16, WIDTH), BF)
        for d in (2, 3):
            at = 32 + (d - 2) * 16
            far_ref[z ^ d, part] = total[at : at + 16].astype(BF)
        for d in range(4, 8):
            at = 64 + (d - 4) * 8
            piece = jnp.concatenate([total[at : at + 8], jnp.zeros((8, WIDTH), F32)], axis=0)
            far_ref[z ^ d, part] = piece.astype(BF)


def sum_kernel(a_ref, b_ref, c_ref, d_ref, out_ref):
    total = a_ref[...].astype(F32) + b_ref[...].astype(F32)
    out_ref[...] = (total + c_ref[...].astype(F32) + d_ref[...].astype(F32)).astype(BF)


def sum8_kernel(a_ref, out_ref):
    total = a_ref[0].astype(F32)
    for j in range(1, 8):
        total = total + a_ref[j].astype(F32)
    out_ref[...] = total.astype(BF)


def final_kernel(
    where_ref, mid_ref, own_ref, got_ref, near_ref, far_ref, below_ref, above_ref, gk_ref, gv_ref
):
    z = where_ref[0]
    m = pool_matrix(128, ROWS, flip=True)
    for part, out in ((0, gk_ref), (1, gv_ref)):
        l0 = own_ref[part] + got_ref[part, 0:64].astype(F32)
        l1 = near_ref[part].astype(F32)
        l2 = far_ref[z ^ 2, part].astype(F32) + far_ref[z ^ 3, part].astype(F32)
        l3 = far_ref[z ^ 4, part].astype(F32) + far_ref[z ^ 5, part].astype(F32)
        l3 = l3 + far_ref[z ^ 6, part].astype(F32) + far_ref[z ^ 7, part].astype(F32)
        stack = jnp.concatenate([l0, l1, l2, l3], axis=0)
        hi = stack.astype(BF)
        lo = (stack - hi.astype(F32)).astype(BF)
        spread = dot(m, hi, NN) + dot(m, lo, NN)
        total = mid_ref[part] + spread
        out[0:128] = (total[0:128] + below_ref[part].astype(F32)).astype(BF)
        out[128:256] = (total[128:256] + above_ref[part].astype(F32)).astype(BF)


def sds(shape, dtype):
    return jax.ShapeDtypeStruct(shape, dtype)


def smem():
    return pl.BlockSpec(memory_space=pltpu.SMEM)


def vmem():
    return pl.BlockSpec(memory_space=pltpu.VMEM)


def cost(flops, size):
    return pl.CostEstimate(flops=flops, bytes_accessed=size, transcendentals=0)


def whole(kernel, scalars, arrays, outs, estimate):
    return pl.pallas_call(
        kernel,
        out_shape=outs,
        in_specs=[smem()] * len(scalars) + [vmem()] * len(arrays),
        out_specs=[vmem()] * len(outs),
        compiler_params=params(),
        cost_estimate=estimate,
    )(*scalars, *arrays)


def permute(x, axis, move):
    size = lax.axis_size(axis)
    return lax.ppermute(x, axis, [(i, move(i) % size) for i in range(size)])


def body(queries, keys, values, out_weight, out_grad):
    z, core, dp = lax.axis_index("z"), lax.axis_index("core"), lax.axis_index("dp")
    where = jnp.stack([z, core, z * 2 + core, dp]).astype(jnp.int32)
    q, k, v = (x.reshape(ROWS, WIDTH) for x in (queries, keys, values))
    n_seq = 16
    up = [(i, i + 1) for i in range(n_seq - 1)]
    down = [(i + 1, i) for i in range(n_seq - 1)]
    seq = ("z", "core")
    swap = functools.partial(permute, axis="core", move=lambda i: i ^ 1)
    hop = functools.partial(permute, axis="z", move=lambda i: i ^ 1)

    og = lax.all_gather(out_grad.reshape(ROWS, WIDTH), "head", axis=1, tiled=True)

    own, near, far, last, first = whole(
        prep_kernel, [where], [k, v],
        [sds((2, 64, WIDTH), BF), sds((2, 32, WIDTH), BF), sds((8, 2, 16, WIDTH), BF),
         sds((2, NR, WIDTH), BF), sds((2, NR, WIDTH), BF)],
        cost(10**8, 2 * 10**6),
    )
    sib = swap(own)
    near_got = hop(near)
    prev = lax.ppermute(last, seq, up)
    after = lax.ppermute(first, seq, down)
    far_got = lax.all_to_all(far, "z", 0, 0)
    far_other = swap(far_got)
    near_other = swap(near_got)

    by_head = lambda rows: pl.BlockSpec((rows, DH), lambda h: (0, h))
    pair = lambda rows: pl.BlockSpec((2, rows, DH), lambda h: (0, 0, h))
    far_spec = pl.BlockSpec((8, 2, 16, DH), lambda h: (0, 0, 0, h))
    lead = lambda *dims: pl.BlockSpec((1,) + dims, lambda h: (h,) + (0,) * len(dims))
    att, attt, prob, kbuf, vbuf = pl.pallas_call(
        fwd_kernel,
        grid=(HEADS,),
        out_shape=[
            sds((ROWS, WIDTH), BF), sds((WIDTH, ROWS), BF), sds((HEADS, 2, NR, JOINT), BF),
            sds((HEADS, KEYS, DH), BF), sds((HEADS, KEYS, DH), BF),
        ],
        in_specs=[
            smem(), by_head(ROWS), by_head(ROWS), by_head(ROWS), pair(NR), pair(NR),
            pair(64), pair(64), pair(32), pair(32), far_spec, far_spec,
        ],
        out_specs=[
            by_head(ROWS), pl.BlockSpec((DH, ROWS), lambda h: (h, 0)), lead(2, NR, JOINT),
            lead(KEYS, DH), lead(KEYS, DH),
        ],
        compiler_params=params(),
        cost_estimate=cost(6 * 10**9, 4 * 10**6),
    )(where, q, k, v, prev, after, own, sib, near_got, near_other, far_got, far_other)

    piece = pl.BlockSpec((4, 1, 128, 128), lambda j: (0, j, 0, 0))
    mine, theirs = pl.pallas_call(
        wgrad_kernel,
        grid=(8,),
        out_shape=[sds((4, 8, 128, 128), BF)] * 2,
        in_specs=[smem(), vmem(), pl.BlockSpec((ROWS, 256), lambda j: (0, j))],
        out_specs=[piece, piece],
        compiler_params=params(),
        cost_estimate=cost(10**9, 3 * 10**6),
    )(where, attt, og)
    got = swap(theirs)

    mix, gatt = pl.pallas_call(
        proj_kernel,
        grid=(4,),
        out_shape=[sds((ROWS, 2048), BF), sds((ROWS, WIDTH), BF)],
        in_specs=[
            vmem(),
            pl.BlockSpec((ROWS, 512), lambda j: (0, j)),
            pl.BlockSpec((WIDTH, 512), lambda j: (0, j)),
        ],
        out_specs=[
            pl.BlockSpec((ROWS, 512), lambda j: (0, j)),
            pl.BlockSpec((ROWS, WIDTH), lambda j: (0, 0)),
        ],
        scratch_shapes=[pltpu.VMEM((ROWS, WIDTH), F32)],
        compiler_params=params(),
        cost_estimate=cost(2 * 10**9, 4 * 10**6),
    )(att, og, out_weight)
    mixed = lax.psum_scatter(mix, "head", scatter_dimension=1, tiled=True)

    kept, to_up, to_down, to_across = whole(
        route_kernel, [where], [mine, got], [sds((8, 128, 128), BF)] * 4, cost(10**6, 3 * 10**6)
    )
    from_down = permute(to_up, "dp", lambda i: i + 1)
    from_up = permute(to_down, "dp", lambda i: i - 1)
    from_across = permute(to_across, "dp", lambda i: i + 2)

    dq, mid, toprev, tonext, own_grad, cross, minec = pl.pallas_call(
        bwd_kernel,
        grid=(HEADS,),
        out_shape=[
            sds((ROWS, WIDTH), BF), sds((2, ROWS, WIDTH), F32), sds((2, NR, WIDTH), BF),
            sds((2, NR, WIDTH), BF), sds((2, 64, WIDTH), F32), sds((2, 160, WIDTH), BF),
            sds((2, 96, WIDTH), F32),
        ],
        in_specs=[
            by_head(ROWS), by_head(ROWS), by_head(ROWS), lead(2, NR, JOINT), lead(KEYS, DH),
            lead(KEYS, DH),
        ],
        out_specs=[by_head(ROWS), pair(ROWS), pair(NR), pair(NR), pair(64), pair(160), pair(96)],
        scratch_shapes=[pltpu.VMEM((KEYS, DH), F32)] * 2,
        compiler_params=params(),
        cost_estimate=cost(6 * 10**9, 5 * 10**6),
    )(q, gatt, att, prob, kbuf, vbuf)
    cross_got = swap(cross)
    above = lax.ppermute(toprev, seq, down)
    below = lax.ppermute(tonext, seq, up)
    near_grad, far_grad = whole(
        gather_kernel, [where], [minec, cross_got],
        [sds((2, 32, WIDTH), BF), sds((8, 2, 16, WIDTH), BF)], cost(10**6, 10**6),
    )
    near_back = hop(near_grad)

    (wsum,) = whole(
        sum_kernel, [], [kept, from_down, from_up, from_across], [sds((8, 128, 128), BF)],
        cost(10**6, 10**6),
    )
    wsum_got = lax.all_to_all(wsum, "z", 0, 0)
    far_back = lax.all_to_all(far_grad, "z", 0, 0)
    (wpart,) = whole(sum8_kernel, [], [wsum_got], [sds((128, 128), BF)], cost(10**6, 10**5))
    wall = lax.all_gather(wpart, "dp", axis=0, tiled=True)
    grad_out_weight = wall.astype(F32)

    grad_keys, grad_values = whole(
        final_kernel, [where],
        [mid, own_grad, cross_got, near_back, far_back, below, above],
        [sds((ROWS, WIDTH), BF)] * 2, cost(10**8, 3 * 10**6),
    )
    shape = (1, ROWS, WIDTH)
    return (
        mixed.reshape(shape), dq.reshape(shape), grad_keys.reshape(shape),
        grad_values.reshape(shape), grad_out_weight,
    )


def solution(mesh):
    dp, seq, head = (mesh.shape[name] for name in ("dp", "seq", "head"))
    cut = Mesh(mesh.devices.reshape(dp, seq // 2, 2, head), ("dp", "z", "core", "head"))
    rows = P("dp", ("z", "core"), "head")
    return jax.shard_map(
        body,
        mesh=cut,
        in_specs=(rows, rows, rows, P("head", None), rows),
        out_specs=(rows, rows, rows, rows, P("head", ("z", "core"))),
        check_vma=False,
    )
```

time: 272 us -> 136 us (0.50)
  waiting for transfers between devices: 94.8 us -> 33.6 us
  local copies, waits for them, and re-layouts: 65.2 us -> 14.6 us
  other arithmetic: 46.3 us -> 0.8 us
  Pallas kernels: 0 us -> 24.1 us
  matrix products: 23.6 us -> 0 us
  blocking collectives: 0 us -> 12.1 us
  starting transfers between devices: 25.3 us -> 36 us
    psum x1 -> x0, waiting for transfers between devices: 44 us -> none  [body(): grad_out_weight = lax.psum(weight_share, 'dp').astype(jnp.float32)]
    ppermute x12 -> x14, waiting for transfers between devices: 50.1 us -> 23.1 us  [the longest x10 23 us: permute(): return lax.ppermute(x, axis, [(i, move(i) % size) for i in range(size)])]
    pallas_call x0 -> x10, Pallas kernels: none -> 24.1 us  [the longest x6 5.88 us: whole(): pl.pallas_call(kernel, out_shape=outs, in_specs=[smem()] * len(scalars) +...]
    dot_general x15 -> x0, matrix products: 23.6 us -> none  [the longest x1 3.36 us: body(): jnp.einsum('blf,bld->fd', attended_rows, piece_cols, preferred_element_ty...]
    all_to_all x0 -> x3, starting transfers between devices: none -> 19.3 us  [the longest x1 8.46 us: body(): far_got = lax.all_to_all(far, 'z', 0, 0)]
    slice x13 -> x0, local copies, waits for them, and re-layouts: 14.9 us -> none  [the longest x2 3.64 us: body(): window[..., width:].reshape(batch_size, block_count, 3 * NR, head_count, DH)]
    reshape x11 -> x0, local copies, waits for them, and re-layouts: 12.6 us -> none  [the longest x8 7.34 us: halve_rows(): return source.reshape(batch_size, row_total // 2, 2, width_all).mean(axis=2)]
    all_gather x0 -> x1, blocking collectives: none -> 12.1 us  [body(): wall = lax.all_gather(wpart, 'dp', axis=0, tiled=True)]
  transfers between devices with their start and end apart: 16 -> 19, of which waited for: 7 -> 8; matrix products, arithmetic and copies ran while one was open for 40% -> 1% of each run, Pallas kernels for 0% -> 15%
where the time goes in v1:
time: 136 us; the launch traced here: 135 us
  starting transfers between devices  36 us (26%)
  waiting for transfers between devices  33.6 us (25%)
  Pallas kernels  24.1 us (18%)
  local copies, waits for them, and re-layouts  14.6 us (11%)
  between operations  14.2 us (10%)
  blocking collectives  12.1 us (9%)
    ppermute x10, waiting for transfers between devices, permute(): return lax.ppermute(x, axis, [(i, move(i) % size) for i in range(size)])  23 us
    unnamed x48, local copies, waits for them, and re-layouts  14.6 us
    all_gather x1, blocking collectives, body(): wall = lax.all_gather(wpart, 'dp', axis=0, tiled=True)  12.1 us
    ppermute x10, starting transfers between devices, permute(): return lax.ppermute(x, axis, [(i, move(i) % size) for i in range(size)])  11.3 us
    all_to_all x1, waiting for transfers between devices, body(): far_got = lax.all_to_all(far, 'z', 0, 0)  9.83 us
    all_to_all x1, starting transfers between devices, body(): far_got = lax.all_to_all(far, 'z', 0, 0)  8.46 us
    all_to_all x1, starting transfers between devices, body(): wsum_got = lax.all_to_all(wsum, 'z', 0, 0)  6.81 us
    pallas_call x6, Pallas kernels, whole(): pl.pallas_call(kernel, out_shape=outs, in_specs=[smem()] * len(scalars) +...  5.88 us
  transfers between devices with their start and end apart: 19, of which 8 were waited for; matrix products, arithmetic and copies ran while one was open for 1% of the time, Pallas kernels for 15%

profile of v1, /device:TPU:8, one launch (start us, length us, event | category | flops | bytes accessed | tf_op | source)
XLA Modules:
  0.0 135.5 jit_solution(11280321182282501146)
XLA Ops:
  8.0 0.9 copy-done
  9.9 1.5 %shard_map.92 = (bf16[2,64,512]{2,1,0:T(8,128)(2,1)S(1)}, bf16[2,32,512]{2,1,0:T(8,128)(2,1)S(1)}, bf16[8,2,16,512]{3,2,1,0:T(8,128)(2,1)}, bf16[2,128,512]{2,1,0:T(8,128)(2,1)S(1)}, bf16[2,128,512]{2,1,0:T(8,128)(2,1)S(1)}) custom-call(s32[4]{0:T(128)S(1)} %pad_add_fusion.where_ref, bf16[256,512]{1,0:T(8,128)(2,1)S(1)} %bitcast.12, ...), custom_call_target="tpu_custom_call" | custom-call | flops 100000000 | bytes 2000000 | tf_op jit(solution)/shard_map/pallas_call | solution.py:269
  11.4 8.5 %all-to-all-start = ((bf16[8,2,16,512]{3,2,1,0:T(8,128)(2,1)}), bf16[8,2,16,512]{3,2,1,0:T(8,128)(2,1)S(1)}, u32[]{:S(2)}, u32[]{:S(2)}) async-start(bf16[8,2,16,512]{3,2,1,0:T(8,128)(2,1)} %get-tuple-element.38), calls=%async_computation | async-start | bytes 524288 | tf_op jit(solution)/shard_map/all_to_all | solution.py:307
  19.9 1.5 %collective-permute-start = (bf16[2,128,512]{2,1,0:T(8,128)(2,1)S(1)}, bf16[2,128,512]{2,1,0:T(8,128)(2,1)S(1)}, u32[]{:S(2)}, u32[]{:S(2)}) collective-permute-start(bf16[2,128,512]{2,1,0:T(8,128)(2,1)S(1)} %get-tuple-element.34), channel_id=1, source_target_pairs={{0,4},{4,8},{8,12},{12,16},{16,20},{20,24},{24,28},{28,32},{32,36}... | collective-permute-start | bytes 786440 | tf_op jit(solution)/shard_map/ppermute | solution.py:305
  21.4 1.3 collective-permute-start.1
  22.7 9.8 %all-to-all-done.far_ref = bf16[8,2,16,512]{3,2,1,0:T(8,128)(2,1)S(1)} async-done(((bf16[8,2,16,512]{3,2,1,0:T(8,128)(2,1)}), bf16[8,2,16,512]{3,2,1,0:T(8,128)(2,1)S(1)}, u32[]{:S(2)}, u32[]{:S(2)}) %all-to-all-start) | async-done | bytes 262176 | tf_op jit(solution)/shard_map/all_to_all | solution.py:307
  33.0 4.0 %collective-permute-done.3.near_ref = bf16[2,32,512]{2,1,0:T(8,128)(2,1)S(1)} collective-permute-done((bf16[2,32,512]{2,1,0:T(8,128)(2,1)S(1)}, bf16[2,32,512]{2,1,0:T(8,128)(2,1)S(1)}, u32[]{:S(2)}, u32[]{:S(2)}) %collective-permute-start.3) | collective-permute-done | bytes 65568 | tf_op jit(solution)/shard_map/ppermute | solution.py:281
  37.0 1.3 collective-permute-done.4.nearo_ref
  41.2 5.8 %shard_map.93 = (bf16[256,512]{1,0:T(8,128)(2,1)S(1)}, bf16[512,256]{1,0:T(8,128)(2,1)S(1)}, bf16[4,2,128,768]{3,2,1,0:T(8,128)(2,1)S(1)}, bf16[4,896,128]{2,1,0:T(8,128)(2,1)S(1)}, bf16[4,896,128]{2,1,0:T(8,128)(2,1)S(1)}) custom-call(s32[4]{0:T(128)S(1)} %pad_add_fusion.where_ref, bf16[256,512]{1,0:T(8,128)(2,1)S(1)} %bitcast.18, ...), custom_call_target="tpu_custom_call" | custom-call | flops 6000000000 | bytes 4000000 | tf_op jit(solution)/shard_map/pallas_call | solution.py:315
  47.0 1.2 copy-done.18
  49.1 1.0 copy-done.22
  50.1 1.3 copy-done.8
  51.4 3.1 %shard_map.94 = (bf16[256,2048]{1,0:T(8,128)(2,1)}, bf16[256,512]{1,0:T(8,128)(2,1)S(1)}) custom-call(bf16[256,512]{1,0:T(8,128)(2,1)S(1)} %get-tuple-element.39.att_ref, bf16[256,2048]{1,0:T(8,128)(2,1)S(1)} %bitcast.16, bf16[512,2048]{1,0:T(8,128)(2,1)S(1)} %copy-done.7), custom_call_target="tpu_custom_call" | custom-call | flops 2000000000 | bytes 4000000 | tf_op jit(solution)/shard_map/pallas_call | solution.py:346
  55.2 1.2 copy-done.9
  56.5 4.5 %shard_map.98 = (bf16[4,8,128,128]{3,2,1,0:T(8,128)(2,1)S(1)}, bf16[4,8,128,128]{3,2,1,0:T(8,128)(2,1)}) custom-call(s32[4]{0:T(128)S(1)} %pad_add_fusion.where_ref, bf16[512,256]{1,0:T(8,128)(2,1)S(1)} %get-tuple-element.56.attt_ref, bf16[256,2048]{1,0:T(8,128)(2,1)S(1)} %bitcast.17), custom_call_target="tpu_custom_call" | custom-call | flops 1000000000 | bytes 3000000 | tf_op jit(solution)/shard_map/pallas_call | solution.py:335
  61.2 1.2 copy-done.23
  62.3 4.8 %shard_map.95 = (bf16[256,512]{1,0:T(8,128)(2,1)}, f32[2,256,512]{2,1,0:T(8,128)S(1)}, bf16[2,128,512]{2,1,0:T(8,128)(2,1)S(1)}, bf16[2,128,512]{2,1,0:T(8,128)(...) custom-call(bf16[256,512]{1,0:T(8,128)(2,1)S(1)} %bitcast.19, ...), custom_call_target="tpu_custom_call" | custom-call | flops 6000000000 | bytes 5000000 | tf_op jit(solution)/shard_map/pallas_call | solution.py:372
  68.2 1.3 collective-permute-done.6.got_ref
  70.8 4.0 %all-to-all-start.1 = ((bf16[8,2,16,512]{3,2,1,0:T(8,128)(2,1)}), bf16[8,2,16,512]{3,2,1,0:T(8,128)(2,1)}, u32[]{:S(2)}, u32[]{:S(2)}) async-start(bf16[8,2,16,512]{3,2,1,0:T(8,128)(2,1)} %copy-done.4), calls=%async_computation.2 | async-start | bytes 524288 | tf_op jit(solution)/shard_map/all_to_all | solution.py:403
  75.6 1.6 %collective-permute-start.11 = (bf16[8,128,128]{2,1,0:T(8,128)(2,1)S(1)}, bf16[8,128,128]{2,1,0:T(8,128)(2,1)S(1)}, u32[]{:S(2)}, u32[]{:S(2)}) collective-permute-start(bf16[8,128,128]{2,1,0:T(8,128)(2,1)S(1)} %get-tuple-element.60), channel_id=1, source_target_pairs={{0,64},{64,128},{128,192},{192,0},{1,65},{65,129},{129,193},{193,1... | collective-permute-start | bytes 786440 | tf_op jit(solution)/shard_map/ppermute | solution.py:281
  77.2 1.7 %collective-permute-start.12 = (bf16[8,128,128]{2,1,0:T(8,128)(2,1)S(1)}, bf16[8,128,128]{2,1,0:T(8,128)(2,1)S(1)}, u32[]{:S(2)}, u32[]{:S(2)}) collective-permute-start(bf16[8,128,128]{2,1,0:T(8,128)(2,1)S(1)} %get-tuple-element.61), channel_id=1, source_target_pairs={{0,192},{64,0},{128,64},{192,128},{1,193},{65,1},{129,65},{193,129... | collective-permute-start | bytes 786440 | tf_op jit(solution)/shard_map/ppermute | solution.py:281
  79.0 1.8 %collective-permute-start.13 = (bf16[8,128,128]{2,1,0:T(8,128)(2,1)S(1)}, bf16[8,128,128]{2,1,0:T(8,128)(2,1)S(1)}, u32[]{:S(2)}, u32[]{:S(2)}) collective-permute-start(bf16[8,128,128]{2,1,0:T(8,128)(2,1)S(1)} %get-tuple-element.62), channel_id=1, source_target_pairs={{0,128},{64,192},{128,0},{192,64},{1,129},{65,193},{129,1},{193,65... | collective-permute-start | bytes 786440 | tf_op jit(solution)/shard_map/ppermute | solution.py:281
  80.8 4.7 %collective-permute-done.11.b_ref = bf16[8,128,128]{2,1,0:T(8,128)(2,1)S(1)} collective-permute-done((bf16[8,128,128]{2,1,0:T(8,128)(2,1)S(1)}, bf16[8,128,128]{2,1,0:T(8,128)(2,1)S(1)}, u32[]{:S(2)}, u32[]{:S(2)}) %collective-permute-start.11) | collective-permute-done | bytes 262176 | tf_op jit(solution)/shard_map/ppermute | solution.py:281
  86.4 5.7 %collective-permute-done.13.d_ref = bf16[8,128,128]{2,1,0:T(8,128)(2,1)S(1)} collective-permute-done((bf16[8,128,128]{2,1,0:T(8,128)(2,1)S(1)}, bf16[8,128,128]{2,1,0:T(8,128)(2,1)S(1)}, u32[]{:S(2)}, u32[]{:S(2)}) %collective-permute-start.13) | collective-permute-done | bytes 262176 | tf_op jit(solution)/shard_map/ppermute | solution.py:281
  93.0 6.8 %all-to-all-start.2 = ((bf16[8,128,128]{2,1,0:T(8,128)(2,1)}), bf16[8,128,128]{2,1,0:T(8,128)(2,1)S(1)}, u32[]{:S(2)}, u32[]{:S(2)}) async-start(bf16[8,128,128]{2,1,0:T(8,128)(2,1)} %shard_map.100), calls=%async_computation.3 | async-start | bytes 524288 | tf_op jit(solution)/shard_map/all_to_all | solution.py:402
  99.8 1.3 collective-permute-start.8
  101.1 1.3 collective-permute-start.9
  102.4 5.1 %collective-permute-start.7 = (bf16[2,32,512]{2,1,0:T(8,128)(2,1)S(1)}, bf16[2,32,512]{2,1,0:T(8,128)(2,1)S(1)}, u32[]{:S(2)}, u32[]{:S(2)}) collective-permute-start(bf16[2,32,512]{2,1,0:T(8,128)(2,1)S(1)} %get-tuple-element.50), channel_id=1, source_target_pairs={{0,8},{8,0},{16,24},{24,16},{32,40},{40,32},{48,56},{56,48},{1,9},... | collective-permute-start | bytes 196616 | tf_op jit(solution)/shard_map/ppermute | solution.py:281
  107.5 5.2 %collective-permute-done.7.near_ref = bf16[2,32,512]{2,1,0:T(8,128)(2,1)S(1)} collective-permute-done((bf16[2,32,512]{2,1,0:T(8,128)(2,1)S(1)}, bf16[2,32,512]{2,1,0:T(8,128)(2,1)S(1)}, u32[]{:S(2)}, u32[]{:S(2)}) %collective-permute-start.7) | collective-permute-done | bytes 65568 | tf_op jit(solution)/shard_map/ppermute | solution.py:281
  112.6 0.9 copy-done.6
  113.6 2.2 %shard_map.97 = (bf16[256,512]{1,0:T(8,128)(2,1)}, bf16[256,512]{1,0:T(8,128)(2,1)}) custom-call(s32[4]{0:T(128)S(1)} %pad_add_fusion.where_ref, f32[2,256,512]{2,1,0:T(8,128)S(1)} %get-tuple-element.46.mid_ref, f32[2,64,512]{2,1,0:T(8,128)S(1)} %copy-done.6, bf16[2,160,512]{2,1,0:T(8,128)(2,1)S(1)} %collective-permute-done.6.got_ref, ...), custom_call_target="tpu_custom_call" | custom-call | flops 100000000 | bytes 3000000 | tf_op jit(solution)/shard_map/pallas_call | solution.py:269
  115.8 12.1 %all_gather.7 = bf16[512,128]{1,0:T(8,128)(2,1)S(1)} all-gather(bf16[128,128]{1,0:T(8,128)(2,1)S(1)} %shard_map.101), channel_id=1, replica_groups=mesh['dp'=4,'z'=8,'core'=2,'head'=4] {'dp'}, dimensions={0}, use_global_device_ids=true | all-gather | bytes 163840 | tf_op jit(solution)/shard_map/all_gather | solution.py:405
  (69 shorter events, 12.6 us)
Async XLA Ops:
  7.2 42.9 %all-gather.3.cloned.1.call-start = ((), (), s32[]{:S(2)}) async-start(), calls=%async_computation.5 | async-start | bytes 1310720 | tf_op jit(solution)/shard_map/all_gather | solution.py:295
  11.4 21.1 %all-to-all-start = ((bf16[8,2,16,512]{3,2,1,0:T(8,128)(2,1)}), bf16[8,2,16,512]{3,2,1,0:T(8,128)(2,1)S(1)}, u32[]{:S(2)}, u32[]{:S(2)}) async-start(bf16[8,2,16,512]{3,2,1,0:T(8,128)(2,1)} %get-tuple-element.38), calls=%async_computation | async-start | bytes 524288 | tf_op jit(solution)/shard_map/all_to_all | solution.py:307
  19.9 108.8 %reduce-scatter.2.cloned.1.call-start = ((), (), s32[]{:S(2)}) async-start(), calls=%async_computation.4 | async-start | bytes 1310720 | tf_op jit(solution)/shard_map/reduce_scatter | solution.py:363
  19.9 18.4 %collective-permute-start = (bf16[2,128,512]{2,1,0:T(8,128)(2,1)S(1)}, bf16[2,128,512]{2,1,0:T(8,128)(2,1)S(1)}, u32[]{:S(2)}, u32[]{:S(2)}) collective-permute-start(bf16[2,128,512]{2,1,0:T(8,128)(2,1)S(1)} %get-tuple-element.34), channel_id=1, source_target_pairs={{0,4},{4,8},{8,12},{12,16},{16,20},{20,24},{24,28},{28,32},{32,36}... | collective-permute-start | bytes 786440 | tf_op jit(solution)/shard_map/ppermute | solution.py:305
  21.4 16.9 %collective-permute-start.1 = (bf16[2,128,512]{2,1,0:T(8,128)(2,1)S(1)}, bf16[2,128,512]{2,1,0:T(8,128)(2,1)S(1)}, u32[]{:S(2)}, u32[]{:S(2)}) collective-permute-start(bf16[2,128,512]{2,1,0:T(8,128)(2,1)S(1)} %get-tuple-element.35), channel_id=1, source_target_pairs={{4,0},{8,4},{12,8},{16,12},{20,16},{24,20},{28,24},{32,28},{36,32}... | collective-permute-start | bytes 786440 | tf_op jit(solution)/shard_map/ppermute | solution.py:306
  32.5 5.8 %collective-permute-start.5 = (bf16[8,2,16,512]{3,2,1,0:T(8,128)(2,1)S(1)}, bf16[8,2,16,512]{3,2,1,0:T(8,128)(2,1)S(1)}, u32[]{:S(2)}, u32[]{:S(2)}) collective-permute-start(bf16[8,2,16,512]{3,2,1,0:T(8,128)(2,1)S(1)} %all-to-all-done.far_ref), channel_id=1, source_target_pairs={{0,4},{4,0},{1,5},{5,1},{2,6},{6,2},{3,7},{7,3},{8,12},{12,8},{9,1... | collective-permute-start | bytes 786440 | tf_op jit(solution)/shard_map/ppermute | solution.py:281
  32.5 4.5 %collective-permute-start.3 = (bf16[2,32,512]{2,1,0:T(8,128)(2,1)S(1)}, bf16[2,32,512]{2,1,0:T(8,128)(2,1)S(1)}, u32[]{:S(2)}, u32[]{:S(2)}) collective-permute-start(bf16[2,32,512]{2,1,0:T(8,128)(2,1)S(1)} %get-tuple-element.37), channel_id=1, source_target_pairs={{0,8},{8,0},{16,24},{24,16},{32,40},{40,32},{48,56},{56,48},{1,9},... | collective-permute-start | bytes 196616 | tf_op jit(solution)/shard_map/ppermute | solution.py:281
  32.5 5.8 %collective-permute-start.2 = (bf16[2,64,512]{2,1,0:T(8,128)(2,1)S(1)}, bf16[2,64,512]{2,1,0:T(8,128)(2,1)S(1)}, u32[]{:S(2)}, u32[]{:S(2)}) collective-permute-start(bf16[2,64,512]{2,1,0:T(8,128)(2,1)S(1)} %get-tuple-element.36.own_ref), channel_id=1, source_target_pairs={{0,4},{4,0},{1,5},{5,1},{2,6},{6,2},{3,7},{7,3},{8,12},{12,8},{9,1... | collective-permute-start | bytes 393224 | tf_op jit(solution)/shard_map/ppermute | solution.py:281
  37.0 1.3 collective-permute-start.4
  41.2 8.9 %copy-start.7 = (bf16[512,2048]{1,0:T(8,128)(2,1)S(1)}, bf16[512,2048]{1,0:T(8,128)(2,1)}, u32[]{:S(2)}) copy-start(bf16[512,2048]{1,0:T(8,128)(2,1)} %w_ref.1) | copy-start | bytes 6291460
  47.0 1.2 copy-start.18
  50.0 4.5 %copy-start.14 = (bf16[256,512]{1,0:T(8,128)(2,1)}, bf16[256,512]{1,0:T(8,128)(2,1)S(1)}, u32[]{:S(2)}) copy-start(bf16[256,512]{1,0:T(8,128)(2,1)S(1)} %get-tuple-element.39.att_ref) | copy-start | bytes 786436
  50.1 1.3 copy-start.8
  55.2 1.2 copy-start.9
  56.5 4.7 %copy-start.11 = (bf16[1,256,512]{2,1,0:T(8,128)(2,1)S(1)}, bf16[1,256,512]{2,1,0:T(8,128)(2,1)}, u32[]{:S(2)}) copy-start(bf16[1,256,512]{2,1,0:T(8,128)(2,1)} %param.5) | copy-start | bytes 786436
  56.5 4.7 %copy-start.15 = (bf16[256,512]{1,0:T(8,128)(2,1)S(1)}, bf16[256,512]{1,0:T(8,128)(2,1)}, u32[]{:S(2)}) copy-start(bf16[256,512]{1,0:T(8,128)(2,1)} %copy-done.14) | copy-start | bytes 786436
  56.5 4.7 %copy-start.17 = (bf16[256,512]{1,0:T(8,128)(2,1)S(1)}, bf16[256,512]{1,0:T(8,128)(2,1)}, u32[]{:S(2)}) copy-start(bf16[256,512]{1,0:T(8,128)(2,1)} %copy-done.16) | copy-start | bytes 786436
  56.5 4.7 %copy-start.19 = (bf16[4,2,128,768]{3,2,1,0:T(8,128)(2,1)S(1)}, bf16[4,2,128,768]{3,2,1,0:T(8,128)(2,1)}, u32[]{:S(2)}) copy-start(bf16[4,2,128,768]{3,2,1,0:T(8,128)(2,1)} %copy-done.18) | copy-start | bytes 4718596
  56.5 4.7 %copy-start.21 = (bf16[4,896,128]{2,1,0:T(8,128)(2,1)S(1)}, bf16[4,896,128]{2,1,0:T(8,128)(2,1)}, u32[]{:S(2)}) copy-start(bf16[4,896,128]{2,1,0:T(8,128)(2,1)} %copy-done.20) | copy-start | bytes 2752516
  61.0 13.9 %collective-permute-start.10 = (bf16[4,8,128,128]{3,2,1,0:T(8,128)(2,1)}, bf16[4,8,128,128]{3,2,1,0:T(8,128)(2,1)S(1)}, u32[]{:S(2)}, u32[]{:S(2)}) collective-permute-start(bf16[4,8,128,128]{3,2,1,0:T(8,128)(2,1)} %get-tuple-element.58), channel_id=1, source_target_pairs={{0,4},{4,0},{1,5},{5,1},{2,6},{6,2},{3,7},{7,3},{8,12},{12,8},{9,1... | collective-permute-start | bytes 3145736 | tf_op jit(solution)/shard_map/ppermute | solution.py:281
  61.2 1.2 copy-start.23
  67.8 2.2 %copy-start.5 = (f32[2,64,512]{2,1,0:T(8,128)}, f32[2,64,512]{2,1,0:T(8,128)S(1)}, u32[]{:S(2)}) copy-start(f32[2,64,512]{2,1,0:T(8,128)S(1)} %get-tuple-element.47.own_ref) | copy-start | bytes 786436
  67.8 2.2 %copy-start.12 = (bf16[2,128,512]{2,1,0:T(8,128)(2,1)}, bf16[2,128,512]{2,1,0:T(8,128)(2,1)S(1)}, u32[]{:S(2)}) copy-start(bf16[2,128,512]{2,1,0:T(8,128)(2,1)S(1)} %get-tuple-element.53) | copy-start | bytes 786436
  67.8 1.6 %collective-permute-start.6 = (bf16[2,160,512]{2,1,0:T(8,128)(2,1)S(1)}, bf16[2,160,512]{2,1,0:T(8,128)(2,1)S(1)}, u32[]{:S(2)}, u32[]{:S(2)}) collective-permute-start(bf16[2,160,512]{2,1,0:T(8,128)(2,1)S(1)} %get-tuple-element.48), channel_id=1, source_target_pairs={{0,4},{4,0},{1,5},{5,1},{2,6},{6,2},{3,7},{7,3},{8,12},{12,8},{9,1... | collective-permute-start | bytes 983048 | tf_op jit(solution)/shard_map/ppermute | solution.py:281
  70.8 22.2 %all-to-all-start.1 = ((bf16[8,2,16,512]{3,2,1,0:T(8,128)(2,1)}), bf16[8,2,16,512]{3,2,1,0:T(8,128)(2,1)}, u32[]{:S(2)}, u32[]{:S(2)}) async-start(bf16[8,2,16,512]{3,2,1,0:T(8,128)(2,1)} %copy-done.4), calls=%async_computation.2 | async-start | bytes 524288 | tf_op jit(solution)/shard_map/all_to_all | solution.py:403
  75.6 9.9 %collective-permute-start.11 = (bf16[8,128,128]{2,1,0:T(8,128)(2,1)S(1)}, bf16[8,128,128]{2,1,0:T(8,128)(2,1)S(1)}, u32[]{:S(2)}, u32[]{:S(2)}) collective-permute-start(bf16[8,128,128]{2,1,0:T(8,128)(2,1)S(1)} %get-tuple-element.60), channel_id=1, source_target_pairs={{0,64},{64,128},{128,192},{192,0},{1,65},{65,129},{129,193},{193,1... | collective-permute-start | bytes 786440 | tf_op jit(solution)/shard_map/ppermute | solution.py:281
  77.2 9.2 %collective-permute-start.12 = (bf16[8,128,128]{2,1,0:T(8,128)(2,1)S(1)}, bf16[8,128,128]{2,1,0:T(8,128)(2,1)S(1)}, u32[]{:S(2)}, u32[]{:S(2)}) collective-permute-start(bf16[8,128,128]{2,1,0:T(8,128)(2,1)S(1)} %get-tuple-element.61), channel_id=1, source_target_pairs={{0,192},{64,0},{128,64},{192,128},{1,193},{65,1},{129,65},{193,129... | collective-permute-start | bytes 786440 | tf_op jit(solution)/shard_map/ppermute | solution.py:281
  79.0 13.2 %collective-permute-start.13 = (bf16[8,128,128]{2,1,0:T(8,128)(2,1)S(1)}, bf16[8,128,128]{2,1,0:T(8,128)(2,1)S(1)}, u32[]{:S(2)}, u32[]{:S(2)}) collective-permute-start(bf16[8,128,128]{2,1,0:T(8,128)(2,1)S(1)} %get-tuple-element.62), channel_id=1, source_target_pairs={{0,128},{64,192},{128,0},{192,64},{1,129},{65,193},{129,1},{193,65... | collective-permute-start | bytes 786440 | tf_op jit(solution)/shard_map/ppermute | solution.py:281
  93.0 22.8 %all-to-all-start.2 = ((bf16[8,128,128]{2,1,0:T(8,128)(2,1)}), bf16[8,128,128]{2,1,0:T(8,128)(2,1)S(1)}, u32[]{:S(2)}, u32[]{:S(2)}) async-start(bf16[8,128,128]{2,1,0:T(8,128)(2,1)} %shard_map.100), calls=%async_computation.3 | async-start | bytes 524288 | tf_op jit(solution)/shard_map/all_to_all | solution.py:402
  99.8 7.7 %collective-permute-start.8 = (bf16[2,128,512]{2,1,0:T(8,128)(2,1)}, bf16[2,128,512]{2,1,0:T(8,128)(2,1)S(1)}, u32[]{:S(2)}, u32[]{:S(2)}) collective-permute-start(bf16[2,128,512]{2,1,0:T(8,128)(2,1)} %copy-done.13), channel_id=1, source_target_pairs={{0,4},{4,8},{8,12},{12,16},{16,20},{20,24},{24,28},{28,32},{32,36}... | collective-permute-start | bytes 786440 | tf_op jit(solution)/shard_map/ppermute | solution.py:391
  101.1 6.4 %collective-permute-start.9 = (bf16[2,128,512]{2,1,0:T(8,128)(2,1)}, bf16[2,128,512]{2,1,0:T(8,128)(2,1)S(1)}, u32[]{:S(2)}, u32[]{:S(2)}) collective-permute-start(bf16[2,128,512]{2,1,0:T(8,128)(2,1)} %copy-done.12), channel_id=1, source_target_pairs={{4,0},{8,4},{12,8},{16,12},{20,16},{24,20},{28,24},{32,28},{36,32}... | collective-permute-start | bytes 786440 | tf_op jit(solution)/shard_map/ppermute | solution.py:390
  102.4 10.3 %collective-permute-start.7 = (bf16[2,32,512]{2,1,0:T(8,128)(2,1)S(1)}, bf16[2,32,512]{2,1,0:T(8,128)(2,1)S(1)}, u32[]{:S(2)}, u32[]{:S(2)}) collective-permute-start(bf16[2,32,512]{2,1,0:T(8,128)(2,1)S(1)} %get-tuple-element.50), channel_id=1, source_target_pairs={{0,8},{8,0},{16,24},{24,16},{32,40},{40,32},{48,56},{56,48},{1,9},... | collective-permute-start | bytes 196616 | tf_op jit(solution)/shard_map/ppermute | solution.py:281
  (11 other events, 9.7 us)
Sparse Core Ops, SparseCore 0:
  9.8 28.4 all-gather.2
  54.7 20.4 reduce-scatter.1

commit v2 on v1

v2 whole, which is shorter than its diff:
```python
import functools
import math

import jax
import jax.numpy as jnp
from jax import lax
from jax.experimental import pallas as pl
from jax.experimental.pallas import tpu as pltpu
from jax.sharding import Mesh, PartitionSpec as P

DH = 128
NR = 128
C = 64
HEADS = 4
ROWS = 256
WIDTH = 512
NEAR = 704
JOINT = 576
FAR = 192
BF = jnp.bfloat16
F32 = jnp.float32
LIMIT = 36 * 1024 * 1024
SCALE = 1.0 / math.sqrt(DH)
LOG2E = math.log2(math.e)


def pool_matrix(rows, positions, flip=False):
    shape = (positions, rows) if flip else (rows, positions)
    r = lax.broadcasted_iota(jnp.int32, shape, 1 if flip else 0)
    p = lax.broadcasted_iota(jnp.int32, shape, 0 if flip else 1)
    l0 = (r < 64) & ((p >> 2) == r)
    l1 = (r >= 64) & (r < 96) & ((p >> 3) == r - 64)
    l2 = (r >= 96) & (r < 112) & ((p >> 4) == r - 96)
    l3 = (r >= 112) & (r < 120) & ((p >> 5) == r - 112)
    out = jnp.where(l0, 0.25, 0.0) + jnp.where(l1, 0.125, 0.0)
    out = out + jnp.where(l2, 0.0625, 0.0) + jnp.where(l3, 0.03125, 0.0)
    return out.astype(BF)


def top_near():
    r = lax.broadcasted_iota(jnp.int32, (64, 192), 0)
    j = lax.broadcasted_iota(jnp.int32, (64, 192), 1)
    l0 = (j < 128) & ((j >> 4) == r)
    l1 = (j >= 128) & (8 + ((j - 128) >> 3) == r)
    return (jnp.where(l0, 0.0625, 0.0) + jnp.where(l1, 0.125, 0.0)).astype(BF)


def top_far():
    r = lax.broadcasted_iota(jnp.int32, (64, 128), 0)
    j = lax.broadcasted_iota(jnp.int32, (64, 128), 1)
    l2 = (j < 64) & (16 + (j >> 2) == r)
    l3 = (j >= 64) & (32 + ((j - 64) >> 1) == r)
    return (jnp.where(l2, 0.25, 0.0) + jnp.where(l3, 0.5, 0.0)).astype(BF)


def dot(a, b, dims):
    return lax.dot_general(a, b, (dims, ((), ())), preferred_element_type=F32)


NN = ((1,), (0,))
NT = ((1,), (1,))
TN = ((0,), (0,))


def prep_kernel(
    q_hbm, k_hbm, v_hbm, qkv_ref, own_ref, near_ref, far_ref, last_ref, first_ref, sems
):
    z = lax.axis_index("z")
    copies = [
        pltpu.make_async_copy(src, qkv_ref.at[at], sems.at[at])
        for at, src in ((1, k_hbm), (2, v_hbm), (0, q_hbm))
    ]
    for copy in copies:
        copy.start()
    m = pool_matrix(128, ROWS)
    for part in range(2):
        copies[part].wait()
        x = qkv_ref[1 + part]
        pooled = dot(m, x, NN).astype(BF)
        own_ref[part] = pooled[0:64]
        near_ref[part] = pooled[64:96]
        for d in range(8):
            far_ref[z ^ d, part] = pooled[112:128] if d >= 4 else pooled[96:112]
        last_ref[part] = x[ROWS - NR :]
        first_ref[part] = x[:NR]
    copies[2].wait()


def near_kernel(
    qkv_ref, prev_ref, next_ref, own_ref, sib_ref, near_ref, nearo_ref,
    keys_ref, vals_ref, exps_ref, part_ref, max_ref, sum_ref,
):
    s = lax.axis_index("z") * 2 + lax.axis_index("core")
    col = lax.broadcasted_iota(jnp.int32, (1, JOINT), 1)
    for h in range(HEADS):
        at_h = slice(h * DH, (h + 1) * DH)
        for part, out in ((0, keys_ref), (1, vals_ref)):
            out[h, 0:128] = prev_ref[part, :, at_h]
            out[h, 128:384] = qkv_ref[1 + part, :, at_h]
            out[h, 384:448] = own_ref[part, :, at_h]
            out[h, 448:512] = sib_ref[part, :, at_h]
            out[h, 512:544] = near_ref[part, :, at_h]
            out[h, 544:576] = nearo_ref[part, :, at_h]
            out[h, 576:704] = next_ref[part, :, at_h]
        for n in range(2):
            rows = slice(n * NR, (n + 1) * NR)
            span = slice(n * NR, n * NR + JOINT)
            scores = dot(qkv_ref[0, rows, at_h], keys_ref[h, span], NT)
            if n == 0:
                hidden = (col < NR) & (s == 0)
            else:
                hidden = (col >= JOINT - NR) & (s == 15)
            scores = jnp.where(hidden, -jnp.inf, scores)
            highest = jnp.max(scores, axis=1, keepdims=True)
            e = jnp.exp2((scores - highest) * (SCALE * LOG2E))
            max_ref[h, rows] = highest
            sum_ref[h, rows] = jnp.sum(e, axis=1, keepdims=True)
            e = e.astype(BF)
            exps_ref[h, n] = e
            part_ref[rows, at_h] = dot(e, vals_ref[h, span], NN)


def far_kernel(
    qkv_ref, far_ref, faro_ref, keys_ref, vals_ref, part_ref, max_ref, sum_ref,
    att_ref, attt_ref, exps_ref, fkeys_ref, fvals_ref, rnear_ref, rfar_ref,
):
    z = lax.axis_index("z")
    by_near, by_far = top_near(), top_far()
    for h in range(HEADS):
        at_h = slice(h * DH, (h + 1) * DH)
        for part, near, out in ((0, keys_ref, fkeys_ref), (1, vals_ref, fvals_ref)):
            for d in (2, 3):
                at = (d - 2) * 32
                out[h, at : at + 16] = far_ref[z ^ d, part, :, at_h]
                out[h, at + 16 : at + 32] = faro_ref[z ^ d, part, :, at_h]
            for d in range(4, 8):
                at = 64 + (d - 4) * 16
                low, high = far_ref[z ^ d, part, :, at_h], faro_ref[z ^ d, part, :, at_h]
                out[h, at : at + 16] = jnp.concatenate([low[0:8], high[0:8]], axis=0)
            top = dot(by_near, near[h, 384:576], NN) + dot(by_far, out[h, 0:128], NN)
            out[h, 128:192] = top.astype(BF)
        scores = dot(qkv_ref[0, :, at_h], fkeys_ref[h], NT)
        first = max_ref[h]
        highest = jnp.maximum(first, jnp.max(scores, axis=1, keepdims=True))
        e = jnp.exp2((scores - highest) * (SCALE * LOG2E))
        kept = jnp.exp2((first - highest) * (SCALE * LOG2E))
        inverse = 1.0 / (kept * sum_ref[h] + jnp.sum(e, axis=1, keepdims=True))
        e = e.astype(BF)
        exps_ref[h] = e
        rnear_ref[h] = kept * inverse
        rfar_ref[h] = inverse
        att = part_ref[:, at_h] * (kept * inverse) + dot(e, fvals_ref[h], NN) * inverse
        att_ref[:, at_h] = att.astype(BF)
        attt_ref[at_h, :] = att.T.astype(BF)


def wgrad_kernel(attt_ref, og0_ref, og1_ref, og2_ref, og3_ref, mine_ref, theirs_ref):
    c, me = lax.axis_index("core"), lax.axis_index("head")
    for shift, og_ref in enumerate((og0_ref, og1_ref, og2_ref, og3_ref)):
        j = (me + shift) & 3
        r = dot(attt_ref[...], og_ref[...], NN).astype(BF)
        for i in range(4):
            for t in range(2):
                lo = r[i * 128 : (i + 1) * 128, t * 256 : t * 256 + 128]
                hi = r[i * 128 : (i + 1) * 128, t * 256 + 128 : t * 256 + 256]
                mine_ref[i, 2 * j + t] = jnp.where(c == 0, lo, hi)
                theirs_ref[i, 2 * j + t] = jnp.where(c == 0, hi, lo)


def proj_kernel(
    _, att_ref, w_hbm, og0_ref, og1_ref, og2_ref, og3_ref,
    mix0_ref, mix1_ref, mix2_ref, mix3_ref, gatt_ref, w_ref, sems,
):
    me = lax.axis_index("head")
    copies = []
    for shift in range(4):
        at = pl.multiple_of(((me + shift) & 3) * 512, 512)
        copies.append(
            pltpu.make_async_copy(w_hbm.at[:, pl.ds(at, 512)], w_ref.at[shift], sems.at[shift])
        )
    for copy in copies:
        copy.start()
    total = None
    outs = (mix0_ref, mix1_ref, mix2_ref, mix3_ref)
    for shift, og_ref in enumerate((og0_ref, og1_ref, og2_ref, og3_ref)):
        copies[shift].wait()
        w = w_ref[shift]
        outs[shift][...] = dot(att_ref[...], w, NN).astype(BF)
        term = dot(og_ref[...], w, NT)
        total = term if shift == 0 else total + term
    gatt_ref[...] = total.astype(BF)


def route_kernel(mine_ref, got_ref, own_ref, up_ref, down_ref, across_ref):
    me = lax.axis_index("dp")
    for shift, out in ((0, own_ref), (1, up_ref), (3, down_ref), (2, across_ref)):
        i = (me + shift) & 3
        out[...] = (mine_ref[i].astype(F32) + got_ref[i].astype(F32)).astype(BF)


def bwd_kernel(
    _, qkv_ref, da_ref, att_ref, exps_ref, fexps_ref, keys_ref, vals_ref, fkeys_ref, fvals_ref,
    rnear_ref, rfar_ref,
    dq_ref, mid_ref, toprev_ref, tonext_ref, own_ref, cross_ref, minec_ref, gk_ref, gv_ref,
):
    by_near, by_far = top_near(), top_far()
    for h in range(HEADS):
        at_h = slice(h * DH, (h + 1) * DH)
        q, da = qkv_ref[0, :, at_h], da_ref[:, at_h]
        att = att_ref[:, at_h].astype(F32)
        delta = jnp.sum(da.astype(F32) * att, axis=1, keepdims=True)
        p = fexps_ref[h].astype(F32) * rfar_ref[h]
        pgrad = dot(da, fvals_ref[h], NT)
        sgrad = (p * ((pgrad - delta) * SCALE)).astype(BF)
        dq = dot(sgrad, fkeys_ref[h], NN)
        fgk, fgv = dot(sgrad, q, TN), dot(p.astype(BF), da, TN)
        gk, gv = gk_ref.at[h], gv_ref.at[h]
        gk[576:704] = jnp.zeros((128, DH), F32)
        gv[576:704] = jnp.zeros((128, DH), F32)
        for n in range(2):
            rows = slice(n * NR, (n + 1) * NR)
            span = slice(n * NR, n * NR + JOINT)
            p = exps_ref[h, n].astype(F32) * rnear_ref[h, rows]
            pgrad = dot(da[rows], vals_ref[h, span], NT)
            sgrad = (p * ((pgrad - delta[rows]) * SCALE)).astype(BF)
            p = p.astype(BF)
            dq_ref[rows, at_h] = (dq[rows] + dot(sgrad, keys_ref[h, span], NN)).astype(BF)
            if n == 0:
                gk[0:576] = dot(sgrad, q[rows], TN)
                gv[0:576] = dot(p, da[rows], TN)
            else:
                gk[128:704] += dot(sgrad, q[rows], TN)
                gv[128:704] += dot(p, da[rows], TN)
        for part, g, f in ((0, gk, fgk), (1, gv, fgv)):
            high = f[128:192]
            hi = high.astype(BF)
            lo = (high - hi.astype(F32)).astype(BF)
            near = g[384:576] + dot(by_near, hi, TN) + dot(by_near, lo, TN)
            far = f[0:128] + dot(by_far, hi, TN) + dot(by_far, lo, TN)
            toprev_ref[part, :, at_h] = g[0:128].astype(BF)
            mid_ref[part, :, at_h] = g[128:384]
            tonext_ref[part, :, at_h] = g[576:704].astype(BF)
            own_ref[part, :, at_h] = near[0:64]
            cross_ref[part, 0:64, at_h] = near[64:128].astype(BF)
            cross_ref[part, 64:96, at_h] = near[160:192].astype(BF)
            minec_ref[part, 0:32, at_h] = near[128:160]
            for d in (2, 3):
                at, to = (d - 2) * 32, 32 + (d - 2) * 16
                minec_ref[part, to : to + 16, at_h] = far[at : at + 16]
                cross_ref[part, 64 + to : 64 + to + 16, at_h] = far[at + 16 : at + 32].astype(BF)
            for d in (4, 6):
                at, to = 64 + (d - 4) * 16, 64 + (d - 4) * 8
                minec_ref[part, to : to + 8, at_h] = far[at : at + 8]
                minec_ref[part, to + 8 : to + 16, at_h] = far[at + 16 : at + 24]
                both = jnp.concatenate([far[at + 8 : at + 16], far[at + 24 : at + 32]], axis=0)
                cross_ref[part, 64 + to : 64 + to + 16, at_h] = both.astype(BF)


def merge_kernel(_, __, wsum_ref, minec_ref, got_ref, near_ref, out_ref):
    z = lax.axis_index("z")
    out_ref[:, 0:128] = wsum_ref[...]
    none = jnp.zeros((128, 128), BF)
    out_ref[z, 128:256] = none
    out_ref[z ^ 1, 128:256] = none
    for part in range(2):
        total = (minec_ref[part] + got_ref[part, 64:160].astype(F32)).astype(BF)
        near_ref[part] = total[0:32]
        low = total[64:96]
        for d in range(2, 8):
            if d < 4:
                piece = total[32 + (d - 2) * 16 : 48 + (d - 2) * 16]
            else:
                piece = low[(d - 4) * 8 : (d - 4) * 8 + 8]
                piece = jnp.concatenate([piece, jnp.zeros((8, WIDTH), BF)], axis=0)
            for col in range(4):
                at = 128 + part * 64 + col * 16
                out_ref[z ^ d, at : at + 16] = piece[:, col * 128 : (col + 1) * 128]


def sum_kernel(a_ref, b_ref, c_ref, d_ref, out_ref):
    total = a_ref[...].astype(F32) + b_ref[...].astype(F32)
    total = total + c_ref[...].astype(F32) + d_ref[...].astype(F32)
    out_ref[...] = total.astype(BF)


def sum8_kernel(a_ref, _, out_ref):
    total = a_ref[0, 0:128].astype(F32)
    for j in range(1, 8):
        total = total + a_ref[j, 0:128].astype(F32)
    for i in range(4):
        out_ref[i] = total.astype(BF)


def final_kernel(
    mid_ref, own_ref, got_ref, near_ref, far_ref, below_ref, above_ref, _,
    gk_ref, gv_ref,
):
    z = lax.axis_index("z")
    m = pool_matrix(128, ROWS, flip=True)
    for part, out in ((0, gk_ref), (1, gv_ref)):
        l0 = own_ref[part] + got_ref[part, 0:64].astype(F32)
        l1 = near_ref[part].astype(F32)
        base = 128 + part * 64
        far = [far_ref[z ^ d, base : base + 64].astype(F32) for d in range(2, 8)]
        l2, l3 = far[0] + far[1], far[2] + far[3] + far[4] + far[5]
        l2 = jnp.concatenate([l2[i * 16 : (i + 1) * 16] for i in range(4)], axis=1)
        l3 = jnp.concatenate([l3[i * 16 : (i + 1) * 16] for i in range(4)], axis=1)
        stack = jnp.concatenate([l0, l1, l2, l3], axis=0)
        hi = stack.astype(BF)
        lo = (stack - hi.astype(F32)).astype(BF)
        spread = dot(m, hi, NN) + dot(m, lo, NN)
        total = mid_ref[part] + spread
        out[0:128] = (total[0:128] + below_ref[part].astype(F32)).astype(BF)
        out[128:256] = (total[128:256] + above_ref[part].astype(F32)).astype(BF)


def sds(shape, dtype):
    return jax.ShapeDtypeStruct(shape, dtype)


HBM = pl.BlockSpec(memory_space=pltpu.HBM)
VMEM = pl.BlockSpec(memory_space=pltpu.VMEM)
AFTER = pl.BlockSpec(memory_space=pl.ANY)


def call(kernel, operands, outs, scratch=(), us=1, limit=LIMIT):
    return pl.pallas_call(
        kernel,
        out_shape=outs,
        in_specs=[spec for spec, _ in operands],
        out_specs=[VMEM] * len(outs),
        scratch_shapes=list(scratch),
        compiler_params=pltpu.CompilerParams(vmem_limit_bytes=limit),
        cost_estimate=pl.CostEstimate(flops=us * 10**9, bytes_accessed=1, transcendentals=0),
    )(*[array for _, array in operands])


def here(*arrays):
    return [(VMEM, array) for array in arrays]


def permute(x, axis, move):
    size = lax.axis_size(axis)
    return lax.ppermute(x, axis, [(i, move(i) % size) for i in range(size)])


def body(queries, keys, values, out_weight, out_grad):
    q, k, v = (x.reshape(ROWS, WIDTH) for x in (queries, keys, values))
    n_seq = 16
    up = [(i, i + 1) for i in range(n_seq - 1)]
    down = [(i + 1, i) for i in range(n_seq - 1)]
    seq = ("z", "core")
    swap = functools.partial(permute, axis="core", move=lambda i: i ^ 1)
    hop = functools.partial(permute, axis="z", move=lambda i: i ^ 1)
    dma = pltpu.SemaphoreType.DMA

    og = out_grad.reshape(ROWS, WIDTH)

    qkv, own, near, far, last, first = call(
        prep_kernel, [(HBM, q), (HBM, k), (HBM, v)],
        [sds((3, ROWS, WIDTH), BF), sds((2, 64, WIDTH), BF), sds((2, 32, WIDTH), BF),
         sds((8, 2, 16, WIDTH), BF), sds((2, NR, WIDTH), BF), sds((2, NR, WIDTH), BF)],
        [dma((3,))], limit=62 * 1024 * 1024,
    )
    sib = swap(own)
    near_got = hop(near)
    near_other = swap(near_got)
    prev = lax.ppermute(last, seq, up)
    after = lax.ppermute(first, seq, down)
    far_got = lax.all_to_all(far, "z", 0, 0)
    far_other = swap(far_got)
    ogs = [og] + [permute(og, "head", lambda i, m=m: i - m) for m in (1, 2, 3)]

    column = sds((HEADS, ROWS, 1), F32)
    keys_near, vals_near, exps, part, top, total = call(
        near_kernel, here(qkv, prev, after, own, sib, near_got, near_other),
        [sds((HEADS, NEAR, DH), BF), sds((HEADS, NEAR, DH), BF), sds((HEADS, 2, NR, JOINT), BF),
         sds((ROWS, WIDTH), F32), column, column],
        us=20,
    )
    att, attt, far_exps, keys_far, vals_far, rnear, rfar = call(
        far_kernel, here(qkv, far_got, far_other, keys_near, vals_near, part, top, total),
        [sds((ROWS, WIDTH), BF), sds((WIDTH, ROWS), BF), sds((HEADS, ROWS, FAR), BF),
         sds((HEADS, FAR, DH), BF), sds((HEADS, FAR, DH), BF), column, column],
    )
    mine, theirs = call(wgrad_kernel, here(attt, *ogs), [sds((4, 8, 128, 128), BF)] * 2)
    got = swap(theirs)
    *mixes, gatt = call(
        proj_kernel, [(AFTER, mine), (VMEM, att), (HBM, out_weight)] + here(*ogs),
        [sds((ROWS, WIDTH), BF)] * 5, [pltpu.VMEM((4, WIDTH, 512), BF), dma((4,))],
    )
    mix_parts = [mixes[0]]
    mix_parts += [permute(mixes[m], "head", lambda i, m=m: i + m) for m in (1, 2, 3)]

    kept, to_up, to_down, to_across = call(
        route_kernel, here(mine, got), [sds((8, 128, 128), BF)] * 4
    )
    from_down = permute(to_up, "dp", lambda i: i + 1)
    from_up = permute(to_down, "dp", lambda i: i - 1)
    from_across = permute(to_across, "dp", lambda i: i + 2)

    dq, mid, toprev, tonext, own_grad, cross, minec = call(
        bwd_kernel,
        [(AFTER, kept)]
        + here(qkv, gatt, att, exps, far_exps, keys_near, vals_near, keys_far, vals_far)
        + here(rnear, rfar),
        [sds((ROWS, WIDTH), BF), sds((2, ROWS, WIDTH), F32), sds((2, NR, WIDTH), BF),
         sds((2, NR, WIDTH), BF), sds((2, 64, WIDTH), F32), sds((2, 160, WIDTH), BF),
         sds((2, 96, WIDTH), F32)],
        [pltpu.VMEM((HEADS, NEAR, DH), F32)] * 2, us=20,
    )
    cross_got = swap(cross)
    above = lax.ppermute(toprev, seq, down)
    below = lax.ppermute(tonext, seq, up)
    (wsum,) = call(
        sum_kernel, here(kept, from_down, from_up, from_across), [sds((8, 128, 128), BF)], us=8
    )
    near_grad, both = call(
        merge_kernel, [(AFTER, above), (AFTER, below)] + here(wsum, minec, cross_got),
        [sds((2, 32, WIDTH), BF), sds((8, 256, 128), BF)],
    )
    near_back = hop(near_grad)
    both_got = lax.all_to_all(both, "z", 0, 0)
    (mixed,) = call(sum_kernel, here(*mix_parts), [sds((ROWS, WIDTH), BF)])
    (wpart,) = call(
        sum8_kernel, here(both_got) + [(AFTER, mixed)], [sds((4, 128, 128), BF)]
    )
    wall = lax.all_to_all(wpart, "dp", 0, 0)
    grad_out_weight = wall.reshape(WIDTH, 128).astype(F32)

    grad_keys, grad_values = call(
        final_kernel,
        here(mid, own_grad, cross_got, near_back, both_got, below, above) + [(AFTER, wpart)],
        [sds((ROWS, WIDTH), BF)] * 2,
    )
    shape = (1, ROWS, WIDTH)
    return (
        mixed.reshape(shape), dq.reshape(shape), grad_keys.reshape(shape),
        grad_values.reshape(shape), grad_out_weight,
    )


def solution(mesh):
    dp, seq, head = (mesh.shape[name] for name in ("dp", "seq", "head"))
    cut = Mesh(mesh.devices.reshape(dp, seq // 2, 2, head), ("dp", "z", "core", "head"))
    rows = P("dp", ("z", "core"), "head")
    return jax.shard_map(
        body,
        mesh=cut,
        in_specs=(rows, rows, rows, P("head", None), rows),
        out_specs=(rows, rows, rows, rows, P("head", ("z", "core"))),
        check_vma=False,
    )
```

time: 136 us -> 100 us (0.74)
  starting transfers between devices: 36 us -> 50.7 us
  between operations: 14.2 us -> 0.86 us
  blocking collectives: 12.1 us -> 0 us
  local copies, waits for them, and re-layouts: 14.6 us -> 4.22 us
  waiting for transfers between devices: 33.6 us -> 24.3 us
  Pallas kernels: 24.1 us -> 18.9 us
    all_gather x1 -> x0, blocking collectives: 12.1 us -> none  [body(): wall = lax.all_gather(wpart, 'dp', axis=0, tiled=True)]
    ppermute x10 -> x16, starting transfers between devices: 11.3 us -> 21.9 us  [permute(): return lax.ppermute(x, axis, [(i, move(i) % size) for i in range(size)])]
    unnamed x48 -> x16, local copies, waits for them, and re-layouts: 14.6 us -> 4.22 us
    all_to_all x1, waiting for transfers between devices: 9.83 us -> 0.01 us  [body(): far_got = lax.all_to_all(far, 'z', 0, 0)]
    pallas_call x10 -> x12, Pallas kernels: 24.1 us -> 18.9 us  [call(): pl.pallas_call(kernel, out_shape=outs, in_specs=[spec for spec, _ in oper...]
    all_to_all x2, waiting for transfers between devices: 0.01 us -> 3.51 us  [the longest x1 3.51 us: body(): wall = lax.all_to_all(wpart, 'dp', 0, 0)]
    all_to_all x2, starting transfers between devices: 10.9 us -> 13.2 us  [the longest x1 9.91 us: body(): both_got = lax.all_to_all(both, 'z', 0, 0)]
    ppermute x10 -> x16, waiting for transfers between devices: 23 us -> 20.8 us  [permute(): return lax.ppermute(x, axis, [(i, move(i) % size) for i in range(size)])]
  transfers between devices with their start and end apart: 19 -> 23, of which waited for: 8 -> 9; matrix products, arithmetic and copies ran while one was open for 1% -> 0% of each run, Pallas kernels for 15% -> 15%
where the time goes in v2:
time: 100 us; the launch traced here: 99.8 us
  starting transfers between devices  50.7 us (51%)
  waiting for transfers between devices  24.3 us (24%)
  Pallas kernels  18.9 us (19%)
  local copies, waits for them, and re-layouts  4.22 us (4%)
    ppermute x16, starting transfers between devices, permute(): return lax.ppermute(x, axis, [(i, move(i) % size) for i in range(size)])  21.9 us
    ppermute x16, waiting for transfers between devices, permute(): return lax.ppermute(x, axis, [(i, move(i) % size) for i in range(size)])  20.8 us
    pallas_call x12, Pallas kernels, call(): pl.pallas_call(kernel, out_shape=outs, in_specs=[spec for spec, _ in oper...  18.9 us
    all_to_all x1, starting transfers between devices, body(): both_got = lax.all_to_all(both, 'z', 0, 0)  9.91 us
    all_to_all x1, starting transfers between devices, body(): far_got = lax.all_to_all(far, 'z', 0, 0)  8.48 us
    unnamed x16, local copies, waits for them, and re-layouts  4.22 us
    all_to_all x1, waiting for transfers between devices, body(): wall = lax.all_to_all(wpart, 'dp', 0, 0)  3.51 us
    all_to_all x1, starting transfers between devices, body(): wall = lax.all_to_all(wpart, 'dp', 0, 0)  3.33 us
  transfers between devices with their start and end apart: 23, of which 9 were waited for; matrix products, arithmetic and copies ran while one was open for 0% of the time, Pallas kernels for 15%

profile of v2, /device:TPU:8, one launch (start us, length us, event | category | flops | bytes accessed | tf_op | source)
XLA Modules:
  0.0 99.8 jit_solution(16162849036654052301)
XLA Ops:
  0.6 2.6 %shard_map.92 = (bf16[3,256,512]{2,1,0:T(8,128)(2,1)}, bf16[2,64,512]{2,1,0:T(8,128)(2,1)}, bf16[2,32,512]{2,1,0:T(8,128)(2,1)}, bf16[8,2,16,512]{3,2,1,0:T(8,12...) custom-call(bf16[256,512]{1,0:T(8,128)(2,1)} %bitcast.17, bf16[256,512]{1,0:T(8,128)(2,1)} %bitcast.18, ...), custom_call_target="tpu_custom_call" | custom-call | flops 1000000000 | bytes 1 | tf_op jit(solution)/shard_map/pallas_call | solution.py:327
  3.3 8.5 %all-to-all-start = ((bf16[8,2,16,512]{3,2,1,0:T(8,128)(2,1)}), bf16[8,2,16,512]{3,2,1,0:T(8,128)(2,1)S(1)}, u32[]{:S(2)}, u32[]{:S(2)}) async-start(bf16[8,2,16,512]{3,2,1,0:T(8,128)(2,1)} %get-tuple-element.47), calls=%async_computation | async-start | bytes 524288 | tf_op jit(solution)/shard_map/all_to_all | solution.py:370
  11.7 1.5 %collective-permute-start.1 = (bf16[2,128,512]{2,1,0:T(8,128)(2,1)}, bf16[2,128,512]{2,1,0:T(8,128)(2,1)S(1)}, u32[]{:S(2)}, u32[]{:S(2)}) collective-permute-start(bf16[2,128,512]{2,1,0:T(8,128)(2,1)} %get-tuple-element.48), channel_id=1, source_target_pairs={{0,4},{4,8},{8,12},{12,16},{16,20},{20,24},{24,28},{28,32},{32,36}... | collective-permute-start | bytes 786440 | tf_op jit(solution)/shard_map/ppermute | solution.py:368
  13.2 1.3 %collective-permute-start.2 = (bf16[2,128,512]{2,1,0:T(8,128)(2,1)}, bf16[2,128,512]{2,1,0:T(8,128)(2,1)S(1)}, u32[]{:S(2)}, u32[]{:S(2)}) collective-permute-start(bf16[2,128,512]{2,1,0:T(8,128)(2,1)} %get-tuple-element.49), channel_id=1, source_target_pairs={{4,0},{8,4},{12,8},{16,12},{20,16},{24,20},{28,24},{32,28},{36,32}... | collective-permute-start | bytes 786440 | tf_op jit(solution)/shard_map/ppermute | solution.py:369
  14.5 4.9 %collective-permute-start.4 = (bf16[2,32,512]{2,1,0:T(8,128)(2,1)}, bf16[2,32,512]{2,1,0:T(8,128)(2,1)S(1)}, u32[]{:S(2)}, u32[]{:S(2)}) collective-permute-start(bf16[2,32,512]{2,1,0:T(8,128)(2,1)} %get-tuple-element.51), channel_id=1, source_target_pairs={{0,8},{8,0},{16,24},{24,16},{32,40},{40,32},{48,56},{56,48},{1,9},... | collective-permute-start | bytes 196616 | tf_op jit(solution)/shard_map/ppermute | solution.py:344
  19.4 5.4 %collective-permute-done.4.near_ref = bf16[2,32,512]{2,1,0:T(8,128)(2,1)S(1)} collective-permute-done((bf16[2,32,512]{2,1,0:T(8,128)(2,1)}, bf16[2,32,512]{2,1,0:T(8,128)(2,1)S(1)}, u32[]{:S(2)}, u32[]{:S(2)}) %collective-permute-start.4) | collective-permute-done | bytes 65568 | tf_op jit(solution)/shard_map/ppermute | solution.py:344
  24.8 1.6 %collective-permute-start.8 = (bf16[256,512]{1,0:T(8,128)(2,1)S(1)}, bf16[256,512]{1,0:T(8,128)(2,1)S(1)}, u32[]{:S(2)}, u32[]{:S(2)}) collective-permute-start(bf16[256,512]{1,0:T(8,128)(2,1)S(1)} %bitcast.11), channel_id=1, source_target_pairs={{0,1},{1,2},{2,3},{3,0},{4,5},{5,6},{6,7},{7,4},{8,9},{9,10},{10,1... | collective-permute-start | bytes 786440 | tf_op jit(solution)/shard_map/ppermute | solution.py:344
  26.4 2.0 %collective-permute-start.7 = (bf16[256,512]{1,0:T(8,128)(2,1)S(1)}, bf16[256,512]{1,0:T(8,128)(2,1)S(1)}, u32[]{:S(2)}, u32[]{:S(2)}) collective-permute-start(bf16[256,512]{1,0:T(8,128)(2,1)S(1)} %bitcast.12), channel_id=1, source_target_pairs={{0,2},{1,3},{2,0},{3,1},{4,6},{5,7},{6,4},{7,5},{8,10},{9,11},{10,... | collective-permute-start | bytes 786440 | tf_op jit(solution)/shard_map/ppermute | solution.py:344
  28.4 1.4 %collective-permute-start.6 = (bf16[256,512]{1,0:T(8,128)(2,1)S(1)}, bf16[256,512]{1,0:T(8,128)(2,1)S(1)}, u32[]{:S(2)}, u32[]{:S(2)}) collective-permute-start(bf16[256,512]{1,0:T(8,128)(2,1)S(1)} %bitcast.13), channel_id=1, source_target_pairs={{0,3},{1,0},{2,1},{3,2},{4,7},{5,4},{6,5},{7,6},{8,11},{9,8},{10,9... | collective-permute-start | bytes 786440 | tf_op jit(solution)/shard_map/ppermute | solution.py:344
  29.8 1.1 %copy-done.1 = bf16[3,256,512]{2,1,0:T(8,128)(2,1)S(1)} copy-done((bf16[3,256,512]{2,1,0:T(8,128)(2,1)S(1)}, bf16[3,256,512]{2,1,0:T(8,128)(2,1)}, u32[]{:S(2)}) %copy-start.1) | copy-done | bytes 786456
  31.8 2.6 %shard_map.93 = (bf16[4,704,128]{2,1,0:T(8,128)(2,1)S(1)}, bf16[4,704,128]{2,1,0:T(8,128)(2,1)S(1)}, bf16[4,2,128,576]{3,2,1,0:T(8,128)(2,1)S(1)}, f32[256,512]{...) custom-call(bf16[3,256,512]{2,1,0:T(8,128)(2,1)S(1)} %copy-done.1, ...), custom_call_target="tpu_custom_call" | custom-call | flops 20000000000 | bytes 1 | tf_op jit(solution)/shard_map/pallas_call | solution.py:327
  34.4 2.5 %shard_map.94 = (bf16[256,512]{1,0:T(8,128)(2,1)S(1)}, bf16[512,256]{1,0:T(8,128)(2,1)S(1)}, bf16[4,256,192]{2,1,0:T(8,128)(2,1)S(1)}, bf16[4,192,128]{2,1,0:T(8...) custom-call(bf16[3,256,512]{2,1,0:T(8,128)(2,1)S(1)} %copy-done.1, ...), custom_call_target="tpu_custom_call" | custom-call | flops 1000000000 | bytes 1 | tf_op jit(solution)/shard_map/pallas_call | solution.py:327
  37.1 4.9 %collective-permute-done.6.og1_ref = bf16[256,512]{1,0:T(8,128)(2,1)S(1)} collective-permute-done((bf16[256,512]{1,0:T(8,128)(2,1)S(1)}, bf16[256,512]{1,0:T(8,128)(2,1)S(1)}, u32[]{:S(2)}, u32[]{:S(2)}) %collective-permute-start.6) | collective-permute-done | bytes 262176 | tf_op jit(solution)/shard_map/ppermute | solution.py:344
  42.8 1.9 %shard_map.96 = (bf16[256,512]{1,0:T(8,128)(2,1)S(1)}, bf16[256,512]{1,0:T(8,128)(2,1)S(1)}, bf16[256,512]{1,0:T(8,128)(2,1)S(1)}, bf16[256,512]{1,0:T(8,128)(2,1)S(1)}, bf16[256,512]{1,0:T(8,128)(2,1)S(1)}) custom-call(bf16[4,8,128,128]{3,2,1,0:T(8,128)(2,1)S(1)} %get-tuple-element.58._.mine_ref, bf16[256,512]{1,0:T(8,128)(2,1)S(1)} %get-tuple-element.59.att_ref, ...), custom_call_target="tpu_custom_call" | custom-call | flops 1000000000 | bytes 1 | tf_op jit(solution)/shard_map/pallas_call | solution.py:327
  45.7 1.6 %collective-permute-start.16 = (bf16[8,128,128]{2,1,0:T(8,128)(2,1)S(1)}, bf16[8,128,128]{2,1,0:T(8,128)(2,1)S(1)}, u32[]{:S(2)}, u32[]{:S(2)}) collective-permute-start(bf16[8,128,128]{2,1,0:T(8,128)(2,1)S(1)} %get-tuple-element.79), channel_id=1, source_target_pairs={{0,64},{64,128},{128,192},{192,0},{1,65},{65,129},{129,193},{193,1... | collective-permute-start | bytes 786440 | tf_op jit(solution)/shard_map/ppermute | solution.py:344
  47.2 1.7 %collective-permute-start.17 = (bf16[8,128,128]{2,1,0:T(8,128)(2,1)S(1)}, bf16[8,128,128]{2,1,0:T(8,128)(2,1)S(1)}, u32[]{:S(2)}, u32[]{:S(2)}) collective-permute-start(bf16[8,128,128]{2,1,0:T(8,128)(2,1)S(1)} %get-tuple-element.80), channel_id=1, source_target_pairs={{0,192},{64,0},{128,64},{192,128},{1,193},{65,1},{129,65},{193,129... | collective-permute-start | bytes 786440 | tf_op jit(solution)/shard_map/ppermute | solution.py:344
  49.0 1.8 %collective-permute-start.18 = (bf16[8,128,128]{2,1,0:T(8,128)(2,1)S(1)}, bf16[8,128,128]{2,1,0:T(8,128)(2,1)S(1)}, u32[]{:S(2)}, u32[]{:S(2)}) collective-permute-start(bf16[8,128,128]{2,1,0:T(8,128)(2,1)S(1)} %get-tuple-element.81), channel_id=1, source_target_pairs={{0,128},{64,192},{128,0},{192,64},{1,129},{65,193},{129,1},{193,65... | collective-permute-start | bytes 786440 | tf_op jit(solution)/shard_map/ppermute | solution.py:344
  50.8 4.6 %shard_map.99 = (bf16[256,512]{1,0:T(8,128)(2,1)}, f32[2,256,512]{2,1,0:T(8,128)S(1)}, bf16[2,128,512]{2,1,0:T(8,128)(2,1)S(1)}, bf16[2,128,512]{2,1,0:T(8,128)(...) custom-call(bf16[8,128,128]{2,1,0:T(8,128)(2,1)S(1)} %get-tuple-element.65._.a_ref,, ...), custom_call_target="tpu_custom_call" | custom-call | flops 20000000000 | bytes 1 | tf_op jit(solution)/shard_map/pallas_call | solution.py:327
  55.4 1.3 %collective-permute-start.14 = (bf16[2,128,512]{2,1,0:T(8,128)(2,1)S(1)}, bf16[2,128,512]{2,1,0:T(8,128)(2,1)S(1)}, u32[]{:S(2)}, u32[]{:S(2)}) collective-permute-start(bf16[2,128,512]{2,1,0:T(8,128)(2,1)S(1)} %get-tuple-element.77), channel_id=1, source_target_pairs={{4,0},{8,4},{12,8},{16,12},{20,16},{24,20},{28,24},{32,28},{36,32}... | collective-permute-start | bytes 786440 | tf_op jit(solution)/shard_map/ppermute | solution.py:413
  56.7 3.0 %collective-permute-start.15 = (bf16[2,128,512]{2,1,0:T(8,128)(2,1)S(1)}, bf16[2,128,512]{2,1,0:T(8,128)(2,1)S(1)}, u32[]{:S(2)}, u32[]{:S(2)}) collective-permute-start(bf16[2,128,512]{2,1,0:T(8,128)(2,1)S(1)} %get-tuple-element.78), channel_id=1, source_target_pairs={{0,4},{4,8},{8,12},{12,16},{16,20},{20,24},{24,28},{28,32},{32,36}... | collective-permute-start | bytes 786440 | tf_op jit(solution)/shard_map/ppermute | solution.py:414
  60.4 1.5 %collective-permute-done.18.d_ref = bf16[8,128,128]{2,1,0:T(8,128)(2,1)S(1)} collective-permute-done((bf16[8,128,128]{2,1,0:T(8,128)(2,1)S(1)}, bf16[8,128,128]{2,1,0:T(8,128)(2,1)S(1)}, u32[]{:S(2)}, u32[]{:S(2)}) %collective-permute-start.18) | collective-permute-done | bytes 262176 | tf_op jit(solution)/shard_map/ppermute | solution.py:344
  62.9 9.9 %all-to-all-start.1 = ((bf16[8,256,128]{2,1,0:T(8,128)(2,1)}), bf16[8,256,128]{2,1,0:T(8,128)(2,1)S(1)}, u32[]{:S(2)}, u32[]{:S(2)}) async-start(bf16[8,256,128]{2,1,0:T(8,128)(2,1)} %get-tuple-element.84), calls=%async_computation.1 | async-start | bytes 1048576 | tf_op jit(solution)/shard_map/all_to_all | solution.py:423
  73.5 1.9 %collective-permute-start.10 = (bf16[256,512]{1,0:T(8,128)(2,1)S(1)}, bf16[256,512]{1,0:T(8,128)(2,1)S(1)}, u32[]{:S(2)}, u32[]{:S(2)}) collective-permute-start(bf16[256,512]{1,0:T(8,128)(2,1)S(1)} %get-tuple-element.62), channel_id=1, source_target_pairs={{0,2},{1,3},{2,0},{3,1},{4,6},{5,7},{6,4},{7,5},{8,10},{9,11},{10,... | collective-permute-start | bytes 786440 | tf_op jit(solution)/shard_map/ppermute | solution.py:344
  75.4 2.0 %collective-permute-start.11 = (bf16[256,512]{1,0:T(8,128)(2,1)S(1)}, bf16[256,512]{1,0:T(8,128)(2,1)S(1)}, u32[]{:S(2)}, u32[]{:S(2)}) collective-permute-start(bf16[256,512]{1,0:T(8,128)(2,1)S(1)} %get-tuple-element.63), channel_id=1, source_target_pairs={{0,3},{1,0},{2,1},{3,2},{4,7},{5,4},{6,5},{7,6},{8,11},{9,8},{10,9... | collective-permute-start | bytes 786440 | tf_op jit(solution)/shard_map/ppermute | solution.py:344
  77.4 3.6 %collective-permute-done.9.b_ref = bf16[256,512]{1,0:T(8,128)(2,1)S(1)} collective-permute-done((bf16[256,512]{1,0:T(8,128)(2,1)S(1)}, bf16[256,512]{1,0:T(8,128)(2,1)S(1)}, u32[]{:S(2)}, u32[]{:S(2)}) %collective-permute-start.9) | collective-permute-done | bytes 262176 | tf_op jit(solution)/shard_map/ppermute | solution.py:344
  80.9 2.0 %collective-permute-done.10.c_ref = bf16[256,512]{1,0:T(8,128)(2,1)S(1)} collective-permute-done((bf16[256,512]{1,0:T(8,128)(2,1)S(1)}, bf16[256,512]{1,0:T(8,128)(2,1)S(1)}, u32[]{:S(2)}, u32[]{:S(2)}) %collective-permute-start.10) | collective-permute-done | bytes 262176 | tf_op jit(solution)/shard_map/ppermute | solution.py:344
  82.9 2.7 %collective-permute-done.11.d_ref = bf16[256,512]{1,0:T(8,128)(2,1)S(1)} collective-permute-done((bf16[256,512]{1,0:T(8,128)(2,1)S(1)}, bf16[256,512]{1,0:T(8,128)(2,1)S(1)}, u32[]{:S(2)}, u32[]{:S(2)}) %collective-permute-start.11) | collective-permute-done | bytes 262176 | tf_op jit(solution)/shard_map/ppermute | solution.py:344
  86.4 1.7 %collective-permute-start.19 = (bf16[2,32,512]{2,1,0:T(8,128)(2,1)S(1)}, bf16[2,32,512]{2,1,0:T(8,128)(2,1)S(1)}, u32[]{:S(2)}, u32[]{:S(2)}) collective-permute-start(bf16[2,32,512]{2,1,0:T(8,128)(2,1)S(1)} %get-tuple-element.83), channel_id=1, source_target_pairs={{0,8},{8,0},{16,24},{24,16},{32,40},{40,32},{48,56},{56,48},{1,9},... | collective-permute-start | bytes 196616 | tf_op jit(solution)/shard_map/ppermute | solution.py:344
  89.8 3.3 %all-to-all-start.2 = ((bf16[4,128,128]{2,1,0:T(8,128)(2,1)}), bf16[4,128,128]{2,1,0:T(8,128)(2,1)S(1)}, u32[]{:S(2)}, u32[]{:S(2)}) async-start(bf16[4,128,128]{2,1,0:T(8,128)(2,1)} %shard_map.102._), calls=%async_computation.2 | async-start | bytes 262144 | tf_op jit(solution)/shard_map/all_to_all | solution.py:428
  93.1 1.2 %copy-done.7 = f32[2,256,512]{2,1,0:T(8,128)S(1)} copy-done((f32[2,256,512]{2,1,0:T(8,128)S(1)}, f32[2,256,512]{2,1,0:T(8,128)}, u32[]{:S(2)}) %copy-start.7) | copy-done | bytes 1048600
  94.4 1.2 %shard_map.103 = (bf16[256,512]{1,0:T(8,128)(2,1)}, bf16[256,512]{1,0:T(8,128)(2,1)}) custom-call(f32[2,256,512]{2,1,0:T(8,128)S(1)} %copy-done.7, f32[2,64,512]{2,1,0:T(8,128)S(1)} %get-tuple-element.75.own_ref, bf16[2,160,512]{2,1,0:T(8,128)(2,1)S(1)} %collective-permute-done.13.got_ref, bf16[2,32,512]{2,1,0:T(8,128)(2,1)S(1)} %collective-permute-done.19.near_ref, ...), custom_call_target="tpu_custom_call" | custom-call | flops 1000000000 | bytes 1 | tf_op jit(solution)/shard_map/pallas_call | solution.py:327
  95.6 3.5 %all-to-all-done.2 = bf16[4,128,128]{2,1,0:T(8,128)(2,1)S(1)} async-done(((bf16[4,128,128]{2,1,0:T(8,128)(2,1)}), bf16[4,128,128]{2,1,0:T(8,128)(2,1)S(1)}, u32[]{:S(2)}, u32[]{:S(2)}) %all-to-all-start.2) | async-done | bytes 131104 | tf_op jit(solution)/shard_map/all_to_all | solution.py:428
  (43 shorter events, 8.3 us)
Async XLA Ops:
  0.6 24.2 %copy-start.3 = (bf16[1,256,512]{2,1,0:T(8,128)(2,1)S(1)}, bf16[1,256,512]{2,1,0:T(8,128)(2,1)}, u32[]{:S(2)}) copy-start(bf16[1,256,512]{2,1,0:T(8,128)(2,1)} %param.9) | copy-start | bytes 786436
  3.3 26.5 %all-to-all-start = ((bf16[8,2,16,512]{3,2,1,0:T(8,128)(2,1)}), bf16[8,2,16,512]{3,2,1,0:T(8,128)(2,1)S(1)}, u32[]{:S(2)}, u32[]{:S(2)}) async-start(bf16[8,2,16,512]{3,2,1,0:T(8,128)(2,1)} %get-tuple-element.47), calls=%async_computation | async-start | bytes 524288 | tf_op jit(solution)/shard_map/all_to_all | solution.py:370
  11.7 18.0 %collective-permute-start.1 = (bf16[2,128,512]{2,1,0:T(8,128)(2,1)}, bf16[2,128,512]{2,1,0:T(8,128)(2,1)S(1)}, u32[]{:S(2)}, u32[]{:S(2)}) collective-permute-start(bf16[2,128,512]{2,1,0:T(8,128)(2,1)} %get-tuple-element.48), channel_id=1, source_target_pairs={{0,4},{4,8},{8,12},{12,16},{16,20},{20,24},{24,28},{28,32},{32,36}... | collective-permute-start | bytes 786440 | tf_op jit(solution)/shard_map/ppermute | solution.py:368
  13.2 16.6 %collective-permute-start.2 = (bf16[2,128,512]{2,1,0:T(8,128)(2,1)}, bf16[2,128,512]{2,1,0:T(8,128)(2,1)S(1)}, u32[]{:S(2)}, u32[]{:S(2)}) collective-permute-start(bf16[2,128,512]{2,1,0:T(8,128)(2,1)} %get-tuple-element.49), channel_id=1, source_target_pairs={{4,0},{8,4},{12,8},{16,12},{20,16},{24,20},{28,24},{32,28},{36,32}... | collective-permute-start | bytes 786440 | tf_op jit(solution)/shard_map/ppermute | solution.py:369
  14.5 10.3 %collective-permute-start.4 = (bf16[2,32,512]{2,1,0:T(8,128)(2,1)}, bf16[2,32,512]{2,1,0:T(8,128)(2,1)S(1)}, u32[]{:S(2)}, u32[]{:S(2)}) collective-permute-start(bf16[2,32,512]{2,1,0:T(8,128)(2,1)} %get-tuple-element.51), channel_id=1, source_target_pairs={{0,8},{8,0},{16,24},{24,16},{32,40},{40,32},{48,56},{56,48},{1,9},... | collective-permute-start | bytes 196616 | tf_op jit(solution)/shard_map/ppermute | solution.py:344
  19.4 9.0 %collective-permute-start.3 = (bf16[2,64,512]{2,1,0:T(8,128)(2,1)}, bf16[2,64,512]{2,1,0:T(8,128)(2,1)S(1)}, u32[]{:S(2)}, u32[]{:S(2)}) collective-permute-start(bf16[2,64,512]{2,1,0:T(8,128)(2,1)} %get-tuple-element.50.own_ref), channel_id=1, source_target_pairs={{0,4},{4,0},{1,5},{5,1},{2,6},{6,2},{3,7},{7,3},{8,12},{12,8},{9,1... | collective-permute-start | bytes 393224 | tf_op jit(solution)/shard_map/ppermute | solution.py:344
  24.8 1.6 %collective-permute-start.5 = (bf16[2,32,512]{2,1,0:T(8,128)(2,1)S(1)}, bf16[2,32,512]{2,1,0:T(8,128)(2,1)S(1)}, u32[]{:S(2)}, u32[]{:S(2)}) collective-permute-start(bf16[2,32,512]{2,1,0:T(8,128)(2,1)S(1)} %collective-permute-done.4.near_ref), channel_id=1, source_target_pairs={{0,4},{4,0},{1,5},{5,1},{2,6},{6,2},{3,7},{7,3},{8,12},{12,8},{9,1... | collective-permute-start | bytes 196616 | tf_op jit(solution)/shard_map/ppermute | solution.py:344
  24.8 12.1 %collective-permute-start.8 = (bf16[256,512]{1,0:T(8,128)(2,1)S(1)}, bf16[256,512]{1,0:T(8,128)(2,1)S(1)}, u32[]{:S(2)}, u32[]{:S(2)}) collective-permute-start(bf16[256,512]{1,0:T(8,128)(2,1)S(1)} %bitcast.11), channel_id=1, source_target_pairs={{0,1},{1,2},{2,3},{3,0},{4,5},{5,6},{6,7},{7,4},{8,9},{9,10},{10,1... | collective-permute-start | bytes 786440 | tf_op jit(solution)/shard_map/ppermute | solution.py:344
  26.4 10.7 %collective-permute-start.7 = (bf16[256,512]{1,0:T(8,128)(2,1)S(1)}, bf16[256,512]{1,0:T(8,128)(2,1)S(1)}, u32[]{:S(2)}, u32[]{:S(2)}) collective-permute-start(bf16[256,512]{1,0:T(8,128)(2,1)S(1)} %bitcast.12), channel_id=1, source_target_pairs={{0,2},{1,3},{2,0},{3,1},{4,6},{5,7},{6,4},{7,5},{8,10},{9,11},{10,... | collective-permute-start | bytes 786440 | tf_op jit(solution)/shard_map/ppermute | solution.py:344
  28.4 13.6 %collective-permute-start.6 = (bf16[256,512]{1,0:T(8,128)(2,1)S(1)}, bf16[256,512]{1,0:T(8,128)(2,1)S(1)}, u32[]{:S(2)}, u32[]{:S(2)}) collective-permute-start(bf16[256,512]{1,0:T(8,128)(2,1)S(1)} %bitcast.13), channel_id=1, source_target_pairs={{0,3},{1,0},{2,1},{3,2},{4,7},{5,4},{6,5},{7,6},{8,11},{9,8},{10,9... | collective-permute-start | bytes 786440 | tf_op jit(solution)/shard_map/ppermute | solution.py:344
  29.8 4.7 %collective-permute-start = (bf16[8,2,16,512]{3,2,1,0:T(8,128)(2,1)S(1)}, bf16[8,2,16,512]{3,2,1,0:T(8,128)(2,1)S(1)}, u32[]{:S(2)}, u32[]{:S(2)}) collective-permute-start(bf16[8,2,16,512]{3,2,1,0:T(8,128)(2,1)S(1)} %all-to-all-done.far_ref), channel_id=1, source_target_pairs={{0,4},{4,0},{1,5},{5,1},{2,6},{6,2},{3,7},{7,3},{8,12},{12,8},{9,1... | collective-permute-start | bytes 786440 | tf_op jit(solution)/shard_map/ppermute | solution.py:344
  29.8 1.1 %copy-start.1 = (bf16[3,256,512]{2,1,0:T(8,128)(2,1)S(1)}, bf16[3,256,512]{2,1,0:T(8,128)(2,1)}, u32[]{:S(2)}) copy-start(bf16[3,256,512]{2,1,0:T(8,128)(2,1)} %get-tuple-element.46.qkv_ref) | copy-start | bytes 2359300
  30.9 0.9 copy-start.4
  36.9 5.8 %copy-start = (bf16[512,2048]{1,0:T(8,128)(2,1)S(1)}, bf16[512,2048]{1,0:T(8,128)(2,1)}, u32[]{:S(2)}) copy-start(bf16[512,2048]{1,0:T(8,128)(2,1)} %w_hbm.1) | copy-start | bytes 6291460
  42.7 2.7 %collective-permute-start.12 = (bf16[4,8,128,128]{3,2,1,0:T(8,128)(2,1)S(1)}, bf16[4,8,128,128]{3,2,1,0:T(8,128)(2,1)S(1)}, u32[]{:S(2)}, u32[]{:S(2)}) collective-permute-start(bf16[4,8,128,128]{3,2,1,0:T(8,128)(2,1)S(1)} %get-tuple-element.64), channel_id=1, source_target_pairs={{0,4},{4,0},{1,5},{5,1},{2,6},{6,2},{3,7},{7,3},{8,12},{12,8},{9,1... | collective-permute-start | bytes 3145736 | tf_op jit(solution)/shard_map/ppermute | solution.py:344
  44.7 6.1 %copy-start.2 = (bf16[3,256,512]{2,1,0:T(8,128)(2,1)S(1)}, bf16[3,256,512]{2,1,0:T(8,128)(2,1)}, u32[]{:S(2)}) copy-start(bf16[3,256,512]{2,1,0:T(8,128)(2,1)} %get-tuple-element.46.qkv_ref) | copy-start | bytes 2359300
  45.7 14.1 %collective-permute-start.16 = (bf16[8,128,128]{2,1,0:T(8,128)(2,1)S(1)}, bf16[8,128,128]{2,1,0:T(8,128)(2,1)S(1)}, u32[]{:S(2)}, u32[]{:S(2)}) collective-permute-start(bf16[8,128,128]{2,1,0:T(8,128)(2,1)S(1)} %get-tuple-element.79), channel_id=1, source_target_pairs={{0,64},{64,128},{128,192},{192,0},{1,65},{65,129},{129,193},{193,1... | collective-permute-start | bytes 786440 | tf_op jit(solution)/shard_map/ppermute | solution.py:344
  47.2 13.2 %collective-permute-start.17 = (bf16[8,128,128]{2,1,0:T(8,128)(2,1)S(1)}, bf16[8,128,128]{2,1,0:T(8,128)(2,1)S(1)}, u32[]{:S(2)}, u32[]{:S(2)}) collective-permute-start(bf16[8,128,128]{2,1,0:T(8,128)(2,1)S(1)} %get-tuple-element.80), channel_id=1, source_target_pairs={{0,192},{64,0},{128,64},{192,128},{1,193},{65,1},{129,65},{193,129... | collective-permute-start | bytes 786440 | tf_op jit(solution)/shard_map/ppermute | solution.py:344
  49.0 12.9 %collective-permute-start.18 = (bf16[8,128,128]{2,1,0:T(8,128)(2,1)S(1)}, bf16[8,128,128]{2,1,0:T(8,128)(2,1)S(1)}, u32[]{:S(2)}, u32[]{:S(2)}) collective-permute-start(bf16[8,128,128]{2,1,0:T(8,128)(2,1)S(1)} %get-tuple-element.81), channel_id=1, source_target_pairs={{0,128},{64,192},{128,0},{192,64},{1,129},{65,193},{129,1},{193,65... | collective-permute-start | bytes 786440 | tf_op jit(solution)/shard_map/ppermute | solution.py:344
  55.4 6.6 %copy-start.6 = (f32[2,256,512]{2,1,0:T(8,128)}, f32[2,256,512]{2,1,0:T(8,128)S(1)}, u32[]{:S(2)}) copy-start(f32[2,256,512]{2,1,0:T(8,128)S(1)} %get-tuple-element.74.mid_ref) | copy-start | bytes 3145732
  55.4 6.6 %collective-permute-start.14 = (bf16[2,128,512]{2,1,0:T(8,128)(2,1)S(1)}, bf16[2,128,512]{2,1,0:T(8,128)(2,1)S(1)}, u32[]{:S(2)}, u32[]{:S(2)}) collective-permute-start(bf16[2,128,512]{2,1,0:T(8,128)(2,1)S(1)} %get-tuple-element.77), channel_id=1, source_target_pairs={{4,0},{8,4},{12,8},{16,12},{20,16},{24,20},{28,24},{32,28},{36,32}... | collective-permute-start | bytes 786440 | tf_op jit(solution)/shard_map/ppermute | solution.py:413
  56.7 5.4 %collective-permute-start.15 = (bf16[2,128,512]{2,1,0:T(8,128)(2,1)S(1)}, bf16[2,128,512]{2,1,0:T(8,128)(2,1)S(1)}, u32[]{:S(2)}, u32[]{:S(2)}) collective-permute-start(bf16[2,128,512]{2,1,0:T(8,128)(2,1)S(1)} %get-tuple-element.78), channel_id=1, source_target_pairs={{0,4},{4,8},{8,12},{12,16},{16,20},{20,24},{24,28},{28,32},{32,36}... | collective-permute-start | bytes 786440 | tf_op jit(solution)/shard_map/ppermute | solution.py:414
  59.8 2.3 %collective-permute-start.13 = (bf16[2,160,512]{2,1,0:T(8,128)(2,1)S(1)}, bf16[2,160,512]{2,1,0:T(8,128)(2,1)S(1)}, u32[]{:S(2)}, u32[]{:S(2)}) collective-permute-start(bf16[2,160,512]{2,1,0:T(8,128)(2,1)S(1)} %get-tuple-element.76), channel_id=1, source_target_pairs={{0,4},{4,0},{1,5},{5,1},{2,6},{6,2},{3,7},{7,3},{8,12},{12,8},{9,1... | collective-permute-start | bytes 983048 | tf_op jit(solution)/shard_map/ppermute | solution.py:344
  62.9 25.2 %all-to-all-start.1 = ((bf16[8,256,128]{2,1,0:T(8,128)(2,1)}), bf16[8,256,128]{2,1,0:T(8,128)(2,1)S(1)}, u32[]{:S(2)}, u32[]{:S(2)}) async-start(bf16[8,256,128]{2,1,0:T(8,128)(2,1)} %get-tuple-element.84), calls=%async_computation.1 | async-start | bytes 1048576 | tf_op jit(solution)/shard_map/all_to_all | solution.py:423
  72.9 8.1 %collective-permute-start.9 = (bf16[256,512]{1,0:T(8,128)(2,1)S(1)}, bf16[256,512]{1,0:T(8,128)(2,1)S(1)}, u32[]{:S(2)}, u32[]{:S(2)}) collective-permute-start(bf16[256,512]{1,0:T(8,128)(2,1)S(1)} %get-tuple-element.61), channel_id=1, source_target_pairs={{0,1},{1,2},{2,3},{3,0},{4,5},{5,6},{6,7},{7,4},{8,9},{9,10},{10,1... | collective-permute-start | bytes 786440 | tf_op jit(solution)/shard_map/ppermute | solution.py:344
  73.5 9.4 %collective-permute-start.10 = (bf16[256,512]{1,0:T(8,128)(2,1)S(1)}, bf16[256,512]{1,0:T(8,128)(2,1)S(1)}, u32[]{:S(2)}, u32[]{:S(2)}) collective-permute-start(bf16[256,512]{1,0:T(8,128)(2,1)S(1)} %get-tuple-element.62), channel_id=1, source_target_pairs={{0,2},{1,3},{2,0},{3,1},{4,6},{5,7},{6,4},{7,5},{8,10},{9,11},{10,... | collective-permute-start | bytes 786440 | tf_op jit(solution)/shard_map/ppermute | solution.py:344
  75.4 10.2 %collective-permute-start.11 = (bf16[256,512]{1,0:T(8,128)(2,1)S(1)}, bf16[256,512]{1,0:T(8,128)(2,1)S(1)}, u32[]{:S(2)}, u32[]{:S(2)}) collective-permute-start(bf16[256,512]{1,0:T(8,128)(2,1)S(1)} %get-tuple-element.63), channel_id=1, source_target_pairs={{0,3},{1,0},{2,1},{3,2},{4,7},{5,4},{6,5},{7,6},{8,11},{9,8},{10,9... | collective-permute-start | bytes 786440 | tf_op jit(solution)/shard_map/ppermute | solution.py:344
  86.4 6.7 %collective-permute-start.19 = (bf16[2,32,512]{2,1,0:T(8,128)(2,1)S(1)}, bf16[2,32,512]{2,1,0:T(8,128)(2,1)S(1)}, u32[]{:S(2)}, u32[]{:S(2)}) collective-permute-start(bf16[2,32,512]{2,1,0:T(8,128)(2,1)S(1)} %get-tuple-element.83), channel_id=1, source_target_pairs={{0,8},{8,0},{16,24},{24,16},{32,40},{40,32},{48,56},{56,48},{1,9},... | collective-permute-start | bytes 196616 | tf_op jit(solution)/shard_map/ppermute | solution.py:344
  88.2 1.0 copy-start.5
  89.8 9.3 %all-to-all-start.2 = ((bf16[4,128,128]{2,1,0:T(8,128)(2,1)}), bf16[4,128,128]{2,1,0:T(8,128)(2,1)S(1)}, u32[]{:S(2)}, u32[]{:S(2)}) async-start(bf16[4,128,128]{2,1,0:T(8,128)(2,1)} %shard_map.102._), calls=%async_computation.2 | async-start | bytes 262144 | tf_op jit(solution)/shard_map/all_to_all | solution.py:428
  93.1 1.2 %copy-start.7 = (f32[2,256,512]{2,1,0:T(8,128)S(1)}, f32[2,256,512]{2,1,0:T(8,128)}, u32[]{:S(2)}) copy-start(f32[2,256,512]{2,1,0:T(8,128)} %copy-done.6) | copy-start | bytes 3145732

commit v3 on v2

--- a/solution.py
+++ b/solution.py
@@ -63,9 +63,9 @@
 
 
 def prep_kernel(
-    q_hbm, k_hbm, v_hbm, qkv_ref, own_ref, near_ref, far_ref, last_ref, first_ref, sems
-):
-    z = lax.axis_index("z")
+    q_hbm, k_hbm, v_hbm, qkv_ref, chip_ref, near_ref, far_ref, edge_ref, sems
+):
+    z, c = lax.axis_index("z"), lax.axis_index("core")
     copies = [
         pltpu.make_async_copy(src, qkv_ref.at[at], sems.at[at])
         for at, src in ((1, k_hbm), (2, v_hbm), (0, q_hbm))
@@ -77,31 +77,37 @@
         copies[part].wait()
         x = qkv_ref[1 + part]
         pooled = dot(m, x, NN).astype(BF)
-        own_ref[part] = pooled[0:64]
+        chip_ref[part, 0:64] = pooled[0:64]
         near_ref[part] = pooled[64:96]
         for d in range(8):
             far_ref[z ^ d, part] = pooled[112:128] if d >= 4 else pooled[96:112]
-        last_ref[part] = x[ROWS - NR :]
-        first_ref[part] = x[:NR]
+        chip_ref[part, 64:192] = jnp.where(c == 0, x[NR:], x[:NR])
+        edge_ref[part] = jnp.where(c == 0, x[:NR], x[NR:])
     copies[2].wait()
 
 
+def token_kernel(_, __, ___, out_ref):
+    out_ref[...] = jnp.zeros_like(out_ref)
+
+
 def near_kernel(
-    qkv_ref, prev_ref, next_ref, own_ref, sib_ref, near_ref, nearo_ref,
+    _, qkv_ref, edge_ref, chip_ref, sib_ref, near_ref, nearo_ref,
     keys_ref, vals_ref, exps_ref, part_ref, max_ref, sum_ref,
 ):
-    s = lax.axis_index("z") * 2 + lax.axis_index("core")
+    z, c = lax.axis_index("z"), lax.axis_index("core")
+    s = z * 2 + c
     col = lax.broadcasted_iota(jnp.int32, (1, JOINT), 1)
     for h in range(HEADS):
         at_h = slice(h * DH, (h + 1) * DH)
         for part, out in ((0, keys_ref), (1, vals_ref)):
-            out[h, 0:128] = prev_ref[part, :, at_h]
+            beside, across = sib_ref[part, 64:192, at_h], edge_ref[part, :, at_h]
+            out[h, 0:128] = jnp.where(c == 0, across, beside)
             out[h, 128:384] = qkv_ref[1 + part, :, at_h]
-            out[h, 384:448] = own_ref[part, :, at_h]
-            out[h, 448:512] = sib_ref[part, :, at_h]
+            out[h, 384:448] = chip_ref[part, 0:64, at_h]
+            out[h, 448:512] = sib_ref[part, 0:64, at_h]
             out[h, 512:544] = near_ref[part, :, at_h]
             out[h, 544:576] = nearo_ref[part, :, at_h]
-            out[h, 576:704] = next_ref[part, :, at_h]
+            out[h, 576:704] = jnp.where(c == 0, beside, across)
         for n in range(2):
             rows = slice(n * NR, (n + 1) * NR)
             span = slice(n * NR, n * NR + JOINT)
@@ -201,8 +207,9 @@
 def bwd_kernel(
     _, qkv_ref, da_ref, att_ref, exps_ref, fexps_ref, keys_ref, vals_ref, fkeys_ref, fvals_ref,
     rnear_ref, rfar_ref,
-    dq_ref, mid_ref, toprev_ref, tonext_ref, own_ref, cross_ref, minec_ref, gk_ref, gv_ref,
-):
+    dq_ref, mid_ref, edge_ref, own_ref, cross_ref, minec_ref, gk_ref, gv_ref,
+):
+    c = lax.axis_index("core")
     by_near, by_far = top_near(), top_far()
     for h in range(HEADS):
         at_h = slice(h * DH, (h + 1) * DH)
@@ -237,9 +244,10 @@
             lo = (high - hi.astype(F32)).astype(BF)
             near = g[384:576] + dot(by_near, hi, TN) + dot(by_near, lo, TN)
             far = f[0:128] + dot(by_far, hi, TN) + dot(by_far, lo, TN)
-            toprev_ref[part, :, at_h] = g[0:128].astype(BF)
+            before, after = g[0:128].astype(BF), g[576:704].astype(BF)
+            edge_ref[part, :, at_h] = jnp.where(c == 0, before, after)
+            cross_ref[part, 160:288, at_h] = jnp.where(c == 0, after, before)
             mid_ref[part, :, at_h] = g[128:384]
-            tonext_ref[part, :, at_h] = g[576:704].astype(BF)
             own_ref[part, :, at_h] = near[0:64]
             cross_ref[part, 0:64, at_h] = near[64:128].astype(BF)
             cross_ref[part, 64:96, at_h] = near[160:192].astype(BF)
@@ -256,7 +264,7 @@
                 cross_ref[part, 64 + to : 64 + to + 16, at_h] = both.astype(BF)
 
 
-def merge_kernel(_, __, wsum_ref, minec_ref, got_ref, near_ref, out_ref):
+def merge_kernel(_, wsum_ref, minec_ref, got_ref, near_ref, out_ref):
     z = lax.axis_index("z")
     out_ref[:, 0:128] = wsum_ref[...]
     none = jnp.zeros((128, 128), BF)
@@ -283,7 +291,7 @@
     out_ref[...] = total.astype(BF)
 
 
-def sum8_kernel(a_ref, _, out_ref):
+def sum8_kernel(a_ref, out_ref):
     total = a_ref[0, 0:128].astype(F32)
     for j in range(1, 8):
         total = total + a_ref[j, 0:128].astype(F32)
@@ -292,10 +300,10 @@
 
 
 def final_kernel(
-    mid_ref, own_ref, got_ref, near_ref, far_ref, below_ref, above_ref, _,
+    mid_ref, own_ref, got_ref, near_ref, far_ref, edge_ref, _, __,
     gk_ref, gv_ref,
 ):
-    z = lax.axis_index("z")
+    z, c = lax.axis_index("z"), lax.axis_index("core")
     m = pool_matrix(128, ROWS, flip=True)
     for part, out in ((0, gk_ref), (1, gv_ref)):
         l0 = own_ref[part] + got_ref[part, 0:64].astype(F32)
@@ -310,8 +318,9 @@
         lo = (stack - hi.astype(F32)).astype(BF)
         spread = dot(m, hi, NN) + dot(m, lo, NN)
         total = mid_ref[part] + spread
-        out[0:128] = (total[0:128] + below_ref[part].astype(F32)).astype(BF)
-        out[128:256] = (total[128:256] + above_ref[part].astype(F32)).astype(BF)
+        beside, across = got_ref[part, 160:288].astype(F32), edge_ref[part].astype(F32)
+        out[0:128] = (total[0:128] + jnp.where(c == 0, across, beside)).astype(BF)
+        out[128:256] = (total[128:256] + jnp.where(c == 0, beside, across)).astype(BF)
 
 
 def sds(shape, dtype):
@@ -346,34 +355,35 @@
 
 def body(queries, keys, values, out_weight, out_grad):
     q, k, v = (x.reshape(ROWS, WIDTH) for x in (queries, keys, values))
-    n_seq = 16
-    up = [(i, i + 1) for i in range(n_seq - 1)]
-    down = [(i + 1, i) for i in range(n_seq - 1)]
-    seq = ("z", "core")
+    n_seq = 2 * lax.axis_size("z")
+    pairs = [(i, i + 1) for i in range(1, n_seq - 1, 2)]
+    pairs += [(j, i) for i, j in pairs]
+    outer = functools.partial(lax.ppermute, axis_name=("z", "core"), perm=pairs)
     swap = functools.partial(permute, axis="core", move=lambda i: i ^ 1)
     hop = functools.partial(permute, axis="z", move=lambda i: i ^ 1)
     dma = pltpu.SemaphoreType.DMA
 
     og = out_grad.reshape(ROWS, WIDTH)
 
-    qkv, own, near, far, last, first = call(
+    qkv, chip, near, far, edge = call(
         prep_kernel, [(HBM, q), (HBM, k), (HBM, v)],
-        [sds((3, ROWS, WIDTH), BF), sds((2, 64, WIDTH), BF), sds((2, 32, WIDTH), BF),
-         sds((8, 2, 16, WIDTH), BF), sds((2, NR, WIDTH), BF), sds((2, NR, WIDTH), BF)],
+        [sds((3, ROWS, WIDTH), BF), sds((2, 192, WIDTH), BF), sds((2, 32, WIDTH), BF),
+         sds((8, 2, 16, WIDTH), BF), sds((2, NR, WIDTH), BF)],
         [dma((3,))], limit=62 * 1024 * 1024,
     )
-    sib = swap(own)
+    sib = swap(chip)
     near_got = hop(near)
     near_other = swap(near_got)
-    prev = lax.ppermute(last, seq, up)
-    after = lax.ppermute(first, seq, down)
+    edge_got = outer(edge)
     far_got = lax.all_to_all(far, "z", 0, 0)
     far_other = swap(far_got)
     ogs = [og] + [permute(og, "head", lambda i, m=m: i - m) for m in (1, 2, 3)]
 
+    (token,) = call(token_kernel, [(AFTER, x) for x in ogs[1:]], [sds((8, 128), F32)], us=10)
+
     column = sds((HEADS, ROWS, 1), F32)
     keys_near, vals_near, exps, part, top, total = call(
-        near_kernel, here(qkv, prev, after, own, sib, near_got, near_other),
+        near_kernel, [(AFTER, token)] + here(qkv, edge_got, chip, sib, near_got, near_other),
         [sds((HEADS, NEAR, DH), BF), sds((HEADS, NEAR, DH), BF), sds((HEADS, 2, NR, JOINT), BF),
          sds((ROWS, WIDTH), F32), column, column],
         us=20,
@@ -399,38 +409,38 @@
     from_up = permute(to_down, "dp", lambda i: i - 1)
     from_across = permute(to_across, "dp", lambda i: i + 2)
 
-    dq, mid, toprev, tonext, own_grad, cross, minec = call(
+    dq, mid, edge_grad, own_grad, cross, minec = call(
         bwd_kernel,
         [(AFTER, kept)]
         + here(qkv, gatt, att, exps, far_exps, keys_near, vals_near, keys_far, vals_far)
         + here(rnear, rfar),
         [sds((ROWS, WIDTH), BF), sds((2, ROWS, WIDTH), F32), sds((2, NR, WIDTH), BF),
-         sds((2, NR, WIDTH), BF), sds((2, 64, WIDTH), F32), sds((2, 160, WIDTH), BF),
+         sds((2, 64, WIDTH), F32), sds((2, 288, WIDTH), BF),
          sds((2, 96, WIDTH), F32)],
         [pltpu.VMEM((HEADS, NEAR, DH), F32)] * 2, us=20,
     )
     cross_got = swap(cross)
-    above = lax.ppermute(toprev, seq, down)
-    below = lax.ppermute(tonext, seq, up)
+    edge_back = outer(edge_grad)
     (wsum,) = call(
         sum_kernel, here(kept, from_down, from_up, from_across), [sds((8, 128, 128), BF)], us=8
     )
     near_grad, both = call(
-        merge_kernel, [(AFTER, above), (AFTER, below)] + here(wsum, minec, cross_got),
+        merge_kernel, [(AFTER, edge_back)] + here(wsum, minec, cross_got),
         [sds((2, 32, WIDTH), BF), sds((8, 256, 128), BF)],
     )
     near_back = hop(near_grad)
     both_got = lax.all_to_all(both, "z", 0, 0)
     (mixed,) = call(sum_kernel, here(*mix_parts), [sds((ROWS, WIDTH), BF)])
     (wpart,) = call(
-        sum8_kernel, here(both_got) + [(AFTER, mixed)], [sds((4, 128, 128), BF)]
+        sum8_kernel, here(both_got), [sds((4, 128, 128), BF)], us=20
     )
     wall = lax.all_to_all(wpart, "dp", 0, 0)
     grad_out_weight = wall.reshape(WIDTH, 128).astype(F32)
 
     grad_keys, grad_values = call(
         final_kernel,
-        here(mid, own_grad, cross_got, near_back, both_got, below, above) + [(AFTER, wpart)],
+        here(mid, own_grad, cross_got, near_back, both_got, edge_back)
+        + [(AFTER, wpart), (AFTER, mixed)],
         [sds((ROWS, WIDTH), BF)] * 2,
     )
     shape = (1, ROWS, WIDTH)

time: 100 us -> 91.3 us (0.913)
  starting transfers between devices: 50.7 us -> 43.4 us
  local copies, waits for them, and re-layouts: 4.22 us -> 2.41 us
    ppermute x16, waiting for transfers between devices: 20.8 us -> 3.64 us  [permute(): return lax.ppermute(x, axis, [(i, move(i) % size) for i in range(size)])]
    all_to_all x1, waiting for transfers between devices: 0.01 us -> 11.3 us  [body(): both_got = lax.all_to_all(both, 'z', 0, 0)]
    all_to_all x1, waiting for transfers between devices: 0.01 us -> 7.03 us  [body(): far_got = lax.all_to_all(far, 'z', 0, 0)]
    ppermute x4 -> x2, starting transfers between devices: 7.08 us -> 1.33 us  [the longest x1 0.67 us: body(): edge_got = outer(edge)]
    all_to_all x1, starting transfers between devices: 9.91 us -> 7.64 us  [body(): both_got = lax.all_to_all(both, 'z', 0, 0)]
    unnamed x16 -> x18, local copies, waits for them, and re-layouts: 4.22 us -> 2.41 us
    ppermute x16, starting transfers between devices: 21.9 us -> 23.5 us  [permute(): return lax.ppermute(x, axis, [(i, move(i) % size) for i in range(size)])]
    all_to_all x1, waiting for transfers between devices: 3.51 us -> 2.43 us  [body(): wall = lax.all_to_all(wpart, 'dp', 0, 0)]
  transfers between devices with their start and end apart: 23 -> 21, of which waited for: 9 -> 6; matrix products, arithmetic and copies ran while one was open for 0% -> 0% of each run, Pallas kernels for 15% -> 16%
where the time goes in v3:
time: 91.3 us; the launch traced here: 90.8 us
  starting transfers between devices  43.4 us (48%)
  waiting for transfers between devices  24.4 us (27%)
  Pallas kernels  19 us (21%)
  local copies, waits for them, and re-layouts  2.41 us (3%)
    ppermute x16, starting transfers between devices, permute(): return lax.ppermute(x, axis, [(i, move(i) % size) for i in range(size)])  23.5 us
    pallas_call x13, Pallas kernels, call(): pl.pallas_call(kernel, out_shape=outs, in_specs=[spec for spec, _ in oper...  19 us
    all_to_all x1, waiting for transfers between devices, body(): both_got = lax.all_to_all(both, 'z', 0, 0)  11.3 us
    all_to_all x1, starting transfers between devices, body(): both_got = lax.all_to_all(both, 'z', 0, 0)  7.64 us
    all_to_all x1, starting transfers between devices, body(): far_got = lax.all_to_all(far, 'z', 0, 0)  7.57 us
    all_to_all x1, waiting for transfers between devices, body(): far_got = lax.all_to_all(far, 'z', 0, 0)  7.03 us
    ppermute x16, waiting for transfers between devices, permute(): return lax.ppermute(x, axis, [(i, move(i) % size) for i in range(size)])  3.64 us
    all_to_all x1, starting transfers between devices, body(): wall = lax.all_to_all(wpart, 'dp', 0, 0)  3.32 us
  transfers between devices with their start and end apart: 21, of which 6 were waited for; matrix products, arithmetic and copies ran while one was open for 0% of the time, Pallas kernels for 16%

profile of v3, /device:TPU:8, one launch (start us, length us, event | category | flops | bytes accessed | tf_op | source)
XLA Modules:
  0.0 90.8 jit_solution(16025074876486501414)
XLA Ops:
  0.6 1.7 %collective-permute-start.3 = (bf16[256,512]{1,0:T(8,128)(2,1)}, bf16[256,512]{1,0:T(8,128)(2,1)S(1)}, u32[]{:S(2)}, u32[]{:S(2)}) collective-permute-start(bf16[256,512]{1,0:T(8,128)(2,1)} %bitcast.11), channel_id=1, source_target_pairs={{0,1},{1,2},{2,3},{3,0},{4,5},{5,6},{6,7},{7,4},{8,9},{9,10},{10,1... | collective-permute-start | bytes 786440 | tf_op jit(solution)/shard_map/ppermute | solution.py:353
  2.3 2.7 %collective-permute-start.2 = (bf16[256,512]{1,0:T(8,128)(2,1)}, bf16[256,512]{1,0:T(8,128)(2,1)S(1)}, u32[]{:S(2)}, u32[]{:S(2)}) collective-permute-start(bf16[256,512]{1,0:T(8,128)(2,1)} %bitcast.12), channel_id=1, source_target_pairs={{0,2},{1,3},{2,0},{3,1},{4,6},{5,7},{6,4},{7,5},{8,10},{9,11},{10,... | collective-permute-start | bytes 786440 | tf_op jit(solution)/shard_map/ppermute | solution.py:353
  5.0 0.7 collective-permute-start.1
  5.6 2.6 %shard_map.92 = (bf16[3,256,512]{2,1,0:T(8,128)(2,1)}, bf16[2,192,512]{2,1,0:T(8,128)(2,1)}, bf16[2,32,512]{2,1,0:T(8,128)(2,1)}, bf16[8,2,16,512]{3,2,1,0:T(8,128)(2,1)}, bf16[2,128,512]{2,1,0:T(8,128)(2,1)}) custom-call(bf16[256,512]{1,0:T(8,128)(2,1)} %bitcast.17, bf16[256,512]{1,0:T(8,128)(2,1)} %bitcast.18, bf16[256,512]{1,0:T(8,128)(2,1)} %bitcast.19), custom_call_target="tpu_custom_call" | custom-call | flops 1000000000 | bytes 1 | tf_op jit(solution)/shard_map/pallas_call | solution.py:336
  8.2 2.0 %collective-permute-start.6 = (bf16[2,32,512]{2,1,0:T(8,128)(2,1)}, bf16[2,32,512]{2,1,0:T(8,128)(2,1)S(1)}, u32[]{:S(2)}, u32[]{:S(2)}) collective-permute-start(bf16[2,32,512]{2,1,0:T(8,128)(2,1)} %get-tuple-element.48), channel_id=1, source_target_pairs={{0,8},{8,0},{16,24},{24,16},{32,40},{40,32},{48,56},{56,48},{1,9},... | collective-permute-start | bytes 196616 | tf_op jit(solution)/shard_map/ppermute | solution.py:353
  10.2 7.6 %all-to-all-start = ((bf16[8,2,16,512]{3,2,1,0:T(8,128)(2,1)}), bf16[8,2,16,512]{3,2,1,0:T(8,128)(2,1)S(1)}, u32[]{:S(2)}, u32[]{:S(2)}) async-start(bf16[8,2,16,512]{3,2,1,0:T(8,128)(2,1)} %get-tuple-element.45), calls=%async_computation | async-start | bytes 524288 | tf_op jit(solution)/shard_map/all_to_all | solution.py:378
  18.5 3.5 %collective-permute-start.5 = (bf16[2,192,512]{2,1,0:T(8,128)(2,1)}, bf16[2,192,512]{2,1,0:T(8,128)(2,1)S(1)}, u32[]{:S(2)}, u32[]{:S(2)}) collective-permute-start(bf16[2,192,512]{2,1,0:T(8,128)(2,1)} %get-tuple-element.47.chip_ref), channel_id=1, source_target_pairs={{0,4},{4,0},{1,5},{5,1},{2,6},{6,2},{3,7},{7,3},{8,12},{12,8},{9,1... | collective-permute-start | bytes 1179656 | tf_op jit(solution)/shard_map/ppermute | solution.py:353
  22.1 7.0 %all-to-all-done.far_ref = bf16[8,2,16,512]{3,2,1,0:T(8,128)(2,1)S(1)} async-done(((bf16[8,2,16,512]{3,2,1,0:T(8,128)(2,1)}), bf16[8,2,16,512]{3,2,1,0:T(8,128)(2,1)S(1)}, u32[]{:S(2)}, u32[]{:S(2)}) %all-to-all-start) | async-done | bytes 262176 | tf_op jit(solution)/shard_map/all_to_all | solution.py:378
  29.1 2.6 %shard_map.94 = (bf16[4,704,128]{2,1,0:T(8,128)(2,1)S(1)}, bf16[4,704,128]{2,1,0:T(8,128)(2,1)S(1)}, bf16[4,2,128,576]{3,2,1,0:T(8,128)(2,1)S(1)}, f32[256,512]{...) custom-call(f32[8,128]{1,0:T(8,128)S(1)} %shard_map.93._, bf16[3,256,512]{2,1,0:T(8,128)(2,1)S(1)} %copy-done.1, ...), custom_call_target="tpu_custom_call" | custom-call | flops 20000000000 | bytes 1 | tf_op jit(solution)/shard_map/pallas_call | solution.py:336
  31.8 2.5 %shard_map.95 = (bf16[256,512]{1,0:T(8,128)(2,1)S(1)}, bf16[512,256]{1,0:T(8,128)(2,1)S(1)}, bf16[4,256,192]{2,1,0:T(8,128)(2,1)S(1)}, bf16[4,192,128]{2,1,0:T(8...) custom-call(bf16[3,256,512]{2,1,0:T(8,128)(2,1)S(1)} %copy-done.1, ...), custom_call_target="tpu_custom_call" | custom-call | flops 1000000000 | bytes 1 | tf_op jit(solution)/shard_map/pallas_call | solution.py:336
  34.3 0.7 shard_map.96
  35.9 1.9 %shard_map.97 = (bf16[256,512]{1,0:T(8,128)(2,1)S(1)}, bf16[256,512]{1,0:T(8,128)(2,1)S(1)}, bf16[256,512]{1,0:T(8,128)(2,1)S(1)}, bf16[256,512]{1,0:T(8,128)(2,1)S(1)}, bf16[256,512]{1,0:T(8,128)(2,1)S(1)}) custom-call(bf16[4,8,128,128]{3,2,1,0:T(8,128)(2,1)S(1)} %get-tuple-element.55._.mine_ref, bf16[256,512]{1,0:T(8,128)(2,1)S(1)} %get-tuple-element.56.att_ref, ...), custom_call_target="tpu_custom_call" | custom-call | flops 1000000000 | bytes 1 | tf_op jit(solution)/shard_map/pallas_call | solution.py:336
  38.2 1.6 %collective-permute-start.14 = (bf16[8,128,128]{2,1,0:T(8,128)(2,1)S(1)}, bf16[8,128,128]{2,1,0:T(8,128)(2,1)S(1)}, u32[]{:S(2)}, u32[]{:S(2)}) collective-permute-start(bf16[8,128,128]{2,1,0:T(8,128)(2,1)S(1)} %get-tuple-element.75), channel_id=1, source_target_pairs={{0,64},{64,128},{128,192},{192,0},{1,65},{65,129},{129,193},{193,1... | collective-permute-start | bytes 786440 | tf_op jit(solution)/shard_map/ppermute | solution.py:353
  39.7 1.7 %collective-permute-start.15 = (bf16[8,128,128]{2,1,0:T(8,128)(2,1)S(1)}, bf16[8,128,128]{2,1,0:T(8,128)(2,1)S(1)}, u32[]{:S(2)}, u32[]{:S(2)}) collective-permute-start(bf16[8,128,128]{2,1,0:T(8,128)(2,1)S(1)} %get-tuple-element.76), channel_id=1, source_target_pairs={{0,192},{64,0},{128,64},{192,128},{1,193},{65,1},{129,65},{193,129... | collective-permute-start | bytes 786440 | tf_op jit(solution)/shard_map/ppermute | solution.py:353
  41.5 1.8 %collective-permute-start.16 = (bf16[8,128,128]{2,1,0:T(8,128)(2,1)S(1)}, bf16[8,128,128]{2,1,0:T(8,128)(2,1)S(1)}, u32[]{:S(2)}, u32[]{:S(2)}) collective-permute-start(bf16[8,128,128]{2,1,0:T(8,128)(2,1)S(1)} %get-tuple-element.77), channel_id=1, source_target_pairs={{0,128},{64,192},{128,0},{192,64},{1,129},{65,193},{129,1},{193,65... | collective-permute-start | bytes 786440 | tf_op jit(solution)/shard_map/ppermute | solution.py:353
  43.3 4.7 %shard_map.100 = (bf16[256,512]{1,0:T(8,128)(2,1)}, f32[2,256,512]{2,1,0:T(8,128)S(1)}, bf16[2,128,512]{2,1,0:T(8,128)(2,1)S(1)}, f32[2,64,512]{2,1,0:T(8,128)S(...) custom-call(bf16[8,128,128]{2,1,0:T(8,128)(2,1)S(1)} %get-tuple-element.62._.a_ref, ...), custom_call_target="tpu_custom_call" | custom-call | flops 20000000000 | bytes 1 | tf_op jit(solution)/shard_map/pallas_call | solution.py:336
  48.0 0.7 copy-done.7
  49.4 1.8 %collective-permute-start.12 = (bf16[2,288,512]{2,1,0:T(8,128)(2,1)S(1)}, bf16[2,288,512]{2,1,0:T(8,128)(2,1)S(1)}, u32[]{:S(2)}, u32[]{:S(2)}) collective-permute-start(bf16[2,288,512]{2,1,0:T(8,128)(2,1)S(1)} %get-tuple-element.73), channel_id=1, source_target_pairs={{0,4},{4,0},{1,5},{5,1},{2,6},{6,2},{3,7},{7,3},{8,12},{12,8},{9,1... | collective-permute-start | bytes 1769480 | tf_op jit(solution)/shard_map/ppermute | solution.py:353
  51.2 1.9 %collective-permute-done.15.c_ref = bf16[8,128,128]{2,1,0:T(8,128)(2,1)S(1)} collective-permute-done((bf16[8,128,128]{2,1,0:T(8,128)(2,1)S(1)}, bf16[8,128,128]{2,1,0:T(8,128)(2,1)S(1)}, u32[]{:S(2)}, u32[]{:S(2)}) %collective-permute-start.15) | collective-permute-done | bytes 262176 | tf_op jit(solution)/shard_map/ppermute | solution.py:353
  53.1 1.6 %collective-permute-done.16.d_ref = bf16[8,128,128]{2,1,0:T(8,128)(2,1)S(1)} collective-permute-done((bf16[8,128,128]{2,1,0:T(8,128)(2,1)S(1)}, bf16[8,128,128]{2,1,0:T(8,128)(2,1)S(1)}, u32[]{:S(2)}, u32[]{:S(2)}) %collective-permute-start.16) | collective-permute-done | bytes 262176 | tf_op jit(solution)/shard_map/ppermute | solution.py:353
  54.9 0.8 shard_map.102
  55.7 7.6 %all-to-all-start.1 = ((bf16[8,256,128]{2,1,0:T(8,128)(2,1)}), bf16[8,256,128]{2,1,0:T(8,128)(2,1)S(1)}, u32[]{:S(2)}, u32[]{:S(2)}) async-start(bf16[8,256,128]{2,1,0:T(8,128)(2,1)} %get-tuple-element.80), calls=%async_computation.1 | async-start | bytes 1048576 | tf_op jit(solution)/shard_map/all_to_all | solution.py:432
  63.4 3.4 %collective-permute-start.9 = (bf16[256,512]{1,0:T(8,128)(2,1)S(1)}, bf16[256,512]{1,0:T(8,128)(2,1)S(1)}, u32[]{:S(2)}, u32[]{:S(2)}) collective-permute-start(bf16[256,512]{1,0:T(8,128)(2,1)S(1)} %get-tuple-element.59), channel_id=1, source_target_pairs={{0,2},{1,3},{2,0},{3,1},{4,6},{5,7},{6,4},{7,5},{8,10},{9,11},{10,... | collective-permute-start | bytes 786440 | tf_op jit(solution)/shard_map/ppermute | solution.py:353
  66.8 2.0 %collective-permute-start.17 = (bf16[2,32,512]{2,1,0:T(8,128)(2,1)S(1)}, bf16[2,32,512]{2,1,0:T(8,128)(2,1)S(1)}, u32[]{:S(2)}, u32[]{:S(2)}) collective-permute-start(bf16[2,32,512]{2,1,0:T(8,128)(2,1)S(1)} %get-tuple-element.79), channel_id=1, source_target_pairs={{0,8},{8,0},{16,24},{24,16},{32,40},{40,32},{48,56},{56,48},{1,9},... | collective-permute-start | bytes 196616 | tf_op jit(solution)/shard_map/ppermute | solution.py:353
  68.8 11.3 %all-to-all-done.1.a_ref.far_ref = bf16[8,256,128]{2,1,0:T(8,128)(2,1)S(1)} async-done(((bf16[8,256,128]{2,1,0:T(8,128)(2,1)}), bf16[8,256,128]{2,1,0:T(8,128)(2,1)S(1)}, u32[]{:S(2)}, u32[]{:S(2)}) %all-to-all-start.1) | async-done | bytes 524320 | tf_op jit(solution)/shard_map/all_to_all | solution.py:432
  80.1 0.7 shard_map.103._
  80.8 3.3 %all-to-all-start.2 = ((bf16[4,128,128]{2,1,0:T(8,128)(2,1)}), bf16[4,128,128]{2,1,0:T(8,128)(2,1)S(1)}, u32[]{:S(2)}, u32[]{:S(2)}) async-start(bf16[4,128,128]{2,1,0:T(8,128)(2,1)} %shard_map.103._), calls=%async_computation.2 | async-start | bytes 262144 | tf_op jit(solution)/shard_map/all_to_all | solution.py:437
  84.1 0.8 shard_map.98.__
  85.5 0.9 %copy-done.4 = bf16[256,512]{1,0:T(8,128)(2,1)S(1)} copy-done((bf16[256,512]{1,0:T(8,128)(2,1)S(1)}, bf16[256,512]{1,0:T(8,128)(2,1)}, u32[]{:S(2)}) %copy-start.4) | copy-done | bytes 262168
  86.4 1.2 %shard_map.104 = (bf16[256,512]{1,0:T(8,128)(2,1)}, bf16[256,512]{1,0:T(8,128)(2,1)}) custom-call(f32[2,256,512]{2,1,0:T(8,128)S(1)} %copy-done.6, f32[2,64,512]{2,1,0:T(8,128)S(1)} %copy-done.8, bf16[2,288,512]{2,1,0:T(8,128)(2,1)S(1)} %collective-permute-done.12.got_ref, bf16[2,32,512]{2,1,0:T(8,128)(2,1)S(1)} %collective-permute-done.17.near_ref, ...), custom_call_target="tpu_custom_call" | custom-call | flops 1000000000 | bytes 1 | tf_op jit(solution)/shard_map/pallas_call | solution.py:336
  87.6 2.4 %all-to-all-done.2 = bf16[4,128,128]{2,1,0:T(8,128)(2,1)S(1)} async-done(((bf16[4,128,128]{2,1,0:T(8,128)(2,1)}), bf16[4,128,128]{2,1,0:T(8,128)(2,1)S(1)}, u32[]{:S(2)}, u32[]{:S(2)}) %all-to-all-start.2) | async-done | bytes 131104 | tf_op jit(solution)/shard_map/all_to_all | solution.py:437
  90.0 0.7 bitcast_convert_fusion
  (42 shorter events, 3.3 us)
Async XLA Ops:
  0.6 21.3 %collective-permute-start.3 = (bf16[256,512]{1,0:T(8,128)(2,1)}, bf16[256,512]{1,0:T(8,128)(2,1)S(1)}, u32[]{:S(2)}, u32[]{:S(2)}) collective-permute-start(bf16[256,512]{1,0:T(8,128)(2,1)} %bitcast.11), channel_id=1, source_target_pairs={{0,1},{1,2},{2,3},{3,0},{4,5},{5,6},{6,7},{7,4},{8,9},{9,10},{10,1... | collective-permute-start | bytes 786440 | tf_op jit(solution)/shard_map/ppermute | solution.py:353
  2.3 19.8 %collective-permute-start.2 = (bf16[256,512]{1,0:T(8,128)(2,1)}, bf16[256,512]{1,0:T(8,128)(2,1)S(1)}, u32[]{:S(2)}, u32[]{:S(2)}) collective-permute-start(bf16[256,512]{1,0:T(8,128)(2,1)} %bitcast.12), channel_id=1, source_target_pairs={{0,2},{1,3},{2,0},{3,1},{4,6},{5,7},{6,4},{7,5},{8,10},{9,11},{10,... | collective-permute-start | bytes 786440 | tf_op jit(solution)/shard_map/ppermute | solution.py:353
  5.0 17.1 %collective-permute-start.1 = (bf16[256,512]{1,0:T(8,128)(2,1)}, bf16[256,512]{1,0:T(8,128)(2,1)S(1)}, u32[]{:S(2)}, u32[]{:S(2)}) collective-permute-start(bf16[256,512]{1,0:T(8,128)(2,1)} %bitcast.13), channel_id=1, source_target_pairs={{0,3},{1,0},{2,1},{3,2},{4,7},{5,4},{6,5},{7,6},{8,11},{9,8},{10,9... | collective-permute-start | bytes 786440 | tf_op jit(solution)/shard_map/ppermute | solution.py:353
  8.2 10.2 %collective-permute-start.6 = (bf16[2,32,512]{2,1,0:T(8,128)(2,1)}, bf16[2,32,512]{2,1,0:T(8,128)(2,1)S(1)}, u32[]{:S(2)}, u32[]{:S(2)}) collective-permute-start(bf16[2,32,512]{2,1,0:T(8,128)(2,1)} %get-tuple-element.48), channel_id=1, source_target_pairs={{0,8},{8,0},{16,24},{24,16},{32,40},{40,32},{48,56},{56,48},{1,9},... | collective-permute-start | bytes 196616 | tf_op jit(solution)/shard_map/ppermute | solution.py:353
  10.2 18.9 %all-to-all-start = ((bf16[8,2,16,512]{3,2,1,0:T(8,128)(2,1)}), bf16[8,2,16,512]{3,2,1,0:T(8,128)(2,1)S(1)}, u32[]{:S(2)}, u32[]{:S(2)}) async-start(bf16[8,2,16,512]{3,2,1,0:T(8,128)(2,1)} %get-tuple-element.45), calls=%async_computation | async-start | bytes 524288 | tf_op jit(solution)/shard_map/all_to_all | solution.py:378
  17.8 11.3 %collective-permute-start.4 = (bf16[2,128,512]{2,1,0:T(8,128)(2,1)}, bf16[2,128,512]{2,1,0:T(8,128)(2,1)S(1)}, u32[]{:S(2)}, u32[]{:S(2)}) collective-permute-start(bf16[2,128,512]{2,1,0:T(8,128)(2,1)} %get-tuple-element.46), channel_id=1, source_target_pairs={{4,8},{12,16},{20,24},{28,32},{36,40},{44,48},{52,56},{8,4},{16,12... | collective-permute-start | bytes 786440 | tf_op jit(solution)/shard_map/ppermute | solution.py:377
  18.5 10.6 %copy-start.1 = (bf16[3,256,512]{2,1,0:T(8,128)(2,1)S(1)}, bf16[3,256,512]{2,1,0:T(8,128)(2,1)}, u32[]{:S(2)}) copy-start(bf16[3,256,512]{2,1,0:T(8,128)(2,1)} %get-tuple-element.44.qkv_ref) | copy-start | bytes 2359300
  18.5 10.6 %copy-start.3 = (bf16[2,192,512]{2,1,0:T(8,128)(2,1)S(1)}, bf16[2,192,512]{2,1,0:T(8,128)(2,1)}, u32[]{:S(2)}) copy-start(bf16[2,192,512]{2,1,0:T(8,128)(2,1)} %get-tuple-element.47.chip_ref) | copy-start | bytes 1179652
  18.5 10.6 %collective-permute-start.5 = (bf16[2,192,512]{2,1,0:T(8,128)(2,1)}, bf16[2,192,512]{2,1,0:T(8,128)(2,1)S(1)}, u32[]{:S(2)}, u32[]{:S(2)}) collective-permute-start(bf16[2,192,512]{2,1,0:T(8,128)(2,1)} %get-tuple-element.47.chip_ref), channel_id=1, source_target_pairs={{0,4},{4,0},{1,5},{5,1},{2,6},{6,2},{3,7},{7,3},{8,12},{12,8},{9,1... | collective-permute-start | bytes 1179656 | tf_op jit(solution)/shard_map/ppermute | solution.py:353
  21.9 7.2 %collective-permute-start.7 = (bf16[2,32,512]{2,1,0:T(8,128)(2,1)S(1)}, bf16[2,32,512]{2,1,0:T(8,128)(2,1)S(1)}, u32[]{:S(2)}, u32[]{:S(2)}) collective-permute-start(bf16[2,32,512]{2,1,0:T(8,128)(2,1)S(1)} %collective-permute-done.6.near_ref), channel_id=1, source_target_pairs={{0,4},{4,0},{1,5},{5,1},{2,6},{6,2},{3,7},{7,3},{8,12},{12,8},{9,1... | collective-permute-start | bytes 196616 | tf_op jit(solution)/shard_map/ppermute | solution.py:353
  29.1 2.7 %collective-permute-start = (bf16[8,2,16,512]{3,2,1,0:T(8,128)(2,1)S(1)}, bf16[8,2,16,512]{3,2,1,0:T(8,128)(2,1)S(1)}, u32[]{:S(2)}, u32[]{:S(2)}) collective-permute-start(bf16[8,2,16,512]{3,2,1,0:T(8,128)(2,1)S(1)} %all-to-all-done.far_ref), channel_id=1, source_target_pairs={{0,4},{4,0},{1,5},{5,1},{2,6},{6,2},{3,7},{7,3},{8,12},{12,8},{9,1... | collective-permute-start | bytes 786440 | tf_op jit(solution)/shard_map/ppermute | solution.py:353
  31.8 2.5 %copy-start.2 = (bf16[1,256,512]{2,1,0:T(8,128)(2,1)S(1)}, bf16[1,256,512]{2,1,0:T(8,128)(2,1)}, u32[]{:S(2)}) copy-start(bf16[1,256,512]{2,1,0:T(8,128)(2,1)} %param.9) | copy-start | bytes 786436
  34.3 1.6 %copy-start = (bf16[512,2048]{1,0:T(8,128)(2,1)S(1)}, bf16[512,2048]{1,0:T(8,128)(2,1)}, u32[]{:S(2)}) copy-start(bf16[512,2048]{1,0:T(8,128)(2,1)} %w_hbm.1) | copy-start | bytes 6291460
  35.1 2.9 %collective-permute-start.11 = (bf16[4,8,128,128]{3,2,1,0:T(8,128)(2,1)S(1)}, bf16[4,8,128,128]{3,2,1,0:T(8,128)(2,1)S(1)}, u32[]{:S(2)}, u32[]{:S(2)}) collective-permute-start(bf16[4,8,128,128]{3,2,1,0:T(8,128)(2,1)S(1)} %get-tuple-element.61), channel_id=1, source_target_pairs={{0,4},{4,0},{1,5},{5,1},{2,6},{6,2},{3,7},{7,3},{8,12},{12,8},{9,1... | collective-permute-start | bytes 3145736 | tf_op jit(solution)/shard_map/ppermute | solution.py:353
  38.2 13.0 %collective-permute-start.14 = (bf16[8,128,128]{2,1,0:T(8,128)(2,1)S(1)}, bf16[8,128,128]{2,1,0:T(8,128)(2,1)S(1)}, u32[]{:S(2)}, u32[]{:S(2)}) collective-permute-start(bf16[8,128,128]{2,1,0:T(8,128)(2,1)S(1)} %get-tuple-element.75), channel_id=1, source_target_pairs={{0,64},{64,128},{128,192},{192,0},{1,65},{65,129},{129,193},{193,1... | collective-permute-start | bytes 786440 | tf_op jit(solution)/shard_map/ppermute | solution.py:353
  39.7 13.3 %collective-permute-start.15 = (bf16[8,128,128]{2,1,0:T(8,128)(2,1)S(1)}, bf16[8,128,128]{2,1,0:T(8,128)(2,1)S(1)}, u32[]{:S(2)}, u32[]{:S(2)}) collective-permute-start(bf16[8,128,128]{2,1,0:T(8,128)(2,1)S(1)} %get-tuple-element.76), channel_id=1, source_target_pairs={{0,192},{64,0},{128,64},{192,128},{1,193},{65,1},{129,65},{193,129... | collective-permute-start | bytes 786440 | tf_op jit(solution)/shard_map/ppermute | solution.py:353
  41.5 13.2 %collective-permute-start.16 = (bf16[8,128,128]{2,1,0:T(8,128)(2,1)S(1)}, bf16[8,128,128]{2,1,0:T(8,128)(2,1)S(1)}, u32[]{:S(2)}, u32[]{:S(2)}) collective-permute-start(bf16[8,128,128]{2,1,0:T(8,128)(2,1)S(1)} %get-tuple-element.77), channel_id=1, source_target_pairs={{0,128},{64,192},{128,0},{192,64},{1,129},{65,193},{129,1},{193,65... | collective-permute-start | bytes 786440 | tf_op jit(solution)/shard_map/ppermute | solution.py:353
  48.0 0.7 copy-start.7
  48.7 6.1 %copy-start.5 = (f32[2,256,512]{2,1,0:T(8,128)}, f32[2,256,512]{2,1,0:T(8,128)S(1)}, u32[]{:S(2)}) copy-start(f32[2,256,512]{2,1,0:T(8,128)S(1)} %get-tuple-element.71.mid_ref) | copy-start | bytes 3145732
  48.7 6.1 %collective-permute-start.13 = (bf16[2,128,512]{2,1,0:T(8,128)(2,1)S(1)}, bf16[2,128,512]{2,1,0:T(8,128)(2,1)S(1)}, u32[]{:S(2)}, u32[]{:S(2)}) collective-permute-start(bf16[2,128,512]{2,1,0:T(8,128)(2,1)S(1)} %get-tuple-element.74), channel_id=1, source_target_pairs={{4,8},{12,16},{20,24},{28,32},{36,40},{44,48},{52,56},{8,4},{16,12... | collective-permute-start | bytes 786440 | tf_op jit(solution)/shard_map/ppermute | solution.py:423
  49.4 5.5 %collective-permute-start.12 = (bf16[2,288,512]{2,1,0:T(8,128)(2,1)S(1)}, bf16[2,288,512]{2,1,0:T(8,128)(2,1)S(1)}, u32[]{:S(2)}, u32[]{:S(2)}) collective-permute-start(bf16[2,288,512]{2,1,0:T(8,128)(2,1)S(1)} %get-tuple-element.73), channel_id=1, source_target_pairs={{0,4},{4,0},{1,5},{5,1},{2,6},{6,2},{3,7},{7,3},{8,12},{12,8},{9,1... | collective-permute-start | bytes 1769480 | tf_op jit(solution)/shard_map/ppermute | solution.py:353
  55.7 24.3 %all-to-all-start.1 = ((bf16[8,256,128]{2,1,0:T(8,128)(2,1)}), bf16[8,256,128]{2,1,0:T(8,128)(2,1)S(1)}, u32[]{:S(2)}, u32[]{:S(2)}) async-start(bf16[8,256,128]{2,1,0:T(8,128)(2,1)} %get-tuple-element.80), calls=%async_computation.1 | async-start | bytes 1048576 | tf_op jit(solution)/shard_map/all_to_all | solution.py:432
  63.4 20.8 %collective-permute-start.8 = (bf16[256,512]{1,0:T(8,128)(2,1)S(1)}, bf16[256,512]{1,0:T(8,128)(2,1)S(1)}, u32[]{:S(2)}, u32[]{:S(2)}) collective-permute-start(bf16[256,512]{1,0:T(8,128)(2,1)S(1)} %get-tuple-element.58), channel_id=1, source_target_pairs={{0,1},{1,2},{2,3},{3,0},{4,5},{5,6},{6,7},{7,4},{8,9},{9,10},{10,1... | collective-permute-start | bytes 786440 | tf_op jit(solution)/shard_map/ppermute | solution.py:353
  63.4 20.8 %collective-permute-start.9 = (bf16[256,512]{1,0:T(8,128)(2,1)S(1)}, bf16[256,512]{1,0:T(8,128)(2,1)S(1)}, u32[]{:S(2)}, u32[]{:S(2)}) collective-permute-start(bf16[256,512]{1,0:T(8,128)(2,1)S(1)} %get-tuple-element.59), channel_id=1, source_target_pairs={{0,2},{1,3},{2,0},{3,1},{4,6},{5,7},{6,4},{7,5},{8,10},{9,11},{10,... | collective-permute-start | bytes 786440 | tf_op jit(solution)/shard_map/ppermute | solution.py:353
  66.8 17.4 %collective-permute-start.10 = (bf16[256,512]{1,0:T(8,128)(2,1)S(1)}, bf16[256,512]{1,0:T(8,128)(2,1)S(1)}, u32[]{:S(2)}, u32[]{:S(2)}) collective-permute-start(bf16[256,512]{1,0:T(8,128)(2,1)S(1)} %get-tuple-element.60), channel_id=1, source_target_pairs={{0,3},{1,0},{2,1},{3,2},{4,7},{5,4},{6,5},{7,6},{8,11},{9,8},{10,9... | collective-permute-start | bytes 786440 | tf_op jit(solution)/shard_map/ppermute | solution.py:353
  66.8 18.2 %collective-permute-start.17 = (bf16[2,32,512]{2,1,0:T(8,128)(2,1)S(1)}, bf16[2,32,512]{2,1,0:T(8,128)(2,1)S(1)}, u32[]{:S(2)}, u32[]{:S(2)}) collective-permute-start(bf16[2,32,512]{2,1,0:T(8,128)(2,1)S(1)} %get-tuple-element.79), channel_id=1, source_target_pairs={{0,8},{8,0},{16,24},{24,16},{32,40},{40,32},{48,56},{56,48},{1,9},... | collective-permute-start | bytes 196616 | tf_op jit(solution)/shard_map/ppermute | solution.py:353
  80.8 9.3 %all-to-all-start.2 = ((bf16[4,128,128]{2,1,0:T(8,128)(2,1)}), bf16[4,128,128]{2,1,0:T(8,128)(2,1)S(1)}, u32[]{:S(2)}, u32[]{:S(2)}) async-start(bf16[4,128,128]{2,1,0:T(8,128)(2,1)} %shard_map.103._), calls=%async_computation.2 | async-start | bytes 262144 | tf_op jit(solution)/shard_map/all_to_all | solution.py:437
  84.1 1.3 %copy-start.6 = (f32[2,256,512]{2,1,0:T(8,128)S(1)}, f32[2,256,512]{2,1,0:T(8,128)}, u32[]{:S(2)}) copy-start(f32[2,256,512]{2,1,0:T(8,128)} %copy-done.5) | copy-start | bytes 3145732
  84.1 1.4 %copy-start.8 = (f32[2,64,512]{2,1,0:T(8,128)S(1)}, f32[2,64,512]{2,1,0:T(8,128)}, u32[]{:S(2)}) copy-start(f32[2,64,512]{2,1,0:T(8,128)} %copy-done.7) | copy-start | bytes 786436
  85.5 0.9 %copy-start.4 = (bf16[256,512]{1,0:T(8,128)(2,1)S(1)}, bf16[256,512]{1,0:T(8,128)(2,1)}, u32[]{:S(2)}) copy-start(bf16[256,512]{1,0:T(8,128)(2,1)} %shard_map.98.__) | copy-start | bytes 786436

commit v4 on v3

--- a/solution.py
+++ b/solution.py
@@ -62,20 +62,18 @@
 TN = ((0,), (0,))
 
 
-def prep_kernel(
-    q_hbm, k_hbm, v_hbm, qkv_ref, chip_ref, near_ref, far_ref, edge_ref, sems
-):
+def prep_kernel(k_hbm, v_hbm, chip_ref, near_ref, far_ref, edge_ref, held, sems):
     z, c = lax.axis_index("z"), lax.axis_index("core")
     copies = [
-        pltpu.make_async_copy(src, qkv_ref.at[at], sems.at[at])
-        for at, src in ((1, k_hbm), (2, v_hbm), (0, q_hbm))
+        pltpu.make_async_copy(src, held.at[at], sems.at[at])
+        for at, src in ((0, k_hbm), (1, v_hbm))
     ]
     for copy in copies:
         copy.start()
     m = pool_matrix(128, ROWS)
     for part in range(2):
         copies[part].wait()
-        x = qkv_ref[1 + part]
+        x = held[part]
         pooled = dot(m, x, NN).astype(BF)
         chip_ref[part, 0:64] = pooled[0:64]
         near_ref[part] = pooled[64:96]
@@ -83,7 +81,6 @@
             far_ref[z ^ d, part] = pooled[112:128] if d >= 4 else pooled[96:112]
         chip_ref[part, 64:192] = jnp.where(c == 0, x[NR:], x[:NR])
         edge_ref[part] = jnp.where(c == 0, x[:NR], x[NR:])
-    copies[2].wait()
 
 
 def token_kernel(_, __, ___, out_ref):
@@ -91,7 +88,7 @@
 
 
 def near_kernel(
-    _, qkv_ref, edge_ref, chip_ref, sib_ref, near_ref, nearo_ref,
+    _, q_ref, k_ref, v_ref, edge_ref, chip_ref, sib_ref, near_ref, nearo_ref,
     keys_ref, vals_ref, exps_ref, part_ref, max_ref, sum_ref,
 ):
     z, c = lax.axis_index("z"), lax.axis_index("core")
@@ -99,10 +96,10 @@
     col = lax.broadcasted_iota(jnp.int32, (1, JOINT), 1)
     for h in range(HEADS):
         at_h = slice(h * DH, (h + 1) * DH)
-        for part, out in ((0, keys_ref), (1, vals_ref)):
+        for part, own_ref, out in ((0, k_ref, keys_ref), (1, v_ref, vals_ref)):
             beside, across = sib_ref[part, 64:192, at_h], edge_ref[part, :, at_h]
             out[h, 0:128] = jnp.where(c == 0, across, beside)
-            out[h, 128:384] = qkv_ref[1 + part, :, at_h]
+            out[h, 128:384] = own_ref[:, at_h]
             out[h, 384:448] = chip_ref[part, 0:64, at_h]
             out[h, 448:512] = sib_ref[part, 0:64, at_h]
             out[h, 512:544] = near_ref[part, :, at_h]
@@ -111,7 +108,7 @@
         for n in range(2):
             rows = slice(n * NR, (n + 1) * NR)
             span = slice(n * NR, n * NR + JOINT)
-            scores = dot(qkv_ref[0, rows, at_h], keys_ref[h, span], NT)
+            scores = dot(q_ref[rows, at_h], keys_ref[h, span], NT)
             if n == 0:
                 hidden = (col < NR) & (s == 0)
             else:
@@ -127,7 +124,7 @@
 
 
 def far_kernel(
-    qkv_ref, far_ref, faro_ref, keys_ref, vals_ref, part_ref, max_ref, sum_ref,
+    q_ref, far_ref, faro_ref, keys_ref, vals_ref, part_ref, max_ref, sum_ref,
     att_ref, attt_ref, exps_ref, fkeys_ref, fvals_ref, rnear_ref, rfar_ref,
 ):
     z = lax.axis_index("z")
@@ -145,7 +142,7 @@
                 out[h, at : at + 16] = jnp.concatenate([low[0:8], high[0:8]], axis=0)
             top = dot(by_near, near[h, 384:576], NN) + dot(by_far, out[h, 0:128], NN)
             out[h, 128:192] = top.astype(BF)
-        scores = dot(qkv_ref[0, :, at_h], fkeys_ref[h], NT)
+        scores = dot(q_ref[:, at_h], fkeys_ref[h], NT)
         first = max_ref[h]
         highest = jnp.maximum(first, jnp.max(scores, axis=1, keepdims=True))
         e = jnp.exp2((scores - highest) * (SCALE * LOG2E))
@@ -205,7 +202,7 @@
 
 
 def bwd_kernel(
-    _, qkv_ref, da_ref, att_ref, exps_ref, fexps_ref, keys_ref, vals_ref, fkeys_ref, fvals_ref,
+    _, q_ref, da_ref, att_ref, exps_ref, fexps_ref, keys_ref, vals_ref, fkeys_ref, fvals_ref,
     rnear_ref, rfar_ref,
     dq_ref, mid_ref, edge_ref, own_ref, cross_ref, minec_ref, gk_ref, gv_ref,
 ):
@@ -213,7 +210,7 @@
     by_near, by_far = top_near(), top_far()
     for h in range(HEADS):
         at_h = slice(h * DH, (h + 1) * DH)
-        q, da = qkv_ref[0, :, at_h], da_ref[:, at_h]
+        q, da = q_ref[:, at_h], da_ref[:, at_h]
         att = att_ref[:, at_h].astype(F32)
         delta = jnp.sum(da.astype(F32) * att, axis=1, keepdims=True)
         p = fexps_ref[h].astype(F32) * rfar_ref[h]
@@ -291,17 +288,27 @@
     out_ref[...] = total.astype(BF)
 
 
+def mixed_kernel(a_ref, b_ref, c_ref, d_ref, out_ref, token_ref):
+    sum_kernel(a_ref, b_ref, c_ref, d_ref, out_ref)
+    token_ref[...] = jnp.zeros_like(token_ref)
+
+
 def sum8_kernel(a_ref, out_ref):
     total = a_ref[0, 0:128].astype(F32)
     for j in range(1, 8):
         total = total + a_ref[j, 0:128].astype(F32)
-    for i in range(4):
-        out_ref[i] = total.astype(BF)
+    out_ref[...] = total.astype(BF)
+
+
+def collect_kernel(_, __, a_ref, b_ref, c_ref, d_ref, out_ref):
+    me = lax.axis_index("dp")
+    for shift, ref in ((0, a_ref), (1, b_ref), (2, c_ref), (3, d_ref)):
+        out_ref[(me + shift) & 3] = ref[...].astype(F32)
 
 
 def final_kernel(
-    mid_ref, own_ref, got_ref, near_ref, far_ref, edge_ref, _, __,
-    gk_ref, gv_ref,
+    mid_ref, own_ref, got_ref, near_ref, far_ref, edge_ref, _,
+    gk_ref, gv_ref, token_ref,
 ):
     z, c = lax.axis_index("z"), lax.axis_index("core")
     m = pool_matrix(128, ROWS, flip=True)
@@ -321,10 +328,14 @@
         beside, across = got_ref[part, 160:288].astype(F32), edge_ref[part].astype(F32)
         out[0:128] = (total[0:128] + jnp.where(c == 0, across, beside)).astype(BF)
         out[128:256] = (total[128:256] + jnp.where(c == 0, beside, across)).astype(BF)
+    token_ref[...] = jnp.zeros_like(token_ref)
 
 
 def sds(shape, dtype):
     return jax.ShapeDtypeStruct(shape, dtype)
+
+
+TOKEN = sds((8, 128), F32)
 
 
 HBM = pl.BlockSpec(memory_space=pltpu.HBM)
@@ -365,11 +376,11 @@
 
     og = out_grad.reshape(ROWS, WIDTH)
 
-    qkv, chip, near, far, edge = call(
-        prep_kernel, [(HBM, q), (HBM, k), (HBM, v)],
-        [sds((3, ROWS, WIDTH), BF), sds((2, 192, WIDTH), BF), sds((2, 32, WIDTH), BF),
-         sds((8, 2, 16, WIDTH), BF), sds((2, NR, WIDTH), BF)],
-        [dma((3,))], limit=62 * 1024 * 1024,
+    chip, near, far, edge = call(
+        prep_kernel, [(HBM, k), (HBM, v)],
+        [sds((2, 192, WIDTH), BF), sds((2, 32, WIDTH), BF), sds((8, 2, 16, WIDTH), BF),
+         sds((2, NR, WIDTH), BF)],
+        [pltpu.VMEM((2, ROWS, WIDTH), BF), dma((2,))], limit=62 * 1024 * 1024,
     )
     sib = swap(chip)
     near_got = hop(near)
@@ -383,13 +394,13 @@
 
     column = sds((HEADS, ROWS, 1), F32)
     keys_near, vals_near, exps, part, top, total = call(
-        near_kernel, [(AFTER, token)] + here(qkv, edge_got, chip, sib, near_got, near_other),
+        near_kernel, [(AFTER, token)] + here(q, k, v, edge_got, chip, sib, near_got, near_other),
         [sds((HEADS, NEAR, DH), BF), sds((HEADS, NEAR, DH), BF), sds((HEADS, 2, NR, JOINT), BF),
          sds((ROWS, WIDTH), F32), column, column],
         us=20,
     )
     att, attt, far_exps, keys_far, vals_far, rnear, rfar = call(
-        far_kernel, here(qkv, far_got, far_other, keys_near, vals_near, part, top, total),
+        far_kernel, here(q, far_got, far_other, keys_near, vals_near, part, top, total),
         [sds((ROWS, WIDTH), BF), sds((WIDTH, ROWS), BF), sds((HEADS, ROWS, FAR), BF),
          sds((HEADS, FAR, DH), BF), sds((HEADS, FAR, DH), BF), column, column],
     )
@@ -400,19 +411,19 @@
         [sds((ROWS, WIDTH), BF)] * 5, [pltpu.VMEM((4, WIDTH, 512), BF), dma((4,))],
     )
     mix_parts = [mixes[0]]
-    mix_parts += [permute(mixes[m], "head", lambda i, m=m: i + m) for m in (1, 2, 3)]
+    mix_parts += [permute(mixes[m], "head", lambda i, m=m: i + m) for m in (2, 1, 3)]
 
     kept, to_up, to_down, to_across = call(
         route_kernel, here(mine, got), [sds((8, 128, 128), BF)] * 4
     )
+    from_across = permute(to_across, "dp", lambda i: i + 2)
     from_down = permute(to_up, "dp", lambda i: i + 1)
     from_up = permute(to_down, "dp", lambda i: i - 1)
-    from_across = permute(to_across, "dp", lambda i: i + 2)
 
     dq, mid, edge_grad, own_grad, cross, minec = call(
         bwd_kernel,
         [(AFTER, kept)]
-        + here(qkv, gatt, att, exps, far_exps, keys_near, vals_near, keys_far, vals_far)
+        + here(q, gatt, att, exps, far_exps, keys_near, vals_near, keys_far, vals_far)
         + here(rnear, rfar),
         [sds((ROWS, WIDTH), BF), sds((2, ROWS, WIDTH), F32), sds((2, NR, WIDTH), BF),
          sds((2, 64, WIDTH), F32), sds((2, 288, WIDTH), BF),
@@ -422,7 +433,7 @@
     cross_got = swap(cross)
     edge_back = outer(edge_grad)
     (wsum,) = call(
-        sum_kernel, here(kept, from_down, from_up, from_across), [sds((8, 128, 128), BF)], us=8
+        sum_kernel, here(kept, from_across, from_down, from_up), [sds((8, 128, 128), BF)], us=8
     )
     near_grad, both = call(
         merge_kernel, [(AFTER, edge_back)] + here(wsum, minec, cross_got),
@@ -430,19 +441,25 @@
     )
     near_back = hop(near_grad)
     both_got = lax.all_to_all(both, "z", 0, 0)
-    (mixed,) = call(sum_kernel, here(*mix_parts), [sds((ROWS, WIDTH), BF)])
     (wpart,) = call(
-        sum8_kernel, here(both_got), [sds((4, 128, 128), BF)], us=20
-    )
-    wall = lax.all_to_all(wpart, "dp", 0, 0)
-    grad_out_weight = wall.reshape(WIDTH, 128).astype(F32)
-
-    grad_keys, grad_values = call(
+        sum8_kernel, here(both_got), [sds((128, 128), BF)], us=20
+    )
+    mixed, token_mixed = call(
+        mixed_kernel, here(*mix_parts), [sds((ROWS, WIDTH), BF), TOKEN],
+    )
+    wparts = [wpart] + [permute(wpart, "dp", lambda i, m=m: i - m) for m in (1, 2, 3)]
+
+    grad_keys, grad_values, token_keys = call(
         final_kernel,
         here(mid, own_grad, cross_got, near_back, both_got, edge_back)
-        + [(AFTER, wpart), (AFTER, mixed)],
-        [sds((ROWS, WIDTH), BF)] * 2,
-    )
+        + [(AFTER, wpart)],
+        [sds((ROWS, WIDTH), BF)] * 2 + [TOKEN],
+    )
+    (wall,) = call(
+        collect_kernel, [(AFTER, token_mixed), (AFTER, token_keys)] + here(*wparts),
+        [sds((4, 128, 128), F32)],
+    )
+    grad_out_weight = wall.reshape(WIDTH, 128)
     shape = (1, ROWS, WIDTH)
     return (
         mixed.reshape(shape), dq.reshape(shape), grad_keys.reshape(shape),

time: 91.3 us -> 88.2 us (0.966); the launches traced: 90.8 us -> 86.7 us
  waiting for transfers between devices: 24.4 us -> 22.1 us
  local copies, waits for them, and re-layouts: 2.41 us -> 0.29 us
  starting transfers between devices: 43.4 us -> 44.8 us
    ppermute x16 -> x19, waiting for transfers between devices: 3.64 us -> 15 us  [permute(): return lax.ppermute(x, axis, [(i, move(i) % size) for i in range(size)])]
    all_to_all x1, waiting for transfers between devices: 11.3 us -> 0.03 us  [body(): both_got = lax.all_to_all(both, 'z', 0, 0)]
    ppermute x16 -> x19, starting transfers between devices: 23.5 us -> 27.2 us  [permute(): return lax.ppermute(x, axis, [(i, move(i) % size) for i in range(size)])]
    all_to_all x1 -> x0, starting transfers between devices: 3.32 us -> none  [body(): wall = lax.all_to_all(wpart, 'dp', 0, 0)]
    all_to_all x1 -> x0, waiting for transfers between devices: 2.43 us -> none  [body(): wall = lax.all_to_all(wpart, 'dp', 0, 0)]
    unnamed x18 -> x16, local copies, waits for them, and re-layouts: 2.41 us -> 0.29 us
    all_to_all x1, starting transfers between devices: 7.64 us -> 8.71 us  [body(): both_got = lax.all_to_all(both, 'z', 0, 0)]
    pallas_call x13 -> x14, Pallas kernels: 19 us -> 18.7 us  [call(): pl.pallas_call(kernel, out_shape=outs, in_specs=[spec for spec, _ in oper...]
  transfers between devices with their start and end apart: 21 -> 23, of which waited for: 6 -> 10; matrix products, arithmetic and copies ran while one was open for 0% -> 0% of each run, Pallas kernels for 16% -> 16%
where the time goes in v4:
time: 88.2 us; the launch traced here: 86.7 us
  starting transfers between devices  44.8 us (51%)
  waiting for transfers between devices  22.1 us (25%)
  Pallas kernels  18.7 us (21%)
    ppermute x19, starting transfers between devices, permute(): return lax.ppermute(x, axis, [(i, move(i) % size) for i in range(size)])  27.2 us
    pallas_call x14, Pallas kernels, call(): pl.pallas_call(kernel, out_shape=outs, in_specs=[spec for spec, _ in oper...  18.7 us
    ppermute x19, waiting for transfers between devices, permute(): return lax.ppermute(x, axis, [(i, move(i) % size) for i in range(size)])  15 us
    all_to_all x1, starting transfers between devices, body(): both_got = lax.all_to_all(both, 'z', 0, 0)  8.71 us
    all_to_all x1, starting transfers between devices, body(): far_got = lax.all_to_all(far, 'z', 0, 0)  7.57 us
    all_to_all x1, waiting for transfers between devices, body(): far_got = lax.all_to_all(far, 'z', 0, 0)  7 us
  transfers between devices with their start and end apart: 23, of which 10 were waited for; matrix products, arithmetic and copies ran while one was open for 0% of the time, Pallas kernels for 16%

profile of v4, /device:TPU:8, one launch (start us, length us, event | category | flops | bytes accessed | tf_op | source)
XLA Modules:
  0.0 86.7 jit_solution(4833492554735853060)
XLA Ops:
  0.6 1.7 %collective-permute-start.3 = (bf16[256,512]{1,0:T(8,128)(2,1)}, bf16[256,512]{1,0:T(8,128)(2,1)S(1)}, u32[]{:S(2)}, u32[]{:S(2)}) collective-permute-start(bf16[256,512]{1,0:T(8,128)(2,1)} %bitcast.9), channel_id=1, source_target_pairs={{0,1},{1,2},{2,3},{3,0},{4,5},{5,6},{6,7},{7,4},{8,9},{9,10},{10,1... | collective-permute-start | bytes 786440 | tf_op jit(solution)/shard_map/ppermute | solution.py:364
  2.3 2.7 %collective-permute-start.2 = (bf16[256,512]{1,0:T(8,128)(2,1)}, bf16[256,512]{1,0:T(8,128)(2,1)S(1)}, u32[]{:S(2)}, u32[]{:S(2)}) collective-permute-start(bf16[256,512]{1,0:T(8,128)(2,1)} %bitcast.10), channel_id=1, source_target_pairs={{0,2},{1,3},{2,0},{3,1},{4,6},{5,7},{6,4},{7,5},{8,10},{9,11},{10,... | collective-permute-start | bytes 786440 | tf_op jit(solution)/shard_map/ppermute | solution.py:364
  5.0 0.7 collective-permute-start.1
  5.6 2.2 %shard_map.92 = (bf16[2,192,512]{2,1,0:T(8,128)(2,1)}, bf16[2,32,512]{2,1,0:T(8,128)(2,1)}, bf16[8,2,16,512]{3,2,1,0:T(8,128)(2,1)}, bf16[2,128,512]{2,1,0:T(8,128)(2,1)}) custom-call(bf16[256,512]{1,0:T(8,128)(2,1)} %bitcast.17, bf16[256,512]{1,0:T(8,128)(2,1)} %bitcast.19), custom_call_target="tpu_custom_call" | custom-call | flops 1000000000 | bytes 1 | tf_op jit(solution)/shard_map/pallas_call | solution.py:347
  7.8 2.0 %collective-permute-start.6 = (bf16[2,32,512]{2,1,0:T(8,128)(2,1)}, bf16[2,32,512]{2,1,0:T(8,128)(2,1)S(1)}, u32[]{:S(2)}, u32[]{:S(2)}) collective-permute-start(bf16[2,32,512]{2,1,0:T(8,128)(2,1)} %get-tuple-element.49), channel_id=1, source_target_pairs={{0,8},{8,0},{16,24},{24,16},{32,40},{40,32},{48,56},{56,48},{1,9},... | collective-permute-start | bytes 196616 | tf_op jit(solution)/shard_map/ppermute | solution.py:364
  9.8 7.6 %all-to-all-start = ((bf16[8,2,16,512]{3,2,1,0:T(8,128)(2,1)}), bf16[8,2,16,512]{3,2,1,0:T(8,128)(2,1)S(1)}, u32[]{:S(2)}, u32[]{:S(2)}) async-start(bf16[8,2,16,512]{3,2,1,0:T(8,128)(2,1)} %get-tuple-element.46), calls=%async_computation | async-start | bytes 524288 | tf_op jit(solution)/shard_map/all_to_all | solution.py:389
  17.4 0.7 collective-permute-start.4
  18.1 3.5 %collective-permute-start.5 = (bf16[2,192,512]{2,1,0:T(8,128)(2,1)}, bf16[2,192,512]{2,1,0:T(8,128)(2,1)S(1)}, u32[]{:S(2)}, u32[]{:S(2)}) collective-permute-start(bf16[2,192,512]{2,1,0:T(8,128)(2,1)} %get-tuple-element.48.chip_ref), channel_id=1, source_target_pairs={{0,4},{4,0},{1,5},{5,1},{2,6},{6,2},{3,7},{7,3},{8,12},{12,8},{9,1... | collective-permute-start | bytes 1179656 | tf_op jit(solution)/shard_map/ppermute | solution.py:364
  21.7 7.0 %all-to-all-done.far_ref = bf16[8,2,16,512]{3,2,1,0:T(8,128)(2,1)S(1)} async-done(((bf16[8,2,16,512]{3,2,1,0:T(8,128)(2,1)}), bf16[8,2,16,512]{3,2,1,0:T(8,128)(2,1)S(1)}, u32[]{:S(2)}, u32[]{:S(2)}) %all-to-all-start) | async-done | bytes 262176 | tf_op jit(solution)/shard_map/all_to_all | solution.py:389
  28.8 2.6 %shard_map.94 = (bf16[4,704,128]{2,1,0:T(8,128)(2,1)S(1)}, bf16[4,704,128]{2,1,0:T(8,128)(2,1)S(1)}, bf16[4,2,128,576]{3,2,1,0:T(8,128)(2,1)S(1)}, f32[256,512]{...) custom-call(f32[8,128]{1,0:T(8,128)S(1)} %shard_map.93._, bf16[256,512]{1,0:T(8,128)(2,1)S(1)} %bitcast.14, ...), custom_call_target="tpu_custom_call" | custom-call | flops 20000000000 | bytes 1 | tf_op jit(solution)/shard_map/pallas_call | solution.py:347
  31.4 2.5 %shard_map.95 = (bf16[256,512]{1,0:T(8,128)(2,1)S(1)}, bf16[512,256]{1,0:T(8,128)(2,1)S(1)}, bf16[4,256,192]{2,1,0:T(8,128)(2,1)S(1)}, bf16[4,192,128]{2,1,0:T(8...) custom-call(bf16[256,512]{1,0:T(8,128)(2,1)S(1)} %bitcast.15, ...), custom_call_target="tpu_custom_call" | custom-call | flops 1000000000 | bytes 1 | tf_op jit(solution)/shard_map/pallas_call | solution.py:347
  34.0 0.7 shard_map.96
  35.6 1.9 %shard_map.97 = (bf16[256,512]{1,0:T(8,128)(2,1)S(1)}, bf16[256,512]{1,0:T(8,128)(2,1)S(1)}, bf16[256,512]{1,0:T(8,128)(2,1)S(1)}, bf16[256,512]{1,0:T(8,128)(2,1)S(1)}, bf16[256,512]{1,0:T(8,128)(2,1)S(1)}) custom-call(bf16[4,8,128,128]{3,2,1,0:T(8,128)(2,1)S(1)} %get-tuple-element.56._.mine_ref, bf16[256,512]{1,0:T(8,128)(2,1)S(1)} %get-tuple-element.57.att_ref, ...), custom_call_target="tpu_custom_call" | custom-call | flops 1000000000 | bytes 1 | tf_op jit(solution)/shard_map/pallas_call | solution.py:347
  37.8 3.1 %collective-permute-start.14 = (bf16[8,128,128]{2,1,0:T(8,128)(2,1)S(1)}, bf16[8,128,128]{2,1,0:T(8,128)(2,1)S(1)}, u32[]{:S(2)}, u32[]{:S(2)}) collective-permute-start(bf16[8,128,128]{2,1,0:T(8,128)(2,1)S(1)} %get-tuple-element.77), channel_id=1, source_target_pairs={{0,128},{64,192},{128,0},{192,64},{1,129},{65,193},{129,1},{193,65... | collective-permute-start | bytes 786440 | tf_op jit(solution)/shard_map/ppermute | solution.py:364
  41.5 2.6 %collective-permute-start.16 = (bf16[8,128,128]{2,1,0:T(8,128)(2,1)S(1)}, bf16[8,128,128]{2,1,0:T(8,128)(2,1)S(1)}, u32[]{:S(2)}, u32[]{:S(2)}) collective-permute-start(bf16[8,128,128]{2,1,0:T(8,128)(2,1)S(1)} %get-tuple-element.79), channel_id=1, source_target_pairs={{0,192},{64,0},{128,64},{192,128},{1,193},{65,1},{129,65},{193,129... | collective-permute-start | bytes 786440 | tf_op jit(solution)/shard_map/ppermute | solution.py:364
  44.2 4.7 %shard_map.100 = (bf16[256,512]{1,0:T(8,128)(2,1)}, f32[2,256,512]{2,1,0:T(8,128)S(1)}, bf16[2,128,512]{2,1,0:T(8,128)(2,1)S(1)}, f32[2,64,512]{2,1,0:T(8,128)S(...) custom-call(bf16[8,128,128]{2,1,0:T(8,128)(2,1)S(1)} %get-tuple-element.64._.a_ref, ...), custom_call_target="tpu_custom_call" | custom-call | flops 20000000000 | bytes 1 | tf_op jit(solution)/shard_map/pallas_call | solution.py:347
  49.6 1.8 %collective-permute-start.12 = (bf16[2,288,512]{2,1,0:T(8,128)(2,1)S(1)}, bf16[2,288,512]{2,1,0:T(8,128)(2,1)S(1)}, u32[]{:S(2)}, u32[]{:S(2)}) collective-permute-start(bf16[2,288,512]{2,1,0:T(8,128)(2,1)S(1)} %get-tuple-element.75), channel_id=1, source_target_pairs={{0,4},{4,0},{1,5},{5,1},{2,6},{6,2},{3,7},{7,3},{8,12},{12,8},{9,1... | collective-permute-start | bytes 1769480 | tf_op jit(solution)/shard_map/ppermute | solution.py:364
  51.4 2.3 %collective-permute-done.15.c_ref = bf16[8,128,128]{2,1,0:T(8,128)(2,1)S(1)} collective-permute-done((bf16[8,128,128]{2,1,0:T(8,128)(2,1)S(1)}, bf16[8,128,128]{2,1,0:T(8,128)(2,1)S(1)}, u32[]{:S(2)}, u32[]{:S(2)}) %collective-permute-start.15) | collective-permute-done | bytes 262176 | tf_op jit(solution)/shard_map/ppermute | solution.py:364
  54.0 0.9 shard_map.102
  54.8 8.7 %all-to-all-start.1 = ((bf16[8,256,128]{2,1,0:T(8,128)(2,1)}), bf16[8,256,128]{2,1,0:T(8,128)(2,1)S(1)}, u32[]{:S(2)}, u32[]{:S(2)}) async-start(bf16[8,256,128]{2,1,0:T(8,128)(2,1)} %get-tuple-element.82), calls=%async_computation.1 | async-start | bytes 1048576 | tf_op jit(solution)/shard_map/all_to_all | solution.py:443
  63.7 2.6 %collective-permute-start.9 = (bf16[256,512]{1,0:T(8,128)(2,1)S(1)}, bf16[256,512]{1,0:T(8,128)(2,1)S(1)}, u32[]{:S(2)}, u32[]{:S(2)}) collective-permute-start(bf16[256,512]{1,0:T(8,128)(2,1)S(1)} %get-tuple-element.60), channel_id=1, source_target_pairs={{0,1},{1,2},{2,3},{3,0},{4,5},{5,6},{6,7},{7,4},{8,9},{9,10},{10,1... | collective-permute-start | bytes 786440 | tf_op jit(solution)/shard_map/ppermute | solution.py:364
  66.4 7.8 %collective-permute-done.8.b_ref = bf16[256,512]{1,0:T(8,128)(2,1)S(1)} collective-permute-done((bf16[256,512]{1,0:T(8,128)(2,1)S(1)}, bf16[256,512]{1,0:T(8,128)(2,1)S(1)}, u32[]{:S(2)}, u32[]{:S(2)}) %collective-permute-start.8) | collective-permute-done | bytes 262176 | tf_op jit(solution)/shard_map/ppermute | solution.py:364
  74.2 0.9 %collective-permute-done.9.c_ref = bf16[256,512]{1,0:T(8,128)(2,1)S(1)} collective-permute-done((bf16[256,512]{1,0:T(8,128)(2,1)S(1)}, bf16[256,512]{1,0:T(8,128)(2,1)S(1)}, u32[]{:S(2)}, u32[]{:S(2)}) %collective-permute-start.9) | collective-permute-done | bytes 262176 | tf_op jit(solution)/shard_map/ppermute | solution.py:364
  75.1 1.8 %collective-permute-done.10.d_ref = bf16[256,512]{1,0:T(8,128)(2,1)S(1)} collective-permute-done((bf16[256,512]{1,0:T(8,128)(2,1)S(1)}, bf16[256,512]{1,0:T(8,128)(2,1)S(1)}, u32[]{:S(2)}, u32[]{:S(2)}) %collective-permute-start.10) | collective-permute-done | bytes 262176 | tf_op jit(solution)/shard_map/ppermute | solution.py:364
  77.0 0.8 shard_map.98
  77.8 1.7 %collective-permute-start.17 = (bf16[2,32,512]{2,1,0:T(8,128)(2,1)S(1)}, bf16[2,32,512]{2,1,0:T(8,128)(2,1)S(1)}, u32[]{:S(2)}, u32[]{:S(2)}) collective-permute-start(bf16[2,32,512]{2,1,0:T(8,128)(2,1)S(1)} %get-tuple-element.81), channel_id=1, source_target_pairs={{0,8},{8,0},{16,24},{24,16},{32,40},{40,32},{48,56},{56,48},{1,9},... | collective-permute-start | bytes 196616 | tf_op jit(solution)/shard_map/ppermute | solution.py:364
  79.7 1.7 %collective-permute-start.19 = (bf16[128,128]{1,0:T(8,128)(2,1)S(1)}, bf16[128,128]{1,0:T(8,128)(2,1)S(1)}, u32[]{:S(2)}, u32[]{:S(2)}) collective-permute-start(bf16[128,128]{1,0:T(8,128)(2,1)S(1)} %shard_map.103._.a_ref), channel_id=1, source_target_pairs={{0,128},{64,192},{128,0},{192,64},{1,129},{65,193},{129,1},{193,65... | collective-permute-start | bytes 98312 | tf_op jit(solution)/shard_map/ppermute | solution.py:364
  81.4 1.5 %collective-permute-start.18 = (bf16[128,128]{1,0:T(8,128)(2,1)S(1)}, bf16[128,128]{1,0:T(8,128)(2,1)S(1)}, u32[]{:S(2)}, u32[]{:S(2)}) collective-permute-start(bf16[128,128]{1,0:T(8,128)(2,1)S(1)} %shard_map.103._.a_ref), channel_id=1, source_target_pairs={{0,192},{64,0},{128,64},{192,128},{1,193},{65,1},{129,65},{193,129... | collective-permute-start | bytes 98312 | tf_op jit(solution)/shard_map/ppermute | solution.py:364
  82.9 1.2 %shard_map.104 = (bf16[256,512]{1,0:T(8,128)(2,1)}, bf16[256,512]{1,0:T(8,128)(2,1)}, f32[8,128]{1,0:T(8,128)S(1)}) custom-call(f32[2,256,512]{2,1,0:T(8,128)S(1)} %copy-done.7, f32[2,64,512]{2,1,0:T(8,128)S(1)} %get-tuple-element.74.own_ref, bf16[2,288,512]{2,1,0:T(8,128)(2,1)S(1)} %collective-permute-done.12.got_ref, ...), custom_call_target="tpu_custom_call" | custom-call | flops 1000000000 | bytes 1 | tf_op jit(solution)/shard_map/pallas_call | solution.py:347
  84.1 0.7 collective-permute-done.20.d_ref
  85.2 0.8 collective-permute-done.18.b_ref
  86.0 0.7 shard_map.105
  (44 shorter events, 3.6 us)
Async XLA Ops:
  0.6 21.0 %collective-permute-start.3 = (bf16[256,512]{1,0:T(8,128)(2,1)}, bf16[256,512]{1,0:T(8,128)(2,1)S(1)}, u32[]{:S(2)}, u32[]{:S(2)}) collective-permute-start(bf16[256,512]{1,0:T(8,128)(2,1)} %bitcast.9), channel_id=1, source_target_pairs={{0,1},{1,2},{2,3},{3,0},{4,5},{5,6},{6,7},{7,4},{8,9},{9,10},{10,1... | collective-permute-start | bytes 786440 | tf_op jit(solution)/shard_map/ppermute | solution.py:364
  2.3 19.4 %collective-permute-start.2 = (bf16[256,512]{1,0:T(8,128)(2,1)}, bf16[256,512]{1,0:T(8,128)(2,1)S(1)}, u32[]{:S(2)}, u32[]{:S(2)}) collective-permute-start(bf16[256,512]{1,0:T(8,128)(2,1)} %bitcast.10), channel_id=1, source_target_pairs={{0,2},{1,3},{2,0},{3,1},{4,6},{5,7},{6,4},{7,5},{8,10},{9,11},{10,... | collective-permute-start | bytes 786440 | tf_op jit(solution)/shard_map/ppermute | solution.py:364
  5.0 16.8 %collective-permute-start.1 = (bf16[256,512]{1,0:T(8,128)(2,1)}, bf16[256,512]{1,0:T(8,128)(2,1)S(1)}, u32[]{:S(2)}, u32[]{:S(2)}) collective-permute-start(bf16[256,512]{1,0:T(8,128)(2,1)} %bitcast.11), channel_id=1, source_target_pairs={{0,3},{1,0},{2,1},{3,2},{4,7},{5,4},{6,5},{7,6},{8,11},{9,8},{10,9... | collective-permute-start | bytes 786440 | tf_op jit(solution)/shard_map/ppermute | solution.py:364
  7.8 10.2 %collective-permute-start.6 = (bf16[2,32,512]{2,1,0:T(8,128)(2,1)}, bf16[2,32,512]{2,1,0:T(8,128)(2,1)S(1)}, u32[]{:S(2)}, u32[]{:S(2)}) collective-permute-start(bf16[2,32,512]{2,1,0:T(8,128)(2,1)} %get-tuple-element.49), channel_id=1, source_target_pairs={{0,8},{8,0},{16,24},{24,16},{32,40},{40,32},{48,56},{56,48},{1,9},... | collective-permute-start | bytes 196616 | tf_op jit(solution)/shard_map/ppermute | solution.py:364
  9.8 18.9 %all-to-all-start = ((bf16[8,2,16,512]{3,2,1,0:T(8,128)(2,1)}), bf16[8,2,16,512]{3,2,1,0:T(8,128)(2,1)S(1)}, u32[]{:S(2)}, u32[]{:S(2)}) async-start(bf16[8,2,16,512]{3,2,1,0:T(8,128)(2,1)} %get-tuple-element.46), calls=%async_computation | async-start | bytes 524288 | tf_op jit(solution)/shard_map/all_to_all | solution.py:389
  17.4 11.3 %collective-permute-start.4 = (bf16[2,128,512]{2,1,0:T(8,128)(2,1)}, bf16[2,128,512]{2,1,0:T(8,128)(2,1)S(1)}, u32[]{:S(2)}, u32[]{:S(2)}) collective-permute-start(bf16[2,128,512]{2,1,0:T(8,128)(2,1)} %get-tuple-element.47), channel_id=1, source_target_pairs={{4,8},{12,16},{20,24},{28,32},{36,40},{44,48},{52,56},{8,4},{16,12... | collective-permute-start | bytes 786440 | tf_op jit(solution)/shard_map/ppermute | solution.py:388
  18.1 10.6 %copy-start.2 = (bf16[1,256,512]{2,1,0:T(8,128)(2,1)S(1)}, bf16[1,256,512]{2,1,0:T(8,128)(2,1)}, u32[]{:S(2)}) copy-start(bf16[1,256,512]{2,1,0:T(8,128)(2,1)} %param.5) | copy-start | bytes 786436
  18.1 10.6 %copy-start.3 = (bf16[2,192,512]{2,1,0:T(8,128)(2,1)S(1)}, bf16[2,192,512]{2,1,0:T(8,128)(2,1)}, u32[]{:S(2)}) copy-start(bf16[2,192,512]{2,1,0:T(8,128)(2,1)} %get-tuple-element.48.chip_ref) | copy-start | bytes 1179652
  18.1 10.6 %copy-start.4 = (bf16[1,256,512]{2,1,0:T(8,128)(2,1)S(1)}, bf16[1,256,512]{2,1,0:T(8,128)(2,1)}, u32[]{:S(2)}) copy-start(bf16[1,256,512]{2,1,0:T(8,128)(2,1)} %param.6) | copy-start | bytes 786436
  18.1 10.6 %copy-start.5 = (bf16[1,256,512]{2,1,0:T(8,128)(2,1)S(1)}, bf16[1,256,512]{2,1,0:T(8,128)(2,1)}, u32[]{:S(2)}) copy-start(bf16[1,256,512]{2,1,0:T(8,128)(2,1)} %param.7) | copy-start | bytes 786436
  18.1 10.6 %collective-permute-start.5 = (bf16[2,192,512]{2,1,0:T(8,128)(2,1)}, bf16[2,192,512]{2,1,0:T(8,128)(2,1)S(1)}, u32[]{:S(2)}, u32[]{:S(2)}) collective-permute-start(bf16[2,192,512]{2,1,0:T(8,128)(2,1)} %get-tuple-element.48.chip_ref), channel_id=1, source_target_pairs={{0,4},{4,0},{1,5},{5,1},{2,6},{6,2},{3,7},{7,3},{8,12},{12,8},{9,1... | collective-permute-start | bytes 1179656 | tf_op jit(solution)/shard_map/ppermute | solution.py:364
  21.6 7.1 %collective-permute-start.7 = (bf16[2,32,512]{2,1,0:T(8,128)(2,1)S(1)}, bf16[2,32,512]{2,1,0:T(8,128)(2,1)S(1)}, u32[]{:S(2)}, u32[]{:S(2)}) collective-permute-start(bf16[2,32,512]{2,1,0:T(8,128)(2,1)S(1)} %collective-permute-done.6.near_ref), channel_id=1, source_target_pairs={{0,4},{4,0},{1,5},{5,1},{2,6},{6,2},{3,7},{7,3},{8,12},{12,8},{9,1... | collective-permute-start | bytes 196616 | tf_op jit(solution)/shard_map/ppermute | solution.py:364
  28.7 2.7 %collective-permute-start = (bf16[8,2,16,512]{3,2,1,0:T(8,128)(2,1)S(1)}, bf16[8,2,16,512]{3,2,1,0:T(8,128)(2,1)S(1)}, u32[]{:S(2)}, u32[]{:S(2)}) collective-permute-start(bf16[8,2,16,512]{3,2,1,0:T(8,128)(2,1)S(1)} %all-to-all-done.far_ref), channel_id=1, source_target_pairs={{0,4},{4,0},{1,5},{5,1},{2,6},{6,2},{3,7},{7,3},{8,12},{12,8},{9,1... | collective-permute-start | bytes 786440 | tf_op jit(solution)/shard_map/ppermute | solution.py:364
  31.4 2.6 %copy-start.1 = (bf16[1,256,512]{2,1,0:T(8,128)(2,1)S(1)}, bf16[1,256,512]{2,1,0:T(8,128)(2,1)}, u32[]{:S(2)}) copy-start(bf16[1,256,512]{2,1,0:T(8,128)(2,1)} %param.9) | copy-start | bytes 786436
  34.0 1.6 %copy-start = (bf16[512,2048]{1,0:T(8,128)(2,1)S(1)}, bf16[512,2048]{1,0:T(8,128)(2,1)}, u32[]{:S(2)}) copy-start(bf16[512,2048]{1,0:T(8,128)(2,1)} %w_hbm.1) | copy-start | bytes 6291460
  34.7 2.9 %collective-permute-start.11 = (bf16[4,8,128,128]{3,2,1,0:T(8,128)(2,1)S(1)}, bf16[4,8,128,128]{3,2,1,0:T(8,128)(2,1)S(1)}, u32[]{:S(2)}, u32[]{:S(2)}) collective-permute-start(bf16[4,8,128,128]{3,2,1,0:T(8,128)(2,1)S(1)} %get-tuple-element.63), channel_id=1, source_target_pairs={{0,4},{4,0},{1,5},{5,1},{2,6},{6,2},{3,7},{7,3},{8,12},{12,8},{9,1... | collective-permute-start | bytes 3145736 | tf_op jit(solution)/shard_map/ppermute | solution.py:364
  37.8 13.6 %collective-permute-start.14 = (bf16[8,128,128]{2,1,0:T(8,128)(2,1)S(1)}, bf16[8,128,128]{2,1,0:T(8,128)(2,1)S(1)}, u32[]{:S(2)}, u32[]{:S(2)}) collective-permute-start(bf16[8,128,128]{2,1,0:T(8,128)(2,1)S(1)} %get-tuple-element.77), channel_id=1, source_target_pairs={{0,128},{64,192},{128,0},{192,64},{1,129},{65,193},{129,1},{193,65... | collective-permute-start | bytes 786440 | tf_op jit(solution)/shard_map/ppermute | solution.py:364
  41.0 12.7 %collective-permute-start.15 = (bf16[8,128,128]{2,1,0:T(8,128)(2,1)S(1)}, bf16[8,128,128]{2,1,0:T(8,128)(2,1)S(1)}, u32[]{:S(2)}, u32[]{:S(2)}) collective-permute-start(bf16[8,128,128]{2,1,0:T(8,128)(2,1)S(1)} %get-tuple-element.78), channel_id=1, source_target_pairs={{0,64},{64,128},{128,192},{192,0},{1,65},{65,129},{129,193},{193,1... | collective-permute-start | bytes 786440 | tf_op jit(solution)/shard_map/ppermute | solution.py:364
  41.5 12.3 %collective-permute-start.16 = (bf16[8,128,128]{2,1,0:T(8,128)(2,1)S(1)}, bf16[8,128,128]{2,1,0:T(8,128)(2,1)S(1)}, u32[]{:S(2)}, u32[]{:S(2)}) collective-permute-start(bf16[8,128,128]{2,1,0:T(8,128)(2,1)S(1)} %get-tuple-element.79), channel_id=1, source_target_pairs={{0,192},{64,0},{128,64},{192,128},{1,193},{65,1},{129,65},{193,129... | collective-permute-start | bytes 786440 | tf_op jit(solution)/shard_map/ppermute | solution.py:364
  48.9 5.0 %copy-start.6 = (f32[2,256,512]{2,1,0:T(8,128)}, f32[2,256,512]{2,1,0:T(8,128)S(1)}, u32[]{:S(2)}) copy-start(f32[2,256,512]{2,1,0:T(8,128)S(1)} %get-tuple-element.73.mid_ref) | copy-start | bytes 3145732
  48.9 5.0 %collective-permute-start.13 = (bf16[2,128,512]{2,1,0:T(8,128)(2,1)S(1)}, bf16[2,128,512]{2,1,0:T(8,128)(2,1)S(1)}, u32[]{:S(2)}, u32[]{:S(2)}) collective-permute-start(bf16[2,128,512]{2,1,0:T(8,128)(2,1)S(1)} %get-tuple-element.76), channel_id=1, source_target_pairs={{4,8},{12,16},{20,24},{28,32},{36,40},{44,48},{52,56},{8,4},{16,12... | collective-permute-start | bytes 786440 | tf_op jit(solution)/shard_map/ppermute | solution.py:434
  49.6 4.4 %collective-permute-start.12 = (bf16[2,288,512]{2,1,0:T(8,128)(2,1)S(1)}, bf16[2,288,512]{2,1,0:T(8,128)(2,1)S(1)}, u32[]{:S(2)}, u32[]{:S(2)}) collective-permute-start(bf16[2,288,512]{2,1,0:T(8,128)(2,1)S(1)} %get-tuple-element.75), channel_id=1, source_target_pairs={{0,4},{4,0},{1,5},{5,1},{2,6},{6,2},{3,7},{7,3},{8,12},{12,8},{9,1... | collective-permute-start | bytes 1769480 | tf_op jit(solution)/shard_map/ppermute | solution.py:364
  54.8 24.7 %all-to-all-start.1 = ((bf16[8,256,128]{2,1,0:T(8,128)(2,1)}), bf16[8,256,128]{2,1,0:T(8,128)(2,1)S(1)}, u32[]{:S(2)}, u32[]{:S(2)}) async-start(bf16[8,256,128]{2,1,0:T(8,128)(2,1)} %get-tuple-element.82), calls=%async_computation.1 | async-start | bytes 1048576 | tf_op jit(solution)/shard_map/all_to_all | solution.py:443
  63.6 10.6 %collective-permute-start.8 = (bf16[256,512]{1,0:T(8,128)(2,1)S(1)}, bf16[256,512]{1,0:T(8,128)(2,1)S(1)}, u32[]{:S(2)}, u32[]{:S(2)}) collective-permute-start(bf16[256,512]{1,0:T(8,128)(2,1)S(1)} %get-tuple-element.59), channel_id=1, source_target_pairs={{0,2},{1,3},{2,0},{3,1},{4,6},{5,7},{6,4},{7,5},{8,10},{9,11},{10,... | collective-permute-start | bytes 786440 | tf_op jit(solution)/shard_map/ppermute | solution.py:364
  63.7 11.4 %collective-permute-start.9 = (bf16[256,512]{1,0:T(8,128)(2,1)S(1)}, bf16[256,512]{1,0:T(8,128)(2,1)S(1)}, u32[]{:S(2)}, u32[]{:S(2)}) collective-permute-start(bf16[256,512]{1,0:T(8,128)(2,1)S(1)} %get-tuple-element.60), channel_id=1, source_target_pairs={{0,1},{1,2},{2,3},{3,0},{4,5},{5,6},{6,7},{7,4},{8,9},{9,10},{10,1... | collective-permute-start | bytes 786440 | tf_op jit(solution)/shard_map/ppermute | solution.py:364
  66.4 10.6 %collective-permute-start.10 = (bf16[256,512]{1,0:T(8,128)(2,1)S(1)}, bf16[256,512]{1,0:T(8,128)(2,1)S(1)}, u32[]{:S(2)}, u32[]{:S(2)}) collective-permute-start(bf16[256,512]{1,0:T(8,128)(2,1)S(1)} %get-tuple-element.61), channel_id=1, source_target_pairs={{0,3},{1,0},{2,1},{3,2},{4,7},{5,4},{6,5},{7,6},{8,11},{9,8},{10,9... | collective-permute-start | bytes 786440 | tf_op jit(solution)/shard_map/ppermute | solution.py:364
  77.8 5.1 %copy-start.7 = (f32[2,256,512]{2,1,0:T(8,128)S(1)}, f32[2,256,512]{2,1,0:T(8,128)}, u32[]{:S(2)}) copy-start(f32[2,256,512]{2,1,0:T(8,128)} %copy-done.6) | copy-start | bytes 3145732
  77.8 5.1 %collective-permute-start.17 = (bf16[2,32,512]{2,1,0:T(8,128)(2,1)S(1)}, bf16[2,32,512]{2,1,0:T(8,128)(2,1)S(1)}, u32[]{:S(2)}, u32[]{:S(2)}) collective-permute-start(bf16[2,32,512]{2,1,0:T(8,128)(2,1)S(1)} %get-tuple-element.81), channel_id=1, source_target_pairs={{0,8},{8,0},{16,24},{24,16},{32,40},{40,32},{48,56},{56,48},{1,9},... | collective-permute-start | bytes 196616 | tf_op jit(solution)/shard_map/ppermute | solution.py:364
  79.6 5.2 %collective-permute-start.20 = (bf16[128,128]{1,0:T(8,128)(2,1)S(1)}, bf16[128,128]{1,0:T(8,128)(2,1)S(1)}, u32[]{:S(2)}, u32[]{:S(2)}) collective-permute-start(bf16[128,128]{1,0:T(8,128)(2,1)S(1)} %shard_map.103._.a_ref), channel_id=1, source_target_pairs={{0,64},{64,128},{128,192},{192,0},{1,65},{65,129},{129,193},{193,1... | collective-permute-start | bytes 98312 | tf_op jit(solution)/shard_map/ppermute | solution.py:364
  79.7 5.5 %collective-permute-start.19 = (bf16[128,128]{1,0:T(8,128)(2,1)S(1)}, bf16[128,128]{1,0:T(8,128)(2,1)S(1)}, u32[]{:S(2)}, u32[]{:S(2)}) collective-permute-start(bf16[128,128]{1,0:T(8,128)(2,1)S(1)} %shard_map.103._.a_ref), channel_id=1, source_target_pairs={{0,128},{64,192},{128,0},{192,64},{1,129},{65,193},{129,1},{193,65... | collective-permute-start | bytes 98312 | tf_op jit(solution)/shard_map/ppermute | solution.py:364
  81.4 4.6 %collective-permute-start.18 = (bf16[128,128]{1,0:T(8,128)(2,1)S(1)}, bf16[128,128]{1,0:T(8,128)(2,1)S(1)}, u32[]{:S(2)}, u32[]{:S(2)}) collective-permute-start(bf16[128,128]{1,0:T(8,128)(2,1)S(1)} %shard_map.103._.a_ref), channel_id=1, source_target_pairs={{0,192},{64,0},{128,64},{192,128},{1,193},{65,1},{129,65},{193,129... | collective-permute-start | bytes 98312 | tf_op jit(solution)/shard_map/ppermute | solution.py:364

commit v5 on v4

--- a/solution.py
+++ b/solution.py
@@ -14,9 +14,9 @@
 HEADS = 4
 ROWS = 256
 WIDTH = 512
-NEAR = 704
-JOINT = 576
-FAR = 192
+NEAR = 640
+JOINT = 512
+FAR = 256
 BF = jnp.bfloat16
 F32 = jnp.float32
 LIMIT = 36 * 1024 * 1024
@@ -38,19 +38,19 @@
 
 
 def top_near():
+    r = lax.broadcasted_iota(jnp.int32, (64, 128), 0)
+    j = lax.broadcasted_iota(jnp.int32, (64, 128), 1)
+    return jnp.where((j >> 4) == r, 0.0625, 0.0).astype(BF)
+
+
+def top_far():
     r = lax.broadcasted_iota(jnp.int32, (64, 192), 0)
     j = lax.broadcasted_iota(jnp.int32, (64, 192), 1)
-    l0 = (j < 128) & ((j >> 4) == r)
-    l1 = (j >= 128) & (8 + ((j - 128) >> 3) == r)
-    return (jnp.where(l0, 0.0625, 0.0) + jnp.where(l1, 0.125, 0.0)).astype(BF)
-
-
-def top_far():
-    r = lax.broadcasted_iota(jnp.int32, (64, 128), 0)
-    j = lax.broadcasted_iota(jnp.int32, (64, 128), 1)
-    l2 = (j < 64) & (16 + (j >> 2) == r)
-    l3 = (j >= 64) & (32 + ((j - 64) >> 1) == r)
-    return (jnp.where(l2, 0.25, 0.0) + jnp.where(l3, 0.5, 0.0)).astype(BF)
+    l1 = (j < 64) & (8 + (j >> 3) == r)
+    l2 = (j >= 64) & (j < 128) & (16 + ((j - 64) >> 2) == r)
+    l3 = (j >= 128) & (32 + ((j - 128) >> 1) == r)
+    out = jnp.where(l1, 0.125, 0.0) + jnp.where(l2, 0.25, 0.0) + jnp.where(l3, 0.5, 0.0)
+    return out.astype(BF)
 
 
 def dot(a, b, dims):
@@ -88,7 +88,7 @@
 
 
 def near_kernel(
-    _, q_ref, k_ref, v_ref, edge_ref, chip_ref, sib_ref, near_ref, nearo_ref,
+    _, q_ref, k_ref, v_ref, edge_ref, chip_ref, sib_ref,
     keys_ref, vals_ref, exps_ref, part_ref, max_ref, sum_ref,
 ):
     z, c = lax.axis_index("z"), lax.axis_index("core")
@@ -102,9 +102,7 @@
             out[h, 128:384] = own_ref[:, at_h]
             out[h, 384:448] = chip_ref[part, 0:64, at_h]
             out[h, 448:512] = sib_ref[part, 0:64, at_h]
-            out[h, 512:544] = near_ref[part, :, at_h]
-            out[h, 544:576] = nearo_ref[part, :, at_h]
-            out[h, 576:704] = jnp.where(c == 0, beside, across)
+            out[h, 512:640] = jnp.where(c == 0, beside, across)
         for n in range(2):
             rows = slice(n * NR, (n + 1) * NR)
             span = slice(n * NR, n * NR + JOINT)
@@ -124,7 +122,7 @@
 
 
 def far_kernel(
-    q_ref, far_ref, faro_ref, keys_ref, vals_ref, part_ref, max_ref, sum_ref,
+    q_ref, near_ref, nearo_ref, far_ref, faro_ref, keys_ref, vals_ref, part_ref, max_ref, sum_ref,
     att_ref, attt_ref, exps_ref, fkeys_ref, fvals_ref, rnear_ref, rfar_ref,
 ):
     z = lax.axis_index("z")
@@ -132,16 +130,18 @@
     for h in range(HEADS):
         at_h = slice(h * DH, (h + 1) * DH)
         for part, near, out in ((0, keys_ref, fkeys_ref), (1, vals_ref, fvals_ref)):
+            out[h, 0:32] = near_ref[part, :, at_h]
+            out[h, 32:64] = nearo_ref[part, :, at_h]
             for d in (2, 3):
-                at = (d - 2) * 32
+                at = 64 + (d - 2) * 32
                 out[h, at : at + 16] = far_ref[z ^ d, part, :, at_h]
                 out[h, at + 16 : at + 32] = faro_ref[z ^ d, part, :, at_h]
             for d in range(4, 8):
-                at = 64 + (d - 4) * 16
+                at = 128 + (d - 4) * 16
                 low, high = far_ref[z ^ d, part, :, at_h], faro_ref[z ^ d, part, :, at_h]
                 out[h, at : at + 16] = jnp.concatenate([low[0:8], high[0:8]], axis=0)
-            top = dot(by_near, near[h, 384:576], NN) + dot(by_far, out[h, 0:128], NN)
-            out[h, 128:192] = top.astype(BF)
+            top = dot(by_near, near[h, 384:512], NN) + dot(by_far, out[h, 0:192], NN)
+            out[h, 192:256] = top.astype(BF)
         scores = dot(q_ref[:, at_h], fkeys_ref[h], NT)
         first = max_ref[h]
         highest = jnp.maximum(first, jnp.max(scores, axis=1, keepdims=True))
@@ -219,8 +219,8 @@
         dq = dot(sgrad, fkeys_ref[h], NN)
         fgk, fgv = dot(sgrad, q, TN), dot(p.astype(BF), da, TN)
         gk, gv = gk_ref.at[h], gv_ref.at[h]
-        gk[576:704] = jnp.zeros((128, DH), F32)
-        gv[576:704] = jnp.zeros((128, DH), F32)
+        gk[512:640] = jnp.zeros((128, DH), F32)
+        gv[512:640] = jnp.zeros((128, DH), F32)
         for n in range(2):
             rows = slice(n * NR, (n + 1) * NR)
             span = slice(n * NR, n * NR + JOINT)
@@ -230,31 +230,31 @@
             p = p.astype(BF)
             dq_ref[rows, at_h] = (dq[rows] + dot(sgrad, keys_ref[h, span], NN)).astype(BF)
             if n == 0:
-                gk[0:576] = dot(sgrad, q[rows], TN)
-                gv[0:576] = dot(p, da[rows], TN)
+                gk[0:512] = dot(sgrad, q[rows], TN)
+                gv[0:512] = dot(p, da[rows], TN)
             else:
-                gk[128:704] += dot(sgrad, q[rows], TN)
-                gv[128:704] += dot(p, da[rows], TN)
+                gk[128:640] += dot(sgrad, q[rows], TN)
+                gv[128:640] += dot(p, da[rows], TN)
         for part, g, f in ((0, gk, fgk), (1, gv, fgv)):
-            high = f[128:192]
+            high = f[192:256]
             hi = high.astype(BF)
             lo = (high - hi.astype(F32)).astype(BF)
-            near = g[384:576] + dot(by_near, hi, TN) + dot(by_near, lo, TN)
-            far = f[0:128] + dot(by_far, hi, TN) + dot(by_far, lo, TN)
-            before, after = g[0:128].astype(BF), g[576:704].astype(BF)
+            near = g[384:512] + dot(by_near, hi, TN) + dot(by_near, lo, TN)
+            far = f[0:192] + dot(by_far, hi, TN) + dot(by_far, lo, TN)
+            before, after = g[0:128].astype(BF), g[512:640].astype(BF)
             edge_ref[part, :, at_h] = jnp.where(c == 0, before, after)
             cross_ref[part, 160:288, at_h] = jnp.where(c == 0, after, before)
             mid_ref[part, :, at_h] = g[128:384]
             own_ref[part, :, at_h] = near[0:64]
             cross_ref[part, 0:64, at_h] = near[64:128].astype(BF)
-            cross_ref[part, 64:96, at_h] = near[160:192].astype(BF)
-            minec_ref[part, 0:32, at_h] = near[128:160]
+            cross_ref[part, 64:96, at_h] = far[32:64].astype(BF)
+            minec_ref[part, 0:32, at_h] = far[0:32]
             for d in (2, 3):
-                at, to = (d - 2) * 32, 32 + (d - 2) * 16
+                at, to = 64 + (d - 2) * 32, 32 + (d - 2) * 16
                 minec_ref[part, to : to + 16, at_h] = far[at : at + 16]
                 cross_ref[part, 64 + to : 64 + to + 16, at_h] = far[at + 16 : at + 32].astype(BF)
             for d in (4, 6):
-                at, to = 64 + (d - 4) * 16, 64 + (d - 4) * 8
+                at, to = 128 + (d - 4) * 16, 64 + (d - 4) * 8
                 minec_ref[part, to : to + 8, at_h] = far[at : at + 8]
                 minec_ref[part, to + 8 : to + 16, at_h] = far[at + 16 : at + 24]
                 both = jnp.concatenate([far[at + 8 : at + 16], far[at + 24 : at + 32]], axis=0)
@@ -394,13 +394,13 @@
 
     column = sds((HEADS, ROWS, 1), F32)
     keys_near, vals_near, exps, part, top, total = call(
-        near_kernel, [(AFTER, token)] + here(q, k, v, edge_got, chip, sib, near_got, near_other),
+        near_kernel, [(AFTER, token)] + here(q, k, v, edge_got, chip, sib),
         [sds((HEADS, NEAR, DH), BF), sds((HEADS, NEAR, DH), BF), sds((HEADS, 2, NR, JOINT), BF),
          sds((ROWS, WIDTH), F32), column, column],
         us=20,
     )
     att, attt, far_exps, keys_far, vals_far, rnear, rfar = call(
-        far_kernel, here(q, far_got, far_other, keys_near, vals_near, part, top, total),
+        far_kernel, here(q, near_got, near_other, far_got, far_other, keys_near, vals_near, part, top, total),
         [sds((ROWS, WIDTH), BF), sds((WIDTH, ROWS), BF), sds((HEADS, ROWS, FAR), BF),
          sds((HEADS, FAR, DH), BF), sds((HEADS, FAR, DH), BF), column, column],
     )

time: 88.2 us -> 87.7 us (level)
  transfers between devices with their start and end apart: 23 -> 23, of which waited for: 10 -> 10; matrix products, arithmetic and copies ran while one was open for 0% -> 0% of each run, Pallas kernels for 16% -> 15%
where the time goes in v5:
time: 87.7 us; the launch traced here: 86.3 us
  starting transfers between devices  44.6 us (51%)
  waiting for transfers between devices  22.2 us (25%)
  Pallas kernels  18.3 us (21%)
    ppermute x19, starting transfers between devices, permute(): return lax.ppermute(x, axis, [(i, move(i) % size) for i in range(size)])  27.2 us
    pallas_call x14, Pallas kernels, call(): pl.pallas_call(kernel, out_shape=outs, in_specs=[spec for spec, _ in oper...  18.3 us
    ppermute x19, waiting for transfers between devices, permute(): return lax.ppermute(x, axis, [(i, move(i) % size) for i in range(size)])  15.2 us
    all_to_all x1, starting transfers between devices, body(): both_got = lax.all_to_all(both, 'z', 0, 0)  8.57 us
    all_to_all x1, starting transfers between devices, body(): far_got = lax.all_to_all(far, 'z', 0, 0)  7.57 us
    all_to_all x1, waiting for transfers between devices, body(): far_got = lax.all_to_all(far, 'z', 0, 0)  7 us
  transfers between devices with their start and end apart: 23, of which 10 were waited for; matrix products, arithmetic and copies ran while one was open for 0% of the time, Pallas kernels for 15%

profile of v5, /device:TPU:8, one launch (start us, length us, event | category | flops | bytes accessed | tf_op | source)
XLA Modules:
  0.0 86.3 jit_solution(14309436321993417121)
XLA Ops:
  0.6 1.7 %collective-permute-start.5 = (bf16[256,512]{1,0:T(8,128)(2,1)}, bf16[256,512]{1,0:T(8,128)(2,1)S(1)}, u32[]{:S(2)}, u32[]{:S(2)}) collective-permute-start(bf16[256,512]{1,0:T(8,128)(2,1)} %bitcast.9), channel_id=1, source_target_pairs={{0,1},{1,2},{2,3},{3,0},{4,5},{5,6},{6,7},{7,4},{8,9},{9,10},{10,1... | collective-permute-start | bytes 786440 | tf_op jit(solution)/shard_map/ppermute | solution.py:364
  2.3 2.7 %collective-permute-start.4 = (bf16[256,512]{1,0:T(8,128)(2,1)}, bf16[256,512]{1,0:T(8,128)(2,1)S(1)}, u32[]{:S(2)}, u32[]{:S(2)}) collective-permute-start(bf16[256,512]{1,0:T(8,128)(2,1)} %bitcast.10), channel_id=1, source_target_pairs={{0,2},{1,3},{2,0},{3,1},{4,6},{5,7},{6,4},{7,5},{8,10},{9,11},{10,... | collective-permute-start | bytes 786440 | tf_op jit(solution)/shard_map/ppermute | solution.py:364
  5.0 0.7 collective-permute-start.3
  5.6 2.2 %shard_map.92 = (bf16[2,192,512]{2,1,0:T(8,128)(2,1)}, bf16[2,32,512]{2,1,0:T(8,128)(2,1)}, bf16[8,2,16,512]{3,2,1,0:T(8,128)(2,1)}, bf16[2,128,512]{2,1,0:T(8,128)(2,1)}) custom-call(bf16[256,512]{1,0:T(8,128)(2,1)} %bitcast.17, bf16[256,512]{1,0:T(8,128)(2,1)} %bitcast.19), custom_call_target="tpu_custom_call" | custom-call | flops 1000000000 | bytes 1 | tf_op jit(solution)/shard_map/pallas_call | solution.py:347
  7.8 2.0 %collective-permute-start = (bf16[2,32,512]{2,1,0:T(8,128)(2,1)}, bf16[2,32,512]{2,1,0:T(8,128)(2,1)S(1)}, u32[]{:S(2)}, u32[]{:S(2)}) collective-permute-start(bf16[2,32,512]{2,1,0:T(8,128)(2,1)} %get-tuple-element.46), channel_id=1, source_target_pairs={{0,8},{8,0},{16,24},{24,16},{32,40},{40,32},{48,56},{56,48},{1,9},... | collective-permute-start | bytes 196616 | tf_op jit(solution)/shard_map/ppermute | solution.py:364
  9.8 7.6 %all-to-all-start = ((bf16[8,2,16,512]{3,2,1,0:T(8,128)(2,1)}), bf16[8,2,16,512]{3,2,1,0:T(8,128)(2,1)S(1)}, u32[]{:S(2)}, u32[]{:S(2)}) async-start(bf16[8,2,16,512]{3,2,1,0:T(8,128)(2,1)} %get-tuple-element.47), calls=%async_computation | async-start | bytes 524288 | tf_op jit(solution)/shard_map/all_to_all | solution.py:389
  17.4 0.7 collective-permute-start.6
  18.1 3.5 %collective-permute-start.7 = (bf16[2,192,512]{2,1,0:T(8,128)(2,1)}, bf16[2,192,512]{2,1,0:T(8,128)(2,1)S(1)}, u32[]{:S(2)}, u32[]{:S(2)}) collective-permute-start(bf16[2,192,512]{2,1,0:T(8,128)(2,1)} %get-tuple-element.49.chip_ref), channel_id=1, source_target_pairs={{0,4},{4,0},{1,5},{5,1},{2,6},{6,2},{3,7},{7,3},{8,12},{12,8},{9,1... | collective-permute-start | bytes 1179656 | tf_op jit(solution)/shard_map/ppermute | solution.py:364
  21.7 7.0 %all-to-all-done.far_ref = bf16[8,2,16,512]{3,2,1,0:T(8,128)(2,1)S(1)} async-done(((bf16[8,2,16,512]{3,2,1,0:T(8,128)(2,1)}), bf16[8,2,16,512]{3,2,1,0:T(8,128)(2,1)S(1)}, u32[]{:S(2)}, u32[]{:S(2)}) %all-to-all-start) | async-done | bytes 262176 | tf_op jit(solution)/shard_map/all_to_all | solution.py:389
  28.8 2.3 %shard_map.94 = (bf16[4,640,128]{2,1,0:T(8,128)(2,1)S(1)}, bf16[4,640,128]{2,1,0:T(8,128)(2,1)S(1)}, bf16[4,2,128,512]{3,2,1,0:T(8,128)(2,1)S(1)}, f32[256,512]{...) custom-call(f32[8,128]{1,0:T(8,128)S(1)} %shard_map.93._, bf16[256,512]{1,0:T(8,128)(2,1)S(1)} %bitcast.14, ...), custom_call_target="tpu_custom_call" | custom-call | flops 20000000000 | bytes 1 | tf_op jit(solution)/shard_map/pallas_call | solution.py:347
  31.1 2.6 %shard_map.95 = (bf16[256,512]{1,0:T(8,128)(2,1)S(1)}, bf16[512,256]{1,0:T(8,128)(2,1)S(1)}, bf16[4,256,256]{2,1,0:T(8,128)(2,1)S(1)}, bf16[4,256,128]{2,1,0:T(8...) custom-call(bf16[256,512]{1,0:T(8,128)(2,1)S(1)} %bitcast.15, ...), custom_call_target="tpu_custom_call" | custom-call | flops 1000000000 | bytes 1 | tf_op jit(solution)/shard_map/pallas_call | solution.py:347
  33.7 0.7 shard_map.96
  35.3 1.9 %shard_map.97 = (bf16[256,512]{1,0:T(8,128)(2,1)S(1)}, bf16[256,512]{1,0:T(8,128)(2,1)S(1)}, bf16[256,512]{1,0:T(8,128)(2,1)S(1)}, bf16[256,512]{1,0:T(8,128)(2,1)S(1)}, bf16[256,512]{1,0:T(8,128)(2,1)S(1)}) custom-call(bf16[4,8,128,128]{3,2,1,0:T(8,128)(2,1)S(1)} %get-tuple-element.56._.mine_ref, bf16[256,512]{1,0:T(8,128)(2,1)S(1)} %get-tuple-element.57.att_ref, ...), custom_call_target="tpu_custom_call" | custom-call | flops 1000000000 | bytes 1 | tf_op jit(solution)/shard_map/pallas_call | solution.py:347
  37.5 3.1 %collective-permute-start.14 = (bf16[8,128,128]{2,1,0:T(8,128)(2,1)S(1)}, bf16[8,128,128]{2,1,0:T(8,128)(2,1)S(1)}, u32[]{:S(2)}, u32[]{:S(2)}) collective-permute-start(bf16[8,128,128]{2,1,0:T(8,128)(2,1)S(1)} %get-tuple-element.77), channel_id=1, source_target_pairs={{0,128},{64,192},{128,0},{192,64},{1,129},{65,193},{129,1},{193,65... | collective-permute-start | bytes 786440 | tf_op jit(solution)/shard_map/ppermute | solution.py:364
  41.2 2.6 %collective-permute-start.16 = (bf16[8,128,128]{2,1,0:T(8,128)(2,1)S(1)}, bf16[8,128,128]{2,1,0:T(8,128)(2,1)S(1)}, u32[]{:S(2)}, u32[]{:S(2)}) collective-permute-start(bf16[8,128,128]{2,1,0:T(8,128)(2,1)S(1)} %get-tuple-element.79), channel_id=1, source_target_pairs={{0,192},{64,0},{128,64},{192,128},{1,193},{65,1},{129,65},{193,129... | collective-permute-start | bytes 786440 | tf_op jit(solution)/shard_map/ppermute | solution.py:364
  43.9 4.6 %shard_map.100 = (bf16[256,512]{1,0:T(8,128)(2,1)}, f32[2,256,512]{2,1,0:T(8,128)S(1)}, bf16[2,128,512]{2,1,0:T(8,128)(2,1)S(1)}, f32[2,64,512]{2,1,0:T(8,128)S(...) custom-call(bf16[8,128,128]{2,1,0:T(8,128)(2,1)S(1)} %get-tuple-element.64._.a_ref, ...), custom_call_target="tpu_custom_call" | custom-call | flops 20000000000 | bytes 1 | tf_op jit(solution)/shard_map/pallas_call | solution.py:347
  49.1 1.8 %collective-permute-start.12 = (bf16[2,288,512]{2,1,0:T(8,128)(2,1)S(1)}, bf16[2,288,512]{2,1,0:T(8,128)(2,1)S(1)}, u32[]{:S(2)}, u32[]{:S(2)}) collective-permute-start(bf16[2,288,512]{2,1,0:T(8,128)(2,1)S(1)} %get-tuple-element.75), channel_id=1, source_target_pairs={{0,4},{4,0},{1,5},{5,1},{2,6},{6,2},{3,7},{7,3},{8,12},{12,8},{9,1... | collective-permute-start | bytes 1769480 | tf_op jit(solution)/shard_map/ppermute | solution.py:364
  50.9 2.4 %collective-permute-done.15.c_ref = bf16[8,128,128]{2,1,0:T(8,128)(2,1)S(1)} collective-permute-done((bf16[8,128,128]{2,1,0:T(8,128)(2,1)S(1)}, bf16[8,128,128]{2,1,0:T(8,128)(2,1)S(1)}, u32[]{:S(2)}, u32[]{:S(2)}) %collective-permute-start.15) | collective-permute-done | bytes 262176 | tf_op jit(solution)/shard_map/ppermute | solution.py:364
  53.7 0.9 shard_map.102
  54.5 8.6 %all-to-all-start.1 = ((bf16[8,256,128]{2,1,0:T(8,128)(2,1)}), bf16[8,256,128]{2,1,0:T(8,128)(2,1)S(1)}, u32[]{:S(2)}, u32[]{:S(2)}) async-start(bf16[8,256,128]{2,1,0:T(8,128)(2,1)} %get-tuple-element.82), calls=%async_computation.1 | async-start | bytes 1048576 | tf_op jit(solution)/shard_map/all_to_all | solution.py:443
  63.3 2.6 %collective-permute-start.9 = (bf16[256,512]{1,0:T(8,128)(2,1)S(1)}, bf16[256,512]{1,0:T(8,128)(2,1)S(1)}, u32[]{:S(2)}, u32[]{:S(2)}) collective-permute-start(bf16[256,512]{1,0:T(8,128)(2,1)S(1)} %get-tuple-element.60), channel_id=1, source_target_pairs={{0,1},{1,2},{2,3},{3,0},{4,5},{5,6},{6,7},{7,4},{8,9},{9,10},{10,1... | collective-permute-start | bytes 786440 | tf_op jit(solution)/shard_map/ppermute | solution.py:364
  65.9 7.8 %collective-permute-done.8.b_ref = bf16[256,512]{1,0:T(8,128)(2,1)S(1)} collective-permute-done((bf16[256,512]{1,0:T(8,128)(2,1)S(1)}, bf16[256,512]{1,0:T(8,128)(2,1)S(1)}, u32[]{:S(2)}, u32[]{:S(2)}) %collective-permute-start.8) | collective-permute-done | bytes 262176 | tf_op jit(solution)/shard_map/ppermute | solution.py:364
  73.7 0.9 %collective-permute-done.9.c_ref = bf16[256,512]{1,0:T(8,128)(2,1)S(1)} collective-permute-done((bf16[256,512]{1,0:T(8,128)(2,1)S(1)}, bf16[256,512]{1,0:T(8,128)(2,1)S(1)}, u32[]{:S(2)}, u32[]{:S(2)}) %collective-permute-start.9) | collective-permute-done | bytes 262176 | tf_op jit(solution)/shard_map/ppermute | solution.py:364
  74.7 1.8 %collective-permute-done.10.d_ref = bf16[256,512]{1,0:T(8,128)(2,1)S(1)} collective-permute-done((bf16[256,512]{1,0:T(8,128)(2,1)S(1)}, bf16[256,512]{1,0:T(8,128)(2,1)S(1)}, u32[]{:S(2)}, u32[]{:S(2)}) %collective-permute-start.10) | collective-permute-done | bytes 262176 | tf_op jit(solution)/shard_map/ppermute | solution.py:364
  76.5 0.8 shard_map.98
  77.3 1.7 %collective-permute-start.17 = (bf16[2,32,512]{2,1,0:T(8,128)(2,1)S(1)}, bf16[2,32,512]{2,1,0:T(8,128)(2,1)S(1)}, u32[]{:S(2)}, u32[]{:S(2)}) collective-permute-start(bf16[2,32,512]{2,1,0:T(8,128)(2,1)S(1)} %get-tuple-element.81), channel_id=1, source_target_pairs={{0,8},{8,0},{16,24},{24,16},{32,40},{40,32},{48,56},{56,48},{1,9},... | collective-permute-start | bytes 196616 | tf_op jit(solution)/shard_map/ppermute | solution.py:364
  79.2 1.7 %collective-permute-start.19 = (bf16[128,128]{1,0:T(8,128)(2,1)S(1)}, bf16[128,128]{1,0:T(8,128)(2,1)S(1)}, u32[]{:S(2)}, u32[]{:S(2)}) collective-permute-start(bf16[128,128]{1,0:T(8,128)(2,1)S(1)} %shard_map.103._.a_ref), channel_id=1, source_target_pairs={{0,128},{64,192},{128,0},{192,64},{1,129},{65,193},{129,1},{193,65... | collective-permute-start | bytes 98312 | tf_op jit(solution)/shard_map/ppermute | solution.py:364
  81.0 1.5 %collective-permute-start.18 = (bf16[128,128]{1,0:T(8,128)(2,1)S(1)}, bf16[128,128]{1,0:T(8,128)(2,1)S(1)}, u32[]{:S(2)}, u32[]{:S(2)}) collective-permute-start(bf16[128,128]{1,0:T(8,128)(2,1)S(1)} %shard_map.103._.a_ref), channel_id=1, source_target_pairs={{0,192},{64,0},{128,64},{192,128},{1,193},{65,1},{129,65},{193,129... | collective-permute-start | bytes 98312 | tf_op jit(solution)/shard_map/ppermute | solution.py:364
  82.5 1.2 %shard_map.104 = (bf16[256,512]{1,0:T(8,128)(2,1)}, bf16[256,512]{1,0:T(8,128)(2,1)}, f32[8,128]{1,0:T(8,128)S(1)}) custom-call(f32[2,256,512]{2,1,0:T(8,128)S(1)} %copy-done.7, f32[2,64,512]{2,1,0:T(8,128)S(1)} %get-tuple-element.74.own_ref, bf16[2,288,512]{2,1,0:T(8,128)(2,1)S(1)} %collective-permute-done.12.got_ref, ...), custom_call_target="tpu_custom_call" | custom-call | flops 1000000000 | bytes 1 | tf_op jit(solution)/shard_map/pallas_call | solution.py:347
  83.7 0.7 collective-permute-done.20.d_ref
  84.7 0.8 collective-permute-done.18.b_ref
  85.6 0.7 shard_map.105
  (44 shorter events, 3.6 us)
Async XLA Ops:
  0.6 21.0 %collective-permute-start.5 = (bf16[256,512]{1,0:T(8,128)(2,1)}, bf16[256,512]{1,0:T(8,128)(2,1)S(1)}, u32[]{:S(2)}, u32[]{:S(2)}) collective-permute-start(bf16[256,512]{1,0:T(8,128)(2,1)} %bitcast.9), channel_id=1, source_target_pairs={{0,1},{1,2},{2,3},{3,0},{4,5},{5,6},{6,7},{7,4},{8,9},{9,10},{10,1... | collective-permute-start | bytes 786440 | tf_op jit(solution)/shard_map/ppermute | solution.py:364
  2.3 19.4 %collective-permute-start.4 = (bf16[256,512]{1,0:T(8,128)(2,1)}, bf16[256,512]{1,0:T(8,128)(2,1)S(1)}, u32[]{:S(2)}, u32[]{:S(2)}) collective-permute-start(bf16[256,512]{1,0:T(8,128)(2,1)} %bitcast.10), channel_id=1, source_target_pairs={{0,2},{1,3},{2,0},{3,1},{4,6},{5,7},{6,4},{7,5},{8,10},{9,11},{10,... | collective-permute-start | bytes 786440 | tf_op jit(solution)/shard_map/ppermute | solution.py:364
  5.0 16.8 %collective-permute-start.3 = (bf16[256,512]{1,0:T(8,128)(2,1)}, bf16[256,512]{1,0:T(8,128)(2,1)S(1)}, u32[]{:S(2)}, u32[]{:S(2)}) collective-permute-start(bf16[256,512]{1,0:T(8,128)(2,1)} %bitcast.11), channel_id=1, source_target_pairs={{0,3},{1,0},{2,1},{3,2},{4,7},{5,4},{6,5},{7,6},{8,11},{9,8},{10,9... | collective-permute-start | bytes 786440 | tf_op jit(solution)/shard_map/ppermute | solution.py:364
  7.8 10.2 %collective-permute-start = (bf16[2,32,512]{2,1,0:T(8,128)(2,1)}, bf16[2,32,512]{2,1,0:T(8,128)(2,1)S(1)}, u32[]{:S(2)}, u32[]{:S(2)}) collective-permute-start(bf16[2,32,512]{2,1,0:T(8,128)(2,1)} %get-tuple-element.46), channel_id=1, source_target_pairs={{0,8},{8,0},{16,24},{24,16},{32,40},{40,32},{48,56},{56,48},{1,9},... | collective-permute-start | bytes 196616 | tf_op jit(solution)/shard_map/ppermute | solution.py:364
  9.8 18.9 %all-to-all-start = ((bf16[8,2,16,512]{3,2,1,0:T(8,128)(2,1)}), bf16[8,2,16,512]{3,2,1,0:T(8,128)(2,1)S(1)}, u32[]{:S(2)}, u32[]{:S(2)}) async-start(bf16[8,2,16,512]{3,2,1,0:T(8,128)(2,1)} %get-tuple-element.47), calls=%async_computation | async-start | bytes 524288 | tf_op jit(solution)/shard_map/all_to_all | solution.py:389
  17.4 11.3 %collective-permute-start.6 = (bf16[2,128,512]{2,1,0:T(8,128)(2,1)}, bf16[2,128,512]{2,1,0:T(8,128)(2,1)S(1)}, u32[]{:S(2)}, u32[]{:S(2)}) collective-permute-start(bf16[2,128,512]{2,1,0:T(8,128)(2,1)} %get-tuple-element.48), channel_id=1, source_target_pairs={{4,8},{12,16},{20,24},{28,32},{36,40},{44,48},{52,56},{8,4},{16,12... | collective-permute-start | bytes 786440 | tf_op jit(solution)/shard_map/ppermute | solution.py:388
  18.1 10.6 %copy-start.2 = (bf16[1,256,512]{2,1,0:T(8,128)(2,1)S(1)}, bf16[1,256,512]{2,1,0:T(8,128)(2,1)}, u32[]{:S(2)}) copy-start(bf16[1,256,512]{2,1,0:T(8,128)(2,1)} %param.5) | copy-start | bytes 786436
  18.1 10.6 %copy-start.3 = (bf16[2,192,512]{2,1,0:T(8,128)(2,1)S(1)}, bf16[2,192,512]{2,1,0:T(8,128)(2,1)}, u32[]{:S(2)}) copy-start(bf16[2,192,512]{2,1,0:T(8,128)(2,1)} %get-tuple-element.49.chip_ref) | copy-start | bytes 1179652
  18.1 10.6 %copy-start.4 = (bf16[1,256,512]{2,1,0:T(8,128)(2,1)S(1)}, bf16[1,256,512]{2,1,0:T(8,128)(2,1)}, u32[]{:S(2)}) copy-start(bf16[1,256,512]{2,1,0:T(8,128)(2,1)} %param.6) | copy-start | bytes 786436
  18.1 10.6 %copy-start.5 = (bf16[1,256,512]{2,1,0:T(8,128)(2,1)S(1)}, bf16[1,256,512]{2,1,0:T(8,128)(2,1)}, u32[]{:S(2)}) copy-start(bf16[1,256,512]{2,1,0:T(8,128)(2,1)} %param.7) | copy-start | bytes 786436
  18.1 10.6 %collective-permute-start.7 = (bf16[2,192,512]{2,1,0:T(8,128)(2,1)}, bf16[2,192,512]{2,1,0:T(8,128)(2,1)S(1)}, u32[]{:S(2)}, u32[]{:S(2)}) collective-permute-start(bf16[2,192,512]{2,1,0:T(8,128)(2,1)} %get-tuple-element.49.chip_ref), channel_id=1, source_target_pairs={{0,4},{4,0},{1,5},{5,1},{2,6},{6,2},{3,7},{7,3},{8,12},{12,8},{9,1... | collective-permute-start | bytes 1179656 | tf_op jit(solution)/shard_map/ppermute | solution.py:364
  21.6 9.5 %collective-permute-start.1 = (bf16[2,32,512]{2,1,0:T(8,128)(2,1)S(1)}, bf16[2,32,512]{2,1,0:T(8,128)(2,1)S(1)}, u32[]{:S(2)}, u32[]{:S(2)}) collective-permute-start(bf16[2,32,512]{2,1,0:T(8,128)(2,1)S(1)} %collective-permute-done.near_ref), channel_id=1, source_target_pairs={{0,4},{4,0},{1,5},{5,1},{2,6},{6,2},{3,7},{7,3},{8,12},{12,8},{9,1... | collective-permute-start | bytes 196616 | tf_op jit(solution)/shard_map/ppermute | solution.py:364
  28.7 2.4 %collective-permute-start.2 = (bf16[8,2,16,512]{3,2,1,0:T(8,128)(2,1)S(1)}, bf16[8,2,16,512]{3,2,1,0:T(8,128)(2,1)S(1)}, u32[]{:S(2)}, u32[]{:S(2)}) collective-permute-start(bf16[8,2,16,512]{3,2,1,0:T(8,128)(2,1)S(1)} %all-to-all-done.far_ref), channel_id=1, source_target_pairs={{0,4},{4,0},{1,5},{5,1},{2,6},{6,2},{3,7},{7,3},{8,12},{12,8},{9,1... | collective-permute-start | bytes 786440 | tf_op jit(solution)/shard_map/ppermute | solution.py:364
  31.1 2.6 %copy-start.1 = (bf16[1,256,512]{2,1,0:T(8,128)(2,1)S(1)}, bf16[1,256,512]{2,1,0:T(8,128)(2,1)}, u32[]{:S(2)}) copy-start(bf16[1,256,512]{2,1,0:T(8,128)(2,1)} %param.9) | copy-start | bytes 786436
  33.7 1.6 %copy-start = (bf16[512,2048]{1,0:T(8,128)(2,1)S(1)}, bf16[512,2048]{1,0:T(8,128)(2,1)}, u32[]{:S(2)}) copy-start(bf16[512,2048]{1,0:T(8,128)(2,1)} %w_hbm.1) | copy-start | bytes 6291460
  34.4 2.9 %collective-permute-start.11 = (bf16[4,8,128,128]{3,2,1,0:T(8,128)(2,1)S(1)}, bf16[4,8,128,128]{3,2,1,0:T(8,128)(2,1)S(1)}, u32[]{:S(2)}, u32[]{:S(2)}) collective-permute-start(bf16[4,8,128,128]{3,2,1,0:T(8,128)(2,1)S(1)} %get-tuple-element.63), channel_id=1, source_target_pairs={{0,4},{4,0},{1,5},{5,1},{2,6},{6,2},{3,7},{7,3},{8,12},{12,8},{9,1... | collective-permute-start | bytes 3145736 | tf_op jit(solution)/shard_map/ppermute | solution.py:364
  37.5 13.4 %collective-permute-start.14 = (bf16[8,128,128]{2,1,0:T(8,128)(2,1)S(1)}, bf16[8,128,128]{2,1,0:T(8,128)(2,1)S(1)}, u32[]{:S(2)}, u32[]{:S(2)}) collective-permute-start(bf16[8,128,128]{2,1,0:T(8,128)(2,1)S(1)} %get-tuple-element.77), channel_id=1, source_target_pairs={{0,128},{64,192},{128,0},{192,64},{1,129},{65,193},{129,1},{193,65... | collective-permute-start | bytes 786440 | tf_op jit(solution)/shard_map/ppermute | solution.py:364
  40.6 12.7 %collective-permute-start.15 = (bf16[8,128,128]{2,1,0:T(8,128)(2,1)S(1)}, bf16[8,128,128]{2,1,0:T(8,128)(2,1)S(1)}, u32[]{:S(2)}, u32[]{:S(2)}) collective-permute-start(bf16[8,128,128]{2,1,0:T(8,128)(2,1)S(1)} %get-tuple-element.78), channel_id=1, source_target_pairs={{0,64},{64,128},{128,192},{192,0},{1,65},{65,129},{129,193},{193,1... | collective-permute-start | bytes 786440 | tf_op jit(solution)/shard_map/ppermute | solution.py:364
  41.2 12.3 %collective-permute-start.16 = (bf16[8,128,128]{2,1,0:T(8,128)(2,1)S(1)}, bf16[8,128,128]{2,1,0:T(8,128)(2,1)S(1)}, u32[]{:S(2)}, u32[]{:S(2)}) collective-permute-start(bf16[8,128,128]{2,1,0:T(8,128)(2,1)S(1)} %get-tuple-element.79), channel_id=1, source_target_pairs={{0,192},{64,0},{128,64},{192,128},{1,193},{65,1},{129,65},{193,129... | collective-permute-start | bytes 786440 | tf_op jit(solution)/shard_map/ppermute | solution.py:364
  48.5 5.2 %copy-start.6 = (f32[2,256,512]{2,1,0:T(8,128)}, f32[2,256,512]{2,1,0:T(8,128)S(1)}, u32[]{:S(2)}) copy-start(f32[2,256,512]{2,1,0:T(8,128)S(1)} %get-tuple-element.73.mid_ref) | copy-start | bytes 3145732
  48.5 5.2 %collective-permute-start.13 = (bf16[2,128,512]{2,1,0:T(8,128)(2,1)S(1)}, bf16[2,128,512]{2,1,0:T(8,128)(2,1)S(1)}, u32[]{:S(2)}, u32[]{:S(2)}) collective-permute-start(bf16[2,128,512]{2,1,0:T(8,128)(2,1)S(1)} %get-tuple-element.76), channel_id=1, source_target_pairs={{4,8},{12,16},{20,24},{28,32},{36,40},{44,48},{52,56},{8,4},{16,12... | collective-permute-start | bytes 786440 | tf_op jit(solution)/shard_map/ppermute | solution.py:434
  49.1 4.5 %collective-permute-start.12 = (bf16[2,288,512]{2,1,0:T(8,128)(2,1)S(1)}, bf16[2,288,512]{2,1,0:T(8,128)(2,1)S(1)}, u32[]{:S(2)}, u32[]{:S(2)}) collective-permute-start(bf16[2,288,512]{2,1,0:T(8,128)(2,1)S(1)} %get-tuple-element.75), channel_id=1, source_target_pairs={{0,4},{4,0},{1,5},{5,1},{2,6},{6,2},{3,7},{7,3},{8,12},{12,8},{9,1... | collective-permute-start | bytes 1769480 | tf_op jit(solution)/shard_map/ppermute | solution.py:364
  54.5 24.6 %all-to-all-start.1 = ((bf16[8,256,128]{2,1,0:T(8,128)(2,1)}), bf16[8,256,128]{2,1,0:T(8,128)(2,1)S(1)}, u32[]{:S(2)}, u32[]{:S(2)}) async-start(bf16[8,256,128]{2,1,0:T(8,128)(2,1)} %get-tuple-element.82), calls=%async_computation.1 | async-start | bytes 1048576 | tf_op jit(solution)/shard_map/all_to_all | solution.py:443
  63.1 10.6 %collective-permute-start.8 = (bf16[256,512]{1,0:T(8,128)(2,1)S(1)}, bf16[256,512]{1,0:T(8,128)(2,1)S(1)}, u32[]{:S(2)}, u32[]{:S(2)}) collective-permute-start(bf16[256,512]{1,0:T(8,128)(2,1)S(1)} %get-tuple-element.59), channel_id=1, source_target_pairs={{0,2},{1,3},{2,0},{3,1},{4,6},{5,7},{6,4},{7,5},{8,10},{9,11},{10,... | collective-permute-start | bytes 786440 | tf_op jit(solution)/shard_map/ppermute | solution.py:364
  63.3 11.4 %collective-permute-start.9 = (bf16[256,512]{1,0:T(8,128)(2,1)S(1)}, bf16[256,512]{1,0:T(8,128)(2,1)S(1)}, u32[]{:S(2)}, u32[]{:S(2)}) collective-permute-start(bf16[256,512]{1,0:T(8,128)(2,1)S(1)} %get-tuple-element.60), channel_id=1, source_target_pairs={{0,1},{1,2},{2,3},{3,0},{4,5},{5,6},{6,7},{7,4},{8,9},{9,10},{10,1... | collective-permute-start | bytes 786440 | tf_op jit(solution)/shard_map/ppermute | solution.py:364
  65.9 10.6 %collective-permute-start.10 = (bf16[256,512]{1,0:T(8,128)(2,1)S(1)}, bf16[256,512]{1,0:T(8,128)(2,1)S(1)}, u32[]{:S(2)}, u32[]{:S(2)}) collective-permute-start(bf16[256,512]{1,0:T(8,128)(2,1)S(1)} %get-tuple-element.61), channel_id=1, source_target_pairs={{0,3},{1,0},{2,1},{3,2},{4,7},{5,4},{6,5},{7,6},{8,11},{9,8},{10,9... | collective-permute-start | bytes 786440 | tf_op jit(solution)/shard_map/ppermute | solution.py:364
  77.3 5.1 %copy-start.7 = (f32[2,256,512]{2,1,0:T(8,128)S(1)}, f32[2,256,512]{2,1,0:T(8,128)}, u32[]{:S(2)}) copy-start(f32[2,256,512]{2,1,0:T(8,128)} %copy-done.6) | copy-start | bytes 3145732
  77.3 5.1 %collective-permute-start.17 = (bf16[2,32,512]{2,1,0:T(8,128)(2,1)S(1)}, bf16[2,32,512]{2,1,0:T(8,128)(2,1)S(1)}, u32[]{:S(2)}, u32[]{:S(2)}) collective-permute-start(bf16[2,32,512]{2,1,0:T(8,128)(2,1)S(1)} %get-tuple-element.81), channel_id=1, source_target_pairs={{0,8},{8,0},{16,24},{24,16},{32,40},{40,32},{48,56},{56,48},{1,9},... | collective-permute-start | bytes 196616 | tf_op jit(solution)/shard_map/ppermute | solution.py:364
  79.1 5.2 %collective-permute-start.20 = (bf16[128,128]{1,0:T(8,128)(2,1)S(1)}, bf16[128,128]{1,0:T(8,128)(2,1)S(1)}, u32[]{:S(2)}, u32[]{:S(2)}) collective-permute-start(bf16[128,128]{1,0:T(8,128)(2,1)S(1)} %shard_map.103._.a_ref), channel_id=1, source_target_pairs={{0,64},{64,128},{128,192},{192,0},{1,65},{65,129},{129,193},{193,1... | collective-permute-start | bytes 98312 | tf_op jit(solution)/shard_map/ppermute | solution.py:364
  79.2 5.5 %collective-permute-start.19 = (bf16[128,128]{1,0:T(8,128)(2,1)S(1)}, bf16[128,128]{1,0:T(8,128)(2,1)S(1)}, u32[]{:S(2)}, u32[]{:S(2)}) collective-permute-start(bf16[128,128]{1,0:T(8,128)(2,1)S(1)} %shard_map.103._.a_ref), channel_id=1, source_target_pairs={{0,128},{64,192},{128,0},{192,64},{1,129},{65,193},{129,1},{193,65... | collective-permute-start | bytes 98312 | tf_op jit(solution)/shard_map/ppermute | solution.py:364
  81.0 4.6 %collective-permute-start.18 = (bf16[128,128]{1,0:T(8,128)(2,1)S(1)}, bf16[128,128]{1,0:T(8,128)(2,1)S(1)}, u32[]{:S(2)}, u32[]{:S(2)}) collective-permute-start(bf16[128,128]{1,0:T(8,128)(2,1)S(1)} %shard_map.103._.a_ref), channel_id=1, source_target_pairs={{0,192},{64,0},{128,64},{192,128},{1,193},{65,1},{129,65},{193,129... | collective-permute-start | bytes 98312 | tf_op jit(solution)/shard_map/ppermute | solution.py:364

commit v6 on v5

--- a/solution.py
+++ b/solution.py
@@ -261,12 +261,11 @@
                 cross_ref[part, 64 + to : 64 + to + 16, at_h] = both.astype(BF)
 
 
-def merge_kernel(_, wsum_ref, minec_ref, got_ref, near_ref, out_ref):
+def gather_kernel(minec_ref, got_ref, near_ref, out_ref):
     z = lax.axis_index("z")
-    out_ref[:, 0:128] = wsum_ref[...]
     none = jnp.zeros((128, 128), BF)
-    out_ref[z, 128:256] = none
-    out_ref[z ^ 1, 128:256] = none
+    out_ref[z] = none
+    out_ref[z ^ 1] = none
     for part in range(2):
         total = (minec_ref[part] + got_ref[part, 64:160].astype(F32)).astype(BF)
         near_ref[part] = total[0:32]
@@ -278,8 +277,13 @@
                 piece = low[(d - 4) * 8 : (d - 4) * 8 + 8]
                 piece = jnp.concatenate([piece, jnp.zeros((8, WIDTH), BF)], axis=0)
             for col in range(4):
-                at = 128 + part * 64 + col * 16
+                at = part * 64 + col * 16
                 out_ref[z ^ d, at : at + 16] = piece[:, col * 128 : (col + 1) * 128]
+
+
+def merge_kernel(_, wsum_ref, far_ref, out_ref):
+    out_ref[:, 0:128] = wsum_ref[...]
+    out_ref[:, 128:256] = far_ref[...]
 
 
 def sum_kernel(a_ref, b_ref, c_ref, d_ref, out_ref):
@@ -435,9 +439,12 @@
     (wsum,) = call(
         sum_kernel, here(kept, from_across, from_down, from_up), [sds((8, 128, 128), BF)], us=8
     )
-    near_grad, both = call(
-        merge_kernel, [(AFTER, edge_back)] + here(wsum, minec, cross_got),
-        [sds((2, 32, WIDTH), BF), sds((8, 256, 128), BF)],
+    near_grad, far_grad = call(
+        gather_kernel, here(minec, cross_got),
+        [sds((2, 32, WIDTH), BF), sds((8, 128, 128), BF)],
+    )
+    (both,) = call(
+        merge_kernel, [(AFTER, edge_back)] + here(wsum, far_grad), [sds((8, 256, 128), BF)]
     )
     near_back = hop(near_grad)
     both_got = lax.all_to_all(both, "z", 0, 0)

time: 87.7 us -> 87.7 us (level)
    pallas_call x14 -> x15, Pallas kernels: 18.3 us -> 18.3 us  [call(): pl.pallas_call(kernel, out_shape=outs, in_specs=[spec for spec, _ in oper...]
where the time goes in v6:
time: 87.7 us; the launch traced here: 86.3 us
  starting transfers between devices  44.6 us (51%)
  waiting for transfers between devices  22.2 us (25%)
  Pallas kernels  18.3 us (21%)
    ppermute x19, starting transfers between devices, permute(): return lax.ppermute(x, axis, [(i, move(i) % size) for i in range(size)])  27.2 us
    pallas_call x15, Pallas kernels, call(): pl.pallas_call(kernel, out_shape=outs, in_specs=[spec for spec, _ in oper...  18.3 us
    ppermute x19, waiting for transfers between devices, permute(): return lax.ppermute(x, axis, [(i, move(i) % size) for i in range(size)])  15.2 us
    all_to_all x1, starting transfers between devices, body(): both_got = lax.all_to_all(both, 'z', 0, 0)  8.5 us
    all_to_all x1, starting transfers between devices, body(): far_got = lax.all_to_all(far, 'z', 0, 0)  7.57 us
    all_to_all x1, waiting for transfers between devices, body(): far_got = lax.all_to_all(far, 'z', 0, 0)  7 us
  transfers between devices with their start and end apart: 23, of which 10 were waited for; matrix products, arithmetic and copies ran while one was open for 0% of the time, Pallas kernels for 15%

profile of v6, /device:TPU:8, one launch (start us, length us, event | category | flops | bytes accessed | tf_op | source)
XLA Modules:
  0.0 86.3 jit_solution(1187844258063183903)
XLA Ops:
  0.6 1.7 %collective-permute-start.5 = (bf16[256,512]{1,0:T(8,128)(2,1)}, bf16[256,512]{1,0:T(8,128)(2,1)S(1)}, u32[]{:S(2)}, u32[]{:S(2)}) collective-permute-start(bf16[256,512]{1,0:T(8,128)(2,1)} %bitcast.9), channel_id=1, source_target_pairs={{0,1},{1,2},{2,3},{3,0},{4,5},{5,6},{6,7},{7,4},{8,9},{9,10},{10,1... | collective-permute-start | bytes 786440 | tf_op jit(solution)/shard_map/ppermute | solution.py:368
  2.3 2.7 %collective-permute-start.4 = (bf16[256,512]{1,0:T(8,128)(2,1)}, bf16[256,512]{1,0:T(8,128)(2,1)S(1)}, u32[]{:S(2)}, u32[]{:S(2)}) collective-permute-start(bf16[256,512]{1,0:T(8,128)(2,1)} %bitcast.10), channel_id=1, source_target_pairs={{0,2},{1,3},{2,0},{3,1},{4,6},{5,7},{6,4},{7,5},{8,10},{9,11},{10,... | collective-permute-start | bytes 786440 | tf_op jit(solution)/shard_map/ppermute | solution.py:368
  5.0 0.7 collective-permute-start.3
  5.6 2.2 %shard_map.92 = (bf16[2,192,512]{2,1,0:T(8,128)(2,1)}, bf16[2,32,512]{2,1,0:T(8,128)(2,1)}, bf16[8,2,16,512]{3,2,1,0:T(8,128)(2,1)}, bf16[2,128,512]{2,1,0:T(8,128)(2,1)}) custom-call(bf16[256,512]{1,0:T(8,128)(2,1)} %bitcast.17, bf16[256,512]{1,0:T(8,128)(2,1)} %bitcast.19), custom_call_target="tpu_custom_call" | custom-call | flops 1000000000 | bytes 1 | tf_op jit(solution)/shard_map/pallas_call | solution.py:351
  7.8 2.0 %collective-permute-start = (bf16[2,32,512]{2,1,0:T(8,128)(2,1)}, bf16[2,32,512]{2,1,0:T(8,128)(2,1)S(1)}, u32[]{:S(2)}, u32[]{:S(2)}) collective-permute-start(bf16[2,32,512]{2,1,0:T(8,128)(2,1)} %get-tuple-element.46), channel_id=1, source_target_pairs={{0,8},{8,0},{16,24},{24,16},{32,40},{40,32},{48,56},{56,48},{1,9},... | collective-permute-start | bytes 196616 | tf_op jit(solution)/shard_map/ppermute | solution.py:368
  9.8 7.6 %all-to-all-start = ((bf16[8,2,16,512]{3,2,1,0:T(8,128)(2,1)}), bf16[8,2,16,512]{3,2,1,0:T(8,128)(2,1)S(1)}, u32[]{:S(2)}, u32[]{:S(2)}) async-start(bf16[8,2,16,512]{3,2,1,0:T(8,128)(2,1)} %get-tuple-element.47), calls=%async_computation | async-start | bytes 524288 | tf_op jit(solution)/shard_map/all_to_all | solution.py:393
  17.4 0.7 collective-permute-start.6
  18.1 3.5 %collective-permute-start.7 = (bf16[2,192,512]{2,1,0:T(8,128)(2,1)}, bf16[2,192,512]{2,1,0:T(8,128)(2,1)S(1)}, u32[]{:S(2)}, u32[]{:S(2)}) collective-permute-start(bf16[2,192,512]{2,1,0:T(8,128)(2,1)} %get-tuple-element.49.chip_ref), channel_id=1, source_target_pairs={{0,4},{4,0},{1,5},{5,1},{2,6},{6,2},{3,7},{7,3},{8,12},{12,8},{9,1... | collective-permute-start | bytes 1179656 | tf_op jit(solution)/shard_map/ppermute | solution.py:368
  21.7 7.0 %all-to-all-done.far_ref = bf16[8,2,16,512]{3,2,1,0:T(8,128)(2,1)S(1)} async-done(((bf16[8,2,16,512]{3,2,1,0:T(8,128)(2,1)}), bf16[8,2,16,512]{3,2,1,0:T(8,128)(2,1)S(1)}, u32[]{:S(2)}, u32[]{:S(2)}) %all-to-all-start) | async-done | bytes 262176 | tf_op jit(solution)/shard_map/all_to_all | solution.py:393
  28.8 2.3 %shard_map.94 = (bf16[4,640,128]{2,1,0:T(8,128)(2,1)S(1)}, bf16[4,640,128]{2,1,0:T(8,128)(2,1)S(1)}, bf16[4,2,128,512]{3,2,1,0:T(8,128)(2,1)S(1)}, f32[256,512]{...) custom-call(f32[8,128]{1,0:T(8,128)S(1)} %shard_map.93._, bf16[256,512]{1,0:T(8,128)(2,1)S(1)} %bitcast.14, ...), custom_call_target="tpu_custom_call" | custom-call | flops 20000000000 | bytes 1 | tf_op jit(solution)/shard_map/pallas_call | solution.py:351
  31.1 2.6 %shard_map.95 = (bf16[256,512]{1,0:T(8,128)(2,1)S(1)}, bf16[512,256]{1,0:T(8,128)(2,1)S(1)}, bf16[4,256,256]{2,1,0:T(8,128)(2,1)S(1)}, bf16[4,256,128]{2,1,0:T(8...) custom-call(bf16[256,512]{1,0:T(8,128)(2,1)S(1)} %bitcast.15, ...), custom_call_target="tpu_custom_call" | custom-call | flops 1000000000 | bytes 1 | tf_op jit(solution)/shard_map/pallas_call | solution.py:351
  33.7 0.7 shard_map.96
  35.3 1.9 %shard_map.97 = (bf16[256,512]{1,0:T(8,128)(2,1)S(1)}, bf16[256,512]{1,0:T(8,128)(2,1)S(1)}, bf16[256,512]{1,0:T(8,128)(2,1)S(1)}, bf16[256,512]{1,0:T(8,128)(2,1)S(1)}, bf16[256,512]{1,0:T(8,128)(2,1)S(1)}) custom-call(bf16[4,8,128,128]{3,2,1,0:T(8,128)(2,1)S(1)} %get-tuple-element.56._.mine_ref, bf16[256,512]{1,0:T(8,128)(2,1)S(1)} %get-tuple-element.57.att_ref, ...), custom_call_target="tpu_custom_call" | custom-call | flops 1000000000 | bytes 1 | tf_op jit(solution)/shard_map/pallas_call | solution.py:351
  37.5 3.1 %collective-permute-start.15 = (bf16[8,128,128]{2,1,0:T(8,128)(2,1)S(1)}, bf16[8,128,128]{2,1,0:T(8,128)(2,1)S(1)}, u32[]{:S(2)}, u32[]{:S(2)}) collective-permute-start(bf16[8,128,128]{2,1,0:T(8,128)(2,1)S(1)} %get-tuple-element.79), channel_id=1, source_target_pairs={{0,128},{64,192},{128,0},{192,64},{1,129},{65,193},{129,1},{193,65... | collective-permute-start | bytes 786440 | tf_op jit(solution)/shard_map/ppermute | solution.py:368
  41.2 2.6 %collective-permute-start.17 = (bf16[8,128,128]{2,1,0:T(8,128)(2,1)S(1)}, bf16[8,128,128]{2,1,0:T(8,128)(2,1)S(1)}, u32[]{:S(2)}, u32[]{:S(2)}) collective-permute-start(bf16[8,128,128]{2,1,0:T(8,128)(2,1)S(1)} %get-tuple-element.81), channel_id=1, source_target_pairs={{0,192},{64,0},{128,64},{192,128},{1,193},{65,1},{129,65},{193,129... | collective-permute-start | bytes 786440 | tf_op jit(solution)/shard_map/ppermute | solution.py:368
  43.9 4.6 %shard_map.100 = (bf16[256,512]{1,0:T(8,128)(2,1)}, f32[2,256,512]{2,1,0:T(8,128)S(1)}, bf16[2,128,512]{2,1,0:T(8,128)(2,1)S(1)}, f32[2,64,512]{2,1,0:T(8,128)S(...) custom-call(bf16[8,128,128]{2,1,0:T(8,128)(2,1)S(1)} %get-tuple-element.64._.a_ref, ...), custom_call_target="tpu_custom_call" | custom-call | flops 20000000000 | bytes 1 | tf_op jit(solution)/shard_map/pallas_call | solution.py:351
  49.1 1.8 %collective-permute-start.12 = (bf16[2,288,512]{2,1,0:T(8,128)(2,1)S(1)}, bf16[2,288,512]{2,1,0:T(8,128)(2,1)S(1)}, u32[]{:S(2)}, u32[]{:S(2)}) collective-permute-start(bf16[2,288,512]{2,1,0:T(8,128)(2,1)S(1)} %get-tuple-element.75), channel_id=1, source_target_pairs={{0,4},{4,0},{1,5},{5,1},{2,6},{6,2},{3,7},{7,3},{8,12},{12,8},{9,1... | collective-permute-start | bytes 1769480 | tf_op jit(solution)/shard_map/ppermute | solution.py:368
  50.9 2.4 %collective-permute-done.16.c_ref = bf16[8,128,128]{2,1,0:T(8,128)(2,1)S(1)} collective-permute-done((bf16[8,128,128]{2,1,0:T(8,128)(2,1)S(1)}, bf16[8,128,128]{2,1,0:T(8,128)(2,1)S(1)}, u32[]{:S(2)}, u32[]{:S(2)}) %collective-permute-start.16) | collective-permute-done | bytes 262176 | tf_op jit(solution)/shard_map/ppermute | solution.py:368
  53.7 0.8 shard_map.103
  54.6 8.5 %all-to-all-start.1 = ((bf16[8,256,128]{2,1,0:T(8,128)(2,1)}), bf16[8,256,128]{2,1,0:T(8,128)(2,1)S(1)}, u32[]{:S(2)}, u32[]{:S(2)}) async-start(bf16[8,256,128]{2,1,0:T(8,128)(2,1)} %shard_map.103), calls=%async_computation.1 | async-start | bytes 1048576 | tf_op jit(solution)/shard_map/all_to_all | solution.py:450
  63.3 2.6 %collective-permute-start.9 = (bf16[256,512]{1,0:T(8,128)(2,1)S(1)}, bf16[256,512]{1,0:T(8,128)(2,1)S(1)}, u32[]{:S(2)}, u32[]{:S(2)}) collective-permute-start(bf16[256,512]{1,0:T(8,128)(2,1)S(1)} %get-tuple-element.60), channel_id=1, source_target_pairs={{0,1},{1,2},{2,3},{3,0},{4,5},{5,6},{6,7},{7,4},{8,9},{9,10},{10,1... | collective-permute-start | bytes 786440 | tf_op jit(solution)/shard_map/ppermute | solution.py:368
  65.9 7.8 %collective-permute-done.8.b_ref = bf16[256,512]{1,0:T(8,128)(2,1)S(1)} collective-permute-done((bf16[256,512]{1,0:T(8,128)(2,1)S(1)}, bf16[256,512]{1,0:T(8,128)(2,1)S(1)}, u32[]{:S(2)}, u32[]{:S(2)}) %collective-permute-start.8) | collective-permute-done | bytes 262176 | tf_op jit(solution)/shard_map/ppermute | solution.py:368
  73.7 0.9 %collective-permute-done.9.c_ref = bf16[256,512]{1,0:T(8,128)(2,1)S(1)} collective-permute-done((bf16[256,512]{1,0:T(8,128)(2,1)S(1)}, bf16[256,512]{1,0:T(8,128)(2,1)S(1)}, u32[]{:S(2)}, u32[]{:S(2)}) %collective-permute-start.9) | collective-permute-done | bytes 262176 | tf_op jit(solution)/shard_map/ppermute | solution.py:368
  74.6 1.8 %collective-permute-done.10.d_ref = bf16[256,512]{1,0:T(8,128)(2,1)S(1)} collective-permute-done((bf16[256,512]{1,0:T(8,128)(2,1)S(1)}, bf16[256,512]{1,0:T(8,128)(2,1)S(1)}, u32[]{:S(2)}, u32[]{:S(2)}) %collective-permute-start.10) | collective-permute-done | bytes 262176 | tf_op jit(solution)/shard_map/ppermute | solution.py:368
  76.5 0.8 shard_map.98
  77.3 1.7 %collective-permute-start.13 = (bf16[2,32,512]{2,1,0:T(8,128)(2,1)S(1)}, bf16[2,32,512]{2,1,0:T(8,128)(2,1)S(1)}, u32[]{:S(2)}, u32[]{:S(2)}) collective-permute-start(bf16[2,32,512]{2,1,0:T(8,128)(2,1)S(1)} %get-tuple-element.77), channel_id=1, source_target_pairs={{0,8},{8,0},{16,24},{24,16},{32,40},{40,32},{48,56},{56,48},{1,9},... | collective-permute-start | bytes 196616 | tf_op jit(solution)/shard_map/ppermute | solution.py:368
  79.2 1.8 %collective-permute-start.19 = (bf16[128,128]{1,0:T(8,128)(2,1)S(1)}, bf16[128,128]{1,0:T(8,128)(2,1)S(1)}, u32[]{:S(2)}, u32[]{:S(2)}) collective-permute-start(bf16[128,128]{1,0:T(8,128)(2,1)S(1)} %shard_map.104._.a_ref), channel_id=1, source_target_pairs={{0,128},{64,192},{128,0},{192,64},{1,129},{65,193},{129,1},{193,65... | collective-permute-start | bytes 98312 | tf_op jit(solution)/shard_map/ppermute | solution.py:368
  81.0 1.4 %collective-permute-start.18 = (bf16[128,128]{1,0:T(8,128)(2,1)S(1)}, bf16[128,128]{1,0:T(8,128)(2,1)S(1)}, u32[]{:S(2)}, u32[]{:S(2)}) collective-permute-start(bf16[128,128]{1,0:T(8,128)(2,1)S(1)} %shard_map.104._.a_ref), channel_id=1, source_target_pairs={{0,192},{64,0},{128,64},{192,128},{1,193},{65,1},{129,65},{193,129... | collective-permute-start | bytes 98312 | tf_op jit(solution)/shard_map/ppermute | solution.py:368
  82.4 1.2 %shard_map.105 = (bf16[256,512]{1,0:T(8,128)(2,1)}, bf16[256,512]{1,0:T(8,128)(2,1)}, f32[8,128]{1,0:T(8,128)S(1)}) custom-call(f32[2,256,512]{2,1,0:T(8,128)S(1)} %copy-done.7, f32[2,64,512]{2,1,0:T(8,128)S(1)} %get-tuple-element.74.own_ref, bf16[2,288,512]{2,1,0:T(8,128)(2,1)S(1)} %collective-permute-done.12.got_ref, ...), custom_call_target="tpu_custom_call" | custom-call | flops 1000000000 | bytes 1 | tf_op jit(solution)/shard_map/pallas_call | solution.py:351
  83.6 0.7 collective-permute-done.20.d_ref
  84.7 0.8 collective-permute-done.18.b_ref
  85.5 0.7 shard_map.106
  (45 shorter events, 3.7 us)
Async XLA Ops:
  0.6 21.0 %collective-permute-start.5 = (bf16[256,512]{1,0:T(8,128)(2,1)}, bf16[256,512]{1,0:T(8,128)(2,1)S(1)}, u32[]{:S(2)}, u32[]{:S(2)}) collective-permute-start(bf16[256,512]{1,0:T(8,128)(2,1)} %bitcast.9), channel_id=1, source_target_pairs={{0,1},{1,2},{2,3},{3,0},{4,5},{5,6},{6,7},{7,4},{8,9},{9,10},{10,1... | collective-permute-start | bytes 786440 | tf_op jit(solution)/shard_map/ppermute | solution.py:368
  2.3 19.4 %collective-permute-start.4 = (bf16[256,512]{1,0:T(8,128)(2,1)}, bf16[256,512]{1,0:T(8,128)(2,1)S(1)}, u32[]{:S(2)}, u32[]{:S(2)}) collective-permute-start(bf16[256,512]{1,0:T(8,128)(2,1)} %bitcast.10), channel_id=1, source_target_pairs={{0,2},{1,3},{2,0},{3,1},{4,6},{5,7},{6,4},{7,5},{8,10},{9,11},{10,... | collective-permute-start | bytes 786440 | tf_op jit(solution)/shard_map/ppermute | solution.py:368
  5.0 16.8 %collective-permute-start.3 = (bf16[256,512]{1,0:T(8,128)(2,1)}, bf16[256,512]{1,0:T(8,128)(2,1)S(1)}, u32[]{:S(2)}, u32[]{:S(2)}) collective-permute-start(bf16[256,512]{1,0:T(8,128)(2,1)} %bitcast.11), channel_id=1, source_target_pairs={{0,3},{1,0},{2,1},{3,2},{4,7},{5,4},{6,5},{7,6},{8,11},{9,8},{10,9... | collective-permute-start | bytes 786440 | tf_op jit(solution)/shard_map/ppermute | solution.py:368
  7.8 10.2 %collective-permute-start = (bf16[2,32,512]{2,1,0:T(8,128)(2,1)}, bf16[2,32,512]{2,1,0:T(8,128)(2,1)S(1)}, u32[]{:S(2)}, u32[]{:S(2)}) collective-permute-start(bf16[2,32,512]{2,1,0:T(8,128)(2,1)} %get-tuple-element.46), channel_id=1, source_target_pairs={{0,8},{8,0},{16,24},{24,16},{32,40},{40,32},{48,56},{56,48},{1,9},... | collective-permute-start | bytes 196616 | tf_op jit(solution)/shard_map/ppermute | solution.py:368
  9.8 18.9 %all-to-all-start = ((bf16[8,2,16,512]{3,2,1,0:T(8,128)(2,1)}), bf16[8,2,16,512]{3,2,1,0:T(8,128)(2,1)S(1)}, u32[]{:S(2)}, u32[]{:S(2)}) async-start(bf16[8,2,16,512]{3,2,1,0:T(8,128)(2,1)} %get-tuple-element.47), calls=%async_computation | async-start | bytes 524288 | tf_op jit(solution)/shard_map/all_to_all | solution.py:393
  17.4 11.3 %collective-permute-start.6 = (bf16[2,128,512]{2,1,0:T(8,128)(2,1)}, bf16[2,128,512]{2,1,0:T(8,128)(2,1)S(1)}, u32[]{:S(2)}, u32[]{:S(2)}) collective-permute-start(bf16[2,128,512]{2,1,0:T(8,128)(2,1)} %get-tuple-element.48), channel_id=1, source_target_pairs={{4,8},{12,16},{20,24},{28,32},{36,40},{44,48},{52,56},{8,4},{16,12... | collective-permute-start | bytes 786440 | tf_op jit(solution)/shard_map/ppermute | solution.py:392
  18.1 10.6 %copy-start.2 = (bf16[1,256,512]{2,1,0:T(8,128)(2,1)S(1)}, bf16[1,256,512]{2,1,0:T(8,128)(2,1)}, u32[]{:S(2)}) copy-start(bf16[1,256,512]{2,1,0:T(8,128)(2,1)} %param.5) | copy-start | bytes 786436
  18.1 10.6 %copy-start.3 = (bf16[2,192,512]{2,1,0:T(8,128)(2,1)S(1)}, bf16[2,192,512]{2,1,0:T(8,128)(2,1)}, u32[]{:S(2)}) copy-start(bf16[2,192,512]{2,1,0:T(8,128)(2,1)} %get-tuple-element.49.chip_ref) | copy-start | bytes 1179652
  18.1 10.6 %copy-start.4 = (bf16[1,256,512]{2,1,0:T(8,128)(2,1)S(1)}, bf16[1,256,512]{2,1,0:T(8,128)(2,1)}, u32[]{:S(2)}) copy-start(bf16[1,256,512]{2,1,0:T(8,128)(2,1)} %param.6) | copy-start | bytes 786436
  18.1 10.6 %copy-start.5 = (bf16[1,256,512]{2,1,0:T(8,128)(2,1)S(1)}, bf16[1,256,512]{2,1,0:T(8,128)(2,1)}, u32[]{:S(2)}) copy-start(bf16[1,256,512]{2,1,0:T(8,128)(2,1)} %param.7) | copy-start | bytes 786436
  18.1 10.6 %collective-permute-start.7 = (bf16[2,192,512]{2,1,0:T(8,128)(2,1)}, bf16[2,192,512]{2,1,0:T(8,128)(2,1)S(1)}, u32[]{:S(2)}, u32[]{:S(2)}) collective-permute-start(bf16[2,192,512]{2,1,0:T(8,128)(2,1)} %get-tuple-element.49.chip_ref), channel_id=1, source_target_pairs={{0,4},{4,0},{1,5},{5,1},{2,6},{6,2},{3,7},{7,3},{8,12},{12,8},{9,1... | collective-permute-start | bytes 1179656 | tf_op jit(solution)/shard_map/ppermute | solution.py:368
  21.6 9.5 %collective-permute-start.1 = (bf16[2,32,512]{2,1,0:T(8,128)(2,1)S(1)}, bf16[2,32,512]{2,1,0:T(8,128)(2,1)S(1)}, u32[]{:S(2)}, u32[]{:S(2)}) collective-permute-start(bf16[2,32,512]{2,1,0:T(8,128)(2,1)S(1)} %collective-permute-done.near_ref), channel_id=1, source_target_pairs={{0,4},{4,0},{1,5},{5,1},{2,6},{6,2},{3,7},{7,3},{8,12},{12,8},{9,1... | collective-permute-start | bytes 196616 | tf_op jit(solution)/shard_map/ppermute | solution.py:368
  28.7 2.4 %collective-permute-start.2 = (bf16[8,2,16,512]{3,2,1,0:T(8,128)(2,1)S(1)}, bf16[8,2,16,512]{3,2,1,0:T(8,128)(2,1)S(1)}, u32[]{:S(2)}, u32[]{:S(2)}) collective-permute-start(bf16[8,2,16,512]{3,2,1,0:T(8,128)(2,1)S(1)} %all-to-all-done.far_ref), channel_id=1, source_target_pairs={{0,4},{4,0},{1,5},{5,1},{2,6},{6,2},{3,7},{7,3},{8,12},{12,8},{9,1... | collective-permute-start | bytes 786440 | tf_op jit(solution)/shard_map/ppermute | solution.py:368
  31.1 2.6 %copy-start.1 = (bf16[1,256,512]{2,1,0:T(8,128)(2,1)S(1)}, bf16[1,256,512]{2,1,0:T(8,128)(2,1)}, u32[]{:S(2)}) copy-start(bf16[1,256,512]{2,1,0:T(8,128)(2,1)} %param.9) | copy-start | bytes 786436
  33.7 1.6 %copy-start = (bf16[512,2048]{1,0:T(8,128)(2,1)S(1)}, bf16[512,2048]{1,0:T(8,128)(2,1)}, u32[]{:S(2)}) copy-start(bf16[512,2048]{1,0:T(8,128)(2,1)} %w_hbm.1) | copy-start | bytes 6291460
  34.4 2.9 %collective-permute-start.11 = (bf16[4,8,128,128]{3,2,1,0:T(8,128)(2,1)S(1)}, bf16[4,8,128,128]{3,2,1,0:T(8,128)(2,1)S(1)}, u32[]{:S(2)}, u32[]{:S(2)}) collective-permute-start(bf16[4,8,128,128]{3,2,1,0:T(8,128)(2,1)S(1)} %get-tuple-element.63), channel_id=1, source_target_pairs={{0,4},{4,0},{1,5},{5,1},{2,6},{6,2},{3,7},{7,3},{8,12},{12,8},{9,1... | collective-permute-start | bytes 3145736 | tf_op jit(solution)/shard_map/ppermute | solution.py:368
  37.5 13.4 %collective-permute-start.15 = (bf16[8,128,128]{2,1,0:T(8,128)(2,1)S(1)}, bf16[8,128,128]{2,1,0:T(8,128)(2,1)S(1)}, u32[]{:S(2)}, u32[]{:S(2)}) collective-permute-start(bf16[8,128,128]{2,1,0:T(8,128)(2,1)S(1)} %get-tuple-element.79), channel_id=1, source_target_pairs={{0,128},{64,192},{128,0},{192,64},{1,129},{65,193},{129,1},{193,65... | collective-permute-start | bytes 786440 | tf_op jit(solution)/shard_map/ppermute | solution.py:368
  40.6 12.7 %collective-permute-start.16 = (bf16[8,128,128]{2,1,0:T(8,128)(2,1)S(1)}, bf16[8,128,128]{2,1,0:T(8,128)(2,1)S(1)}, u32[]{:S(2)}, u32[]{:S(2)}) collective-permute-start(bf16[8,128,128]{2,1,0:T(8,128)(2,1)S(1)} %get-tuple-element.80), channel_id=1, source_target_pairs={{0,64},{64,128},{128,192},{192,0},{1,65},{65,129},{129,193},{193,1... | collective-permute-start | bytes 786440 | tf_op jit(solution)/shard_map/ppermute | solution.py:368
  41.2 12.3 %collective-permute-start.17 = (bf16[8,128,128]{2,1,0:T(8,128)(2,1)S(1)}, bf16[8,128,128]{2,1,0:T(8,128)(2,1)S(1)}, u32[]{:S(2)}, u32[]{:S(2)}) collective-permute-start(bf16[8,128,128]{2,1,0:T(8,128)(2,1)S(1)} %get-tuple-element.81), channel_id=1, source_target_pairs={{0,192},{64,0},{128,64},{192,128},{1,193},{65,1},{129,65},{193,129... | collective-permute-start | bytes 786440 | tf_op jit(solution)/shard_map/ppermute | solution.py:368
  48.5 5.2 %copy-start.6 = (f32[2,256,512]{2,1,0:T(8,128)}, f32[2,256,512]{2,1,0:T(8,128)S(1)}, u32[]{:S(2)}) copy-start(f32[2,256,512]{2,1,0:T(8,128)S(1)} %get-tuple-element.73.mid_ref) | copy-start | bytes 3145732
  48.5 5.3 %collective-permute-start.14 = (bf16[2,128,512]{2,1,0:T(8,128)(2,1)S(1)}, bf16[2,128,512]{2,1,0:T(8,128)(2,1)S(1)}, u32[]{:S(2)}, u32[]{:S(2)}) collective-permute-start(bf16[2,128,512]{2,1,0:T(8,128)(2,1)S(1)} %get-tuple-element.78), channel_id=1, source_target_pairs={{4,8},{12,16},{20,24},{28,32},{36,40},{44,48},{52,56},{8,4},{16,12... | collective-permute-start | bytes 786440 | tf_op jit(solution)/shard_map/ppermute | solution.py:438
  49.1 4.5 %collective-permute-start.12 = (bf16[2,288,512]{2,1,0:T(8,128)(2,1)S(1)}, bf16[2,288,512]{2,1,0:T(8,128)(2,1)S(1)}, u32[]{:S(2)}, u32[]{:S(2)}) collective-permute-start(bf16[2,288,512]{2,1,0:T(8,128)(2,1)S(1)} %get-tuple-element.75), channel_id=1, source_target_pairs={{0,4},{4,0},{1,5},{5,1},{2,6},{6,2},{3,7},{7,3},{8,12},{12,8},{9,1... | collective-permute-start | bytes 1769480 | tf_op jit(solution)/shard_map/ppermute | solution.py:368
  54.6 24.5 %all-to-all-start.1 = ((bf16[8,256,128]{2,1,0:T(8,128)(2,1)}), bf16[8,256,128]{2,1,0:T(8,128)(2,1)S(1)}, u32[]{:S(2)}, u32[]{:S(2)}) async-start(bf16[8,256,128]{2,1,0:T(8,128)(2,1)} %shard_map.103), calls=%async_computation.1 | async-start | bytes 1048576 | tf_op jit(solution)/shard_map/all_to_all | solution.py:450
  63.1 10.6 %collective-permute-start.8 = (bf16[256,512]{1,0:T(8,128)(2,1)S(1)}, bf16[256,512]{1,0:T(8,128)(2,1)S(1)}, u32[]{:S(2)}, u32[]{:S(2)}) collective-permute-start(bf16[256,512]{1,0:T(8,128)(2,1)S(1)} %get-tuple-element.59), channel_id=1, source_target_pairs={{0,2},{1,3},{2,0},{3,1},{4,6},{5,7},{6,4},{7,5},{8,10},{9,11},{10,... | collective-permute-start | bytes 786440 | tf_op jit(solution)/shard_map/ppermute | solution.py:368
  63.3 11.4 %collective-permute-start.9 = (bf16[256,512]{1,0:T(8,128)(2,1)S(1)}, bf16[256,512]{1,0:T(8,128)(2,1)S(1)}, u32[]{:S(2)}, u32[]{:S(2)}) collective-permute-start(bf16[256,512]{1,0:T(8,128)(2,1)S(1)} %get-tuple-element.60), channel_id=1, source_target_pairs={{0,1},{1,2},{2,3},{3,0},{4,5},{5,6},{6,7},{7,4},{8,9},{9,10},{10,1... | collective-permute-start | bytes 786440 | tf_op jit(solution)/shard_map/ppermute | solution.py:368
  65.9 10.6 %collective-permute-start.10 = (bf16[256,512]{1,0:T(8,128)(2,1)S(1)}, bf16[256,512]{1,0:T(8,128)(2,1)S(1)}, u32[]{:S(2)}, u32[]{:S(2)}) collective-permute-start(bf16[256,512]{1,0:T(8,128)(2,1)S(1)} %get-tuple-element.61), channel_id=1, source_target_pairs={{0,3},{1,0},{2,1},{3,2},{4,7},{5,4},{6,5},{7,6},{8,11},{9,8},{10,9... | collective-permute-start | bytes 786440 | tf_op jit(solution)/shard_map/ppermute | solution.py:368
  77.3 5.1 %copy-start.7 = (f32[2,256,512]{2,1,0:T(8,128)S(1)}, f32[2,256,512]{2,1,0:T(8,128)}, u32[]{:S(2)}) copy-start(f32[2,256,512]{2,1,0:T(8,128)} %copy-done.6) | copy-start | bytes 3145732
  77.3 5.1 %collective-permute-start.13 = (bf16[2,32,512]{2,1,0:T(8,128)(2,1)S(1)}, bf16[2,32,512]{2,1,0:T(8,128)(2,1)S(1)}, u32[]{:S(2)}, u32[]{:S(2)}) collective-permute-start(bf16[2,32,512]{2,1,0:T(8,128)(2,1)S(1)} %get-tuple-element.77), channel_id=1, source_target_pairs={{0,8},{8,0},{16,24},{24,16},{32,40},{40,32},{48,56},{56,48},{1,9},... | collective-permute-start | bytes 196616 | tf_op jit(solution)/shard_map/ppermute | solution.py:368
  79.1 5.2 %collective-permute-start.20 = (bf16[128,128]{1,0:T(8,128)(2,1)S(1)}, bf16[128,128]{1,0:T(8,128)(2,1)S(1)}, u32[]{:S(2)}, u32[]{:S(2)}) collective-permute-start(bf16[128,128]{1,0:T(8,128)(2,1)S(1)} %shard_map.104._.a_ref), channel_id=1, source_target_pairs={{0,64},{64,128},{128,192},{192,0},{1,65},{65,129},{129,193},{193,1... | collective-permute-start | bytes 98312 | tf_op jit(solution)/shard_map/ppermute | solution.py:368
  79.2 5.5 %collective-permute-start.19 = (bf16[128,128]{1,0:T(8,128)(2,1)S(1)}, bf16[128,128]{1,0:T(8,128)(2,1)S(1)}, u32[]{:S(2)}, u32[]{:S(2)}) collective-permute-start(bf16[128,128]{1,0:T(8,128)(2,1)S(1)} %shard_map.104._.a_ref), channel_id=1, source_target_pairs={{0,128},{64,192},{128,0},{192,64},{1,129},{65,193},{129,1},{193,65... | collective-permute-start | bytes 98312 | tf_op jit(solution)/shard_map/ppermute | solution.py:368
  81.0 4.5 %collective-permute-start.18 = (bf16[128,128]{1,0:T(8,128)(2,1)S(1)}, bf16[128,128]{1,0:T(8,128)(2,1)S(1)}, u32[]{:S(2)}, u32[]{:S(2)}) collective-permute-start(bf16[128,128]{1,0:T(8,128)(2,1)S(1)} %shard_map.104._.a_ref), channel_id=1, source_target_pairs={{0,192},{64,0},{128,64},{192,128},{1,193},{65,1},{129,65},{193,129... | collective-permute-start | bytes 98312 | tf_op jit(solution)/shard_map/ppermute | solution.py:368
